TPU v7x, 256 devices: a whole 4x4x8 slice. The times are simulated.
256 devices in a mesh: group: 8 (over y, core), dev: 32 (over x, z).
Axes of the slice: x: 4, y: 4, z: 8, core: 2. Of those that a mesh axis runs over, the one named last changes fastest.
Arguments:
- features_in: bfloat16 [96, 262144], P(None, ('group', 'dev')), may hold values from -6 to 6
- occupancy: int32 [262144], P(('group', 'dev')), may hold values 0 or 1
- cotangent: bfloat16 [96, 262144], P(None, ('group', 'dev')), may hold values from -6 to 6
- kernel_one: bfloat16 [27, 96, 96], replicated, may hold values from -0.125 to 0.125
- kernel_two: bfloat16 [27, 96, 96], replicated, may hold values from -0.125 to 0.125
- neighbours: int32 [512, 27], P(('group', 'dev')), may hold values from -1 to 5, as said below
Outputs:
- features_out: bfloat16 [96, 262144], P(None, ('group', 'dev'))
- kernel_one_grad: float32 [27, 96, 96], replicated
- kernel_two_grad: float32 [27, 96, 96], replicated
Inputs may be any that keep to these rules, and one draw needn't show every extreme that they name: `neighbours`: the blocks of a device sit at distinct places of a 4 by 4 grid in y and z; the device's dev index is its slab's x position in the region. Entry 13 of a block is its own index. Other entries are -1 where no block lies at that offset (always beyond the first and last device of a region), n < 2 for block n of the same device, 2 + n for block n of the device with dev index one lower, 4 + n for block n of the device with dev index one higher; only offsets with dx = -1 or 1 reach other devices. The relation is mutual: entry t of block a names block b exactly when entry 26 - t of b names a.
All inputs are finite; a program needn't handle non-finite values. No bound on the sum of `occupancy` on one device may be relied on, other than what follows from the above.
Results may differ from a plain program's by a relative error of at most 0.0049.
Values may be sent and summed in bfloat16 or wider, within the bound.
No kernel may reach another device: no remote copies, remote signals or barrier semaphores. Data moves between devices by JAX's collectives and lax.ppermute only.
A program may use at most 64 MiB of HBM per device.

v0:
```python
import jax
import jax.numpy as jnp
import numpy as np
from jax import lax
from jax.sharding import PartitionSpec as P


def with_halo(block, sides, width):
    for axis, dim in sides:
        count = lax.axis_size(axis)
        forward = [(i, i + 1) for i in range(count - 1)]
        backward = [(target, source) for source, target in forward]
        low = lax.ppermute(
            lax.slice_in_dim(block, block.shape[dim] - width, None, axis=dim), axis, forward
        )
        high = lax.ppermute(lax.slice_in_dim(block, 0, width, axis=dim), axis, backward)
        block = jnp.concatenate([low, block, high], axis=dim)
    return block


def pad_tables():
    cells = np.arange(1000)
    coord_x = cells // 100
    coord_y = cells // 10 % 10
    coord_z = cells % 10

    def side(coord):
        return np.where(coord == 0, -1, np.where(coord == 9, 1, 0))

    def inner(coord):
        return np.where(coord == 0, 7, np.where(coord == 9, 0, coord - 1))

    offset_of = (side(coord_x) + 1) * 9 + (side(coord_y) + 1) * 3 + (side(coord_z) + 1)
    voxel_of = inner(coord_x) * 64 + inner(coord_y) * 8 + inner(coord_z)
    return (offset_of.astype(np.int32), voxel_of.astype(np.int32))


def cube_window(cube, first, second, third, width):
    return cube[:, :, first : first + 8, second : second + 8, third : third + 8].reshape(width, -1)


def conv_forward(padded, kernel):
    width = padded.shape[0]
    cube = padded.reshape(width, -1, 10, 10, 10)
    total = None
    for first in range(3):
        for second in range(3):
            stacked = jnp.concatenate(
                [cube_window(cube, first, second, third, width) for third in range(3)], axis=0
            )
            start = first * 9 + second * 3
            weights = kernel[start : start + 3].reshape(3 * width, width)
            term = lax.dot_general(
                weights, stacked, (((0,), (0,)), ((), ())), preferred_element_type=jnp.float32
            )
            total = term if total is None else total + term
    return total


def kernel_terms(padded, grad):
    width = padded.shape[0]
    cube = padded.reshape(width, -1, 10, 10, 10)
    pieces = []
    for first in range(3):
        for second in range(3):
            stacked = jnp.concatenate(
                [cube_window(cube, first, second, third, width) for third in range(3)], axis=0
            )
            term = lax.dot_general(
                stacked, grad, (((1,), (1,)), ((), ())), preferred_element_type=jnp.float32
            )
            pieces.append(term.reshape(3, width, width))
    return jnp.concatenate(pieces, axis=0)


def conv_backward(padded, kernel):
    width = padded.shape[0]
    cube = padded.reshape(width, -1, 10, 10, 10)
    total = None
    for first in range(3):
        for second in range(3):
            stacked = jnp.concatenate(
                [cube_window(cube, 2 - first, 2 - second, 2 - third, width) for third in range(3)],
                axis=0,
            )
            start = first * 9 + second * 3
            weights = jnp.concatenate([kernel[start + third] for third in range(3)], axis=1)
            term = jnp.dot(weights, stacked, preferred_element_type=jnp.float32)
            total = term if total is None else total + term
    return total


def rims_beside(values, which):
    if which == "inputs":
        arrived = with_halo(values[None], (("dev", 0),), 1)
    else:
        arrived = with_halo(values[None], (("dev", 0),), 1)
    return (arrived[0], arrived[2], 512)


def padded_of(values, lower, upper, stride, neighbours):
    offset_np, voxel_np = pad_tables()
    offset_of = jnp.asarray(offset_np)
    voxel_of = jnp.asarray(voxel_np)
    inner_of = voxel_of % stride
    blocks_here = neighbours.shape[0]
    local_span = blocks_here * 512
    rim_span = blocks_here * stride
    entries = neighbours[:, offset_of]
    local_col = entries * 512 + voxel_of[None, :]
    lower_col = local_span + (entries - blocks_here) * stride + inner_of[None, :]
    upper_col = local_span + rim_span + (entries - 2 * blocks_here) * stride + inner_of[None, :]
    zero_col = local_span + 2 * rim_span
    columns = jnp.where(
        entries < blocks_here, local_col, jnp.where(entries < 2 * blocks_here, lower_col, upper_col)
    )
    columns = jnp.where(entries < 0, zero_col, columns)
    table = jnp.concatenate(
        [values, lower, upper, jnp.zeros((values.shape[0], 1), values.dtype)], axis=1
    )
    return jnp.take(table, columns.reshape(-1), axis=1)


def reduce_grad(grad):
    flat = grad.reshape(-1)
    whole = lax.psum(flat, ("group", "dev"))
    return whole.reshape(grad.shape)


def per_device(features_in, occupancy, cotangent, kernel_one, kernel_two, neighbours):
    width = features_in.shape[0]
    mask = occupancy.astype(jnp.float32)[None, :]
    occupied = occupancy[None, :] > 0
    total_voxels = features_in.shape[1] * lax.axis_size("group") * lax.axis_size("dev")
    scale = float(total_voxels) ** (-0.5)
    a_zero = jnp.where(occupied, features_in, jnp.zeros_like(features_in))
    g_two = jnp.where(occupied, cotangent, jnp.zeros_like(cotangent))
    both = jnp.concatenate([a_zero, g_two], axis=0)
    lower, upper, stride = rims_beside(both, "inputs")
    padded_both = padded_of(both, lower, upper, stride, neighbours)
    padded_zero = padded_both[:width]
    padded_grad = padded_both[width:]
    z_one = mask * conv_forward(padded_zero, kernel_one)
    a_one = jax.nn.silu(z_one).astype(jnp.bfloat16)
    lower, upper, stride = rims_beside(a_one, "hidden")
    padded_one = padded_of(a_one, lower, upper, stride, neighbours)
    features_out = (mask * conv_forward(padded_one, kernel_two)).astype(jnp.bfloat16)
    kernel_two_grad = reduce_grad(scale * kernel_terms(padded_one, g_two))
    ga_one = mask * conv_backward(padded_grad, kernel_two)
    sigma = jax.nn.sigmoid(z_one)
    gz_one = (ga_one * sigma * (1.0 + z_one * (1.0 - sigma))).astype(jnp.bfloat16)
    kernel_one_grad = reduce_grad(scale * kernel_terms(padded_zero, gz_one))
    return (features_out, kernel_one_grad, kernel_two_grad)


def solution(mesh):
    return jax.shard_map(
        per_device,
        mesh=mesh,
        in_specs=(
            P(None, ("group", "dev")),
            P(("group", "dev")),
            P(None, ("group", "dev")),
            P(),
            P(),
            P(("group", "dev"), None),
        ),
        out_specs=(P(None, ("group", "dev")), P(), P()),
        check_vma=False,
    )
```

profile of v0, /device:TPU:1, one launch (start us, length us, event | category | flops | bytes accessed | tf_op | source)
XLA Modules:
  0.0 380.2 jit_solution(10808691736755201325)
XLA Ops:
  7.2 0.7 broadcast_compare_fusion
  8.0 1.1 copy.37
  9.1 1.1 copy.38
  10.7 1.3 collective-permute-start.1
  12.0 5.8 %collective-permute-start = (bf16[1,192,1024]{1,2,0:T(8,128)(2,1)S(1)}, bf16[1,192,1024]{1,2,0:T(8,128)(2,1)}, u32[]{:S(2)}, u32[]{:S(2)}) collective-permute-start(bf16[1,192,1024]{1,2,0:T(8,128)(2,1)S(1)} %maximum_bitcast_fusion), channel_id=1, source_target_pairs={{0,1},{1,2},{2,3},{3,4},{4,5},{5,6},{6,7},{7,8},{8,9},{9,10},{10,1... | collective-permute-start | bytes 1179656 | tf_op jit(solution)/shard_map/ppermute | solution.py:13
  18.5 0.8 slice_bitcast_fusion.2
  19.4 2.9 gather_fusion
  22.8 0.8 fusion.172
  23.6 0.8 fusion.173
  26.1 4.9 %maximum_maximum_fusion = bf16[192,3073]{0,1:T(8,128)(2,1)S(1)} fusion(bf16[192,1024]{0,1:T(8,128)(2,1)} %bitcast.8, bf16[192,1024]{0,1:T(8,128)(2,1)} %bitcast.7, bf16[96,1024]{0,1:T(8,128)(2,1)S(1)} %get-tuple-element.141, bf16[96,1024]{0,1:T(8,128)(2,1)S(1)} %get-tuple-element.140, bf16[3073]{0:T(1024)(128)(2,1)S(1)} %pad.116.clone), kind=kLoop, calls=%fused_computation.3 | loop fusion | flops 5900160 | bytes 2365826 | tf_op jit(solution)/shard_map/concatenate | solution.py:118
  31.0 8.1 %gather_fusion.1 = bf16[2000,192]{1,0:T(8,128)(2,1)S(1)} fusion(bf16[192,3073]{0,1:T(8,128)(2,1)S(1)} %maximum_maximum_fusion, s32[2048]{0:T(1024)S(1)} %pad_clamp_fusion), kind=kCustom, calls=%fused_computation.1 | custom fusion | bytes 1544000 | tf_op jit(solution)/shard_map/jit(_take)/gather | solution.py:121
  40.0 1.3 fusion.167
  41.2 2.4 fusion.166
  44.3 1.0 fusion.170
  57.3 0.7 convolution_add_fusion.2
  59.6 0.8 fusion.63
  60.4 0.8 fusion.64
  61.2 0.8 fusion.65
  62.0 0.8 fusion.66
  62.8 0.8 fusion.67
  63.5 0.8 fusion.68
  64.3 0.8 fusion.69
  65.1 0.8 fusion.70
  65.9 0.8 fusion.73
  66.7 1.3 collective-permute-start.3
  68.0 5.5 %collective-permute-start.2 = (bf16[1,96,1024]{2,1,0:T(8,128)(2,1)S(1)}, bf16[1,96,1024]{2,1,0:T(8,128)(2,1)S(1)}, u32[]{:S(2)}, u32[]{:S(2)}) collective-permute-start(bf16[1,96,1024]{2,1,0:T(8,128)(2,1)S(1)} %bitcast.388), channel_id=1, source_target_pairs={{0,1},{1,2},{2,3},{3,4},{4,5},{5,6},{6,7},{7,8},{8,9},{9,10},{10,1... | collective-permute-start | bytes 589832 | tf_op jit(solution)/shard_map/ppermute | solution.py:13
  73.7 0.9 collective-permute-done.3
  74.6 1.5 collective-permute-done.2
  76.6 6.3 %gather_fusion.2 = bf16[2000,96]{1,0:T(8,128)(2,1)S(1)} fusion(bf16[96,3073]{0,1:T(8,128)(2,1)S(1)} %copy.39, s32[2048]{0:T(1024)S(1)} %pad_clamp_fusion), kind=kCustom, calls=%fused_computation.2 | custom fusion | bytes 776000 | tf_op jit(solution)/shard_map/jit(_take)/gather | solution.py:121
  83.2 0.8 broadcast_select_fusion
  84.5 0.8 fusion.168
  85.3 0.8 fusion.71
  86.9 0.8 fusion.62
  88.4 0.8 fusion.61
  89.9 0.8 fusion.60
  90.8 1.4 convolution_add_fusion.13
  92.2 0.8 fusion.59
  93.0 0.8 fusion.58
  93.8 0.8 fusion.57
  94.6 0.8 fusion.56
  95.4 0.8 fusion.55
  96.7 1.7 broadcast_multiply_fusion
  98.4 0.9 copy-done.30
  99.3 1.7 convolution_add_fusion.12
  103.3 1.3 fusion.8
  104.6 264.9 %all-reduce.3.cloned.1.call-done = (f32[27,96,96]{2,1,0:T(8,128)}, f32[27,96,96]{2,1,0:T(8,128)}) async-done(((f32[27,96,96]{2,1,0:T(8,128)}, f32[27,96,96]{2,1,0:T(8,128)}), (f32[27,96,96]{2,1,0:T(8,128)}, f32[27,96,96]{2,1,0:T(8,128)})) %all-reduce.3.cloned.1.call-update) | async-done | bytes 1990672 | tf_op jit(solution)/shard_map/psum | solution.py:126
  369.5 2.6 copy.58
  372.1 1.1 copy.59
  (231 shorter events, 24.2 us)
Async XLA Ops:
  7.2 10.6 %copy-start = (bf16[27,96,96]{2,1,0:T(8,128)(2,1)S(1)}, bf16[27,96,96]{2,1,0:T(8,128)(2,1)}, u32[]{:S(2)}) copy-start(bf16[27,96,96]{2,1,0:T(8,128)(2,1)} %param.14) | copy-start | bytes 1492996
  7.2 362.3 %all-reduce.3.cloned.1.call-start = ((), (), s32[]{:S(2)}) async-start(), calls=%async_computation | async-start | bytes 5308416 | tf_op jit(solution)/shard_map/psum | solution.py:126
  10.2 9.1 %copy-start.75 = (s32[1000]{0:T(1024)S(1)}, s32[1000]{0:T(1024)}, u32[]{:S(2)}) copy-start(s32[1000]{0:T(1024)} %constant.102) | copy-start | bytes 12004
  10.2 9.1 %copy-start.77 = (s32[2,27]{1,0:T(2,128)S(1)}, s32[2,27]{1,0:T(2,128)}, u32[]{:S(2)}) copy-start(s32[2,27]{1,0:T(2,128)} %param.15) | copy-start | bytes 652
  10.4 12.1 %copy-start.76 = (s32[1000]{0:T(1024)S(1)}, s32[1000]{0:T(1024)}, u32[]{:S(2)}) copy-start(s32[1000]{0:T(1024)} %constant.83.clone) | copy-start | bytes 12004
  10.7 15.4 %collective-permute-start.1 = (bf16[1,192,1024]{1,2,0:T(8,128)(2,1)S(1)}, bf16[1,192,1024]{1,2,0:T(8,128)(2,1)}, u32[]{:S(2)}, u32[]{:S(2)}) collective-permute-start(bf16[1,192,1024]{1,2,0:T(8,128)(2,1)S(1)} %maximum_bitcast_fusion), channel_id=1, source_target_pairs={{1,0},{2,1},{3,2},{4,3},{5,4},{6,5},{7,6},{8,7},{9,8},{10,9},{11,1... | collective-permute-start | bytes 1179656 | tf_op jit(solution)/shard_map/ppermute | solution.py:16
  12.0 14.1 %collective-permute-start = (bf16[1,192,1024]{1,2,0:T(8,128)(2,1)S(1)}, bf16[1,192,1024]{1,2,0:T(8,128)(2,1)}, u32[]{:S(2)}, u32[]{:S(2)}) collective-permute-start(bf16[1,192,1024]{1,2,0:T(8,128)(2,1)S(1)} %maximum_bitcast_fusion), channel_id=1, source_target_pairs={{0,1},{1,2},{2,3},{3,4},{4,5},{5,6},{6,7},{7,8},{8,9},{9,10},{10,1... | collective-permute-start | bytes 1179656 | tf_op jit(solution)/shard_map/ppermute | solution.py:13
  18.5 5.1 %copy-start.4 = (bf16[27,96,96]{2,1,0:T(8,128)(2,1)S(1)}, bf16[27,96,96]{2,1,0:T(8,128)(2,1)}, u32[]{:S(2)}) copy-start(bf16[27,96,96]{2,1,0:T(8,128)(2,1)} %param.13) | copy-start | bytes 1492996
  22.3 2.0 copy-start.72
  22.8 3.2 copy-start.32
  51.9 1.1 copy-start.26
  51.9 1.1 copy-start.47
  52.6 1.1 copy-start.23
  52.6 1.1 copy-start.69
  52.6 1.1 copy-start.70
  52.6 1.1 copy-start.71
  53.6 1.1 copy-start.20
  53.6 1.1 copy-start.66
  53.6 1.1 copy-start.67
  53.6 1.1 copy-start.68
  54.4 1.1 copy-start.16
  54.4 1.2 copy-start.17
  54.4 1.1 copy-start.63
  54.4 1.1 copy-start.64
  54.4 1.1 copy-start.65
  55.3 1.1 copy-start.14
  55.3 1.1 copy-start.60
  55.3 1.1 copy-start.61
  55.4 1.1 copy-start.62
  56.1 1.1 copy-start.10
  56.1 1.2 copy-start.11
  56.1 1.1 copy-start.57
  56.1 1.1 copy-start.58
  56.1 1.1 copy-start.59
  57.1 1.1 copy-start.8
  57.1 1.1 copy-start.54
  57.1 1.1 copy-start.55
  57.1 1.1 copy-start.56
  66.7 7.9 %collective-permute-start.3 = (bf16[1,96,1024]{2,1,0:T(8,128)(2,1)S(1)}, bf16[1,96,1024]{2,1,0:T(8,128)(2,1)S(1)}, u32[]{:S(2)}, u32[]{:S(2)}) collective-permute-start(bf16[1,96,1024]{2,1,0:T(8,128)(2,1)S(1)} %bitcast.387), channel_id=1, source_target_pairs={{1,0},{2,1},{3,2},{4,3},{5,4},{6,5},{7,6},{8,7},{9,8},{10,9},{11,1... | collective-permute-start | bytes 589832 | tf_op jit(solution)/shard_map/ppermute | solution.py:16
  68.0 8.1 %collective-permute-start.2 = (bf16[1,96,1024]{2,1,0:T(8,128)(2,1)S(1)}, bf16[1,96,1024]{2,1,0:T(8,128)(2,1)S(1)}, u32[]{:S(2)}, u32[]{:S(2)}) collective-permute-start(bf16[1,96,1024]{2,1,0:T(8,128)(2,1)S(1)} %bitcast.388), channel_id=1, source_target_pairs={{0,1},{1,2},{2,3},{3,4},{4,5},{5,6},{6,7},{7,8},{8,9},{9,10},{10,1... | collective-permute-start | bytes 589832 | tf_op jit(solution)/shard_map/ppermute | solution.py:13
  73.7 2.4 copy-start.1
  85.3 6.9 %copy-start.29 = (bf16[96,2,8,8,8]{0,4,3,2,1:T(8,128)(2,1)}, bf16[96,2,8,8,8]{0,4,3,2,1:T(8,128)(2,1)S(1)}, u32[]{:S(2)}) copy-start(bf16[96,2,8,8,8]{0,4,3,2,1:T(8,128)(2,1)S(1)} %get-tuple-element.51) | copy-start | bytes 589828
  85.3 6.9 %copy-start.31 = (bf16[96,2,8,8,8]{0,4,3,2,1:T(8,128)(2,1)}, bf16[96,2,8,8,8]{0,4,3,2,1:T(8,128)(2,1)S(1)}, u32[]{:S(2)}) copy-start(bf16[96,2,8,8,8]{0,4,3,2,1:T(8,128)(2,1)S(1)} %get-tuple-element.52) | copy-start | bytes 589828
  85.3 7.7 %copy-start.27 = (bf16[96,2,8,8,8]{0,4,3,2,1:T(8,128)(2,1)}, bf16[96,2,8,8,8]{0,4,3,2,1:T(8,128)(2,1)S(1)}, u32[]{:S(2)}) copy-start(bf16[96,2,8,8,8]{0,4,3,2,1:T(8,128)(2,1)S(1)} %get-tuple-element.49) | copy-start | bytes 589828
  95.4 1.3 copy-start.2
  98.4 2.7 copy-start.28
  98.4 2.7 copy-start.34
  369.5 2.6 copy-start.3
  (35 other events, 33.1 us)
Sparse Core Ops, SparseCore 0:
  98.5 270.9 all-reduce.2
where the time goes:
time: 387 us; the launch traced here: 380 us
  waiting for transfers between devices  267 us (69%)
  local copies, waits for them, and re-layouts  40.5 us (10%)
  matrix products  32.9 us (9%)
  between operations  15.6 us (4%)
  starting transfers between devices  13.9 us (4%)
  other arithmetic  9.84 us (3%)
    psum x1, waiting for transfers between devices, reduce_grad(): whole = lax.psum(flat, ('group', 'dev'))  265 us
    gather x3, local copies, waits for them, and re-layouts, padded_of(): return jnp.take(table, columns.reshape(-1), axis=1)  14.7 us
    dot_general x18, matrix products, kernel_terms(): lax.dot_general(stacked, grad, (((1,), (1,)), ((), ())), preferred_elemen...  13.9 us
    dot_general x18, matrix products, conv_forward(): lax.dot_general(weights, stacked, (((0,), (0,)), ((), ())), preferred_ele...  13.7 us
    ppermute x2, starting transfers between devices, with_halo(): lax.ppermute(lax.slice_in_dim(block, block.shape[dim] - width, None, axis...  11.3 us
    unnamed x177, local copies, waits for them, and re-layouts  11.1 us
  transfers between devices with their start and end apart: 5, of which 3 were waited for; matrix products, arithmetic and copies ran while one was open for 3% of the time, Pallas kernels for 0%

commit v1 on v0

v1 whole, which is shorter than its diff:
```python
import jax
import jax.numpy as jnp
from jax import lax
from jax.experimental import pallas as pl
from jax.experimental.pallas import tpu as pltpu
from jax.sharding import PartitionSpec as P

CH = 96
PAIRS = [(dy, dz) for dy in (-1, 0, 1) for dz in (-1, 0, 1)]
K9 = 9 * CH
F32 = jnp.float32
BF16 = jnp.bfloat16
NN = (((1,), (0,)), ((), ()))
NT = (((1,), (1,)), ((), ()))
VMEM = pl.BlockSpec(memory_space=pltpu.VMEM)
SMEM = pl.BlockSpec(memory_space=pltpu.SMEM)
ROWS = 4096
PACKED = 1296
LIMIT = 48 * 1024 * 1024


def dot(a, b, dims=NN):
    return lax.dot_general(a, b, dims, preferred_element_type=F32)


def lanes_low(rows):
    return lax.broadcasted_iota(jnp.int32, (rows, 128), 1) < 64


def pair_planes(first, second):
    low = lanes_low(first.shape[0])
    even = jnp.where(low, first, pltpu.roll(second, 64, 1))
    odd = jnp.where(low, pltpu.roll(first, 64, 1), second)
    return even, odd


def to_planes(ref, x):
    first = ref[:, x * 64 : x * 64 + 128].astype(F32)
    second = ref[:, 512 + x * 64 : 640 + x * 64].astype(F32)
    return pair_planes(first, second)


def selection(nb_ref, face):
    base = {0: 0, -1: 2, 1: 4}[face]
    lane = lax.broadcasted_iota(jnp.int32, (1, 128), 1)
    source = lax.broadcasted_iota(jnp.int32, (128, 128), 0)
    y = (lane // 8) % 8
    z = lane % 8
    pieces = []
    for dy, dz in PAIRS:
        far_y = y + dy
        far_z = z + dz
        out_y = (far_y < 0) | (far_y > 7)
        out_z = (far_z < 0) | (far_z > 7)

        def entry(block):
            def at(sy, sz):
                return nb_ref[block, (face + 1) * 9 + (sy + 1) * 3 + sz + 1] - base

            return jnp.where(
                out_y,
                jnp.where(out_z, at(dy, dz), at(dy, 0)),
                jnp.where(out_z, at(0, dz), at(0, 0)),
            )

        found = jnp.where(lane < 64, entry(0), entry(1))
        column = found * 64 + (far_y & 7) * 8 + (far_z & 7)
        column = jnp.where(found < 0, -1, column)
        pieces.append(jnp.where(source == column, 1.0, 0.0).astype(BF16))
    return pieces


def rim_kernel(feat_ref, cot_ref, occ_ref, low_ref, high_ref):
    for x, pick, out_ref in ((0, 0, low_ref), (6, 1, high_ref)):
        mask = to_planes(occ_ref, x)[pick] > 0
        for row, ref in ((0, feat_ref), (CH, cot_ref)):
            plane = to_planes(ref, x)[pick]
            out_ref[row : row + CH, :] = jnp.where(mask, plane, 0.0).astype(BF16)


def prep_kernel(
    feat_ref, cot_ref, occ_ref, w1_ref, w2_ref, nb_ref,
    a_ref, g_ref, zp_ref, gp_ref, w1t_ref, wb_ref, w2t_ref, sel_ref, mask_ref,
    planes_ref,
):
    for x in range(0, 8, 2):
        masks = to_planes(occ_ref, x)
        for k in range(2):
            mask_ref[:, (x + k) * 128 : (x + k + 1) * 128] = masks[k]
        for row, ref in ((0, feat_ref), (CH, cot_ref)):
            both = to_planes(ref, x)
            for k in range(2):
                planes_ref[x + k, row : row + CH, :] = jnp.where(masks[k] > 0, both[k], 0.0).astype(BF16)
    for index, face in enumerate((-1, 0, 1)):
        for j, piece in enumerate(selection(nb_ref, face)):
            sel_ref[index, :, j * 128 : (j + 1) * 128] = piece
    stacked = planes_ref[...].reshape(8 * 2 * CH, 128)
    for j in range(9):
        spread = dot(stacked, sel_ref[1, :, j * 128 : (j + 1) * 128]).astype(BF16)
        for x in range(8):
            a_ref[j * CH : (j + 1) * CH, x * 128 : (x + 1) * 128] = spread[x * 2 * CH : x * 2 * CH + CH]
            g_ref[j * CH : (j + 1) * CH, x * 128 : (x + 1) * 128] = spread[x * 2 * CH + CH : (x + 1) * 2 * CH]
    for d in range(3):
        w1t_ref[d] = w1_ref[d * K9 : (d + 1) * K9, :].astype(F32).T.astype(BF16)
        w2t_ref[d] = w2_ref[d * K9 : (d + 1) * K9, :].astype(F32).T.astype(BF16)
        wb_ref[d] = jnp.concatenate(
            [w2_ref[(26 - d * 9 - j) * CH : (27 - d * 9 - j) * CH, :] for j in range(9)], axis=1
        )
    for w_ref, v_ref, out_ref in ((w1t_ref, a_ref, zp_ref), (wb_ref, g_ref, gp_ref)):
        out_ref[...] = dot(w_ref[1], v_ref[...])
        out_ref[:, 128:] += dot(w_ref[0], v_ref[:, :896])
        out_ref[:, :896] += dot(w_ref[2], v_ref[:, 128:])


def spread_rim(rim, sel_ref, index, rows):
    full = dot(rim, sel_ref[index]).astype(BF16)
    parts = []
    for r in range(0, rows, CH):
        parts.append(
            jnp.concatenate([full[r : r + CH, j * 128 : (j + 1) * 128] for j in range(9)], axis=0)
        )
    return parts


def main_kernel(
    a_ref, g_ref, zp_ref, gp_ref, w1t_ref, wb_ref, sel_ref, mask_ref, low_ref, high_ref,
    own_ref, send_ref, a1_ref, a1_low_ref, a1_high_ref,
    grad_ref, packed_ref,
):
    scale = 262144.0 ** -0.5
    a_low, g_low = spread_rim(low_ref[...], sel_ref, 0, 2 * CH)
    a_high, g_high = spread_rim(high_ref[...], sel_ref, 2, 2 * CH)

    def finish(partial_ref, w_ref, low, high):
        first = partial_ref[:, :128] + dot(w_ref[0], low)
        last = partial_ref[:, 896:] + dot(w_ref[2], high)
        return mask_ref[...] * jnp.concatenate([first, partial_ref[:, 128:896], last], axis=1)

    z = finish(zp_ref, w1t_ref, a_low, a_high)
    ga = finish(gp_ref, wb_ref, g_low, g_high)
    sigma = 1.0 / (1.0 + jnp.exp(-z))
    a1 = (z * sigma).astype(BF16)
    gz = (ga * sigma * (1.0 + z * (1.0 - sigma))).astype(BF16)
    a1_ref[...] = a1
    a1_low_ref[...] = a1[:, :128]
    a1_high_ref[...] = a1[:, 896:]

    def terms(v_ref, low, high, grad, start):
        zero = jnp.zeros((K9, 32), F32)

        def put(d, value):
            r = start + d * K9
            grad_ref[r : r + K9, :] = jnp.concatenate([value * scale, zero], axis=1)

        put(0, dot(v_ref[:, :896], grad[:, 128:], NT) + dot(low, grad[:, :128], NT))
        put(1, dot(v_ref[...], grad, NT))
        put(2, dot(v_ref[:, 128:], grad[:, :896], NT) + dot(high, grad[:, 896:], NT))

    terms(g_ref, g_low, g_high, a1, 27 * CH)
    terms(a_ref, a_low, a_high, gz, 0)
    spare = grad_ref[3 * PACKED :, :]
    lane = lax.broadcasted_iota(jnp.int32, (PACKED, 128), 1)
    for k in range(3):
        moved = pltpu.roll(spare, 96 - 32 * k, 1)
        packed_ref[k * PACKED : (k + 1) * PACKED, :] = jnp.where(
            lane < 96, grad_ref[k * PACKED : (k + 1) * PACKED, :], moved
        ).astype(BF16)
    packed_ref[3 * PACKED :, :] = jnp.zeros((ROWS - 3 * PACKED, 128), BF16)
    half = ROWS // 2
    core = lax.rem(lax.axis_index("group"), 2)
    own_ref[...] = packed_ref[pl.ds(pl.multiple_of(core * half, half), half), :]
    send_ref[...] = packed_ref[pl.ds(pl.multiple_of((1 - core) * half, half), half), :]


def out_kernel(a1_ref, low_ref, high_ref, sel_ref, w2t_ref, mask_ref, out_ref, v_ref, planes_ref):
    for x in range(8):
        planes_ref[x] = a1_ref[:, x * 128 : (x + 1) * 128]
    stacked = planes_ref[...].reshape(8 * CH, 128)
    for j in range(9):
        spread = dot(stacked, sel_ref[1, :, j * 128 : (j + 1) * 128]).astype(BF16)
        for x in range(8):
            v_ref[j * CH : (j + 1) * CH, (x + 1) * 128 : (x + 2) * 128] = spread[x * CH : (x + 1) * CH]
    v_ref[:, :128] = spread_rim(low_ref[...], sel_ref, 0, CH)[0]
    v_ref[:, 1152:] = spread_rim(high_ref[...], sel_ref, 2, CH)[0]
    total = dot(w2t_ref[0], v_ref[:, :1024])
    total += dot(w2t_ref[1], v_ref[:, 128:1152])
    total += dot(w2t_ref[2], v_ref[:, 256:])
    total = mask_ref[...] * total
    for x in range(0, 8, 2):
        even = total[:, x * 128 : (x + 1) * 128]
        odd = total[:, (x + 1) * 128 : (x + 2) * 128]
        first, second = pair_planes(even, odd)
        out_ref[:, x * 64 : x * 64 + 128] = first.astype(BF16)
        out_ref[:, 512 + x * 64 : 640 + x * 64] = second.astype(BF16)


def part_kernel(count, axis_of, *refs):
    arrived, rest = refs[: len(refs) - count - 1], refs[len(refs) - count - 1 :]
    outs, total_ref = rest[:count], rest[count]
    total = arrived[0][...].astype(F32)
    for ref in arrived[1:]:
        total += ref[...].astype(F32)
    rows = total.shape[0] // count
    total_ref[...] = total.astype(BF16)
    me = axis_of()
    for k in range(count):
        start = lax.rem(me + k, count) * rows
        outs[k][...] = total_ref[pl.ds(pl.multiple_of(start, rows), rows), :]


def total_kernel(count, axis_of, *refs):
    arrived, out_ref, slots_ref = refs[:count], refs[count], refs[count + 1]
    me = axis_of()
    for k in range(count):
        slots_ref[lax.rem(me + count - k, count)] = arrived[k][...]
    total = slots_ref[0].astype(F32)
    for k in range(1, count):
        total += slots_ref[k].astype(F32)
    out_ref[...] = total.astype(BF16)


def join_kernel(count, axis_of, *refs):
    arrived, out_ref = refs[:count], refs[count]
    rows = out_ref.shape[0] // count
    me = axis_of()
    for k in range(count):
        start = lax.rem(me + count - k, count) * rows
        out_ref[pl.ds(pl.multiple_of(start, rows), rows), :] = arrived[k][...]


def grads_kernel(own_ref, other_ref, one_ref, two_ref, packed_ref):
    half = ROWS // 2
    core = lax.rem(lax.axis_index("group"), 2)
    packed_ref[pl.ds(pl.multiple_of(core * half, half), half), :] = own_ref[...].astype(F32)
    packed_ref[pl.ds(pl.multiple_of((1 - core) * half, half), half), :] = other_ref[...].astype(F32)

    def put(block, value):
        if block < 27:
            one_ref[block] = value[:, :CH]
        else:
            wide = jnp.concatenate([value, jnp.zeros((32, 128), F32)], axis=0)
            two_ref[53 - block] = wide.T[:CH, :CH]

    lane = lax.broadcasted_iota(jnp.int32, (48, 128), 1)

    def piece(start):
        if start < 3 * PACKED:
            return packed_ref[start : start + 48, :]
        r = start - 3 * PACKED
        value = None
        for k in range(3):
            moved = pltpu.roll(packed_ref[k * PACKED + r : k * PACKED + r + 48, :], (32 + 32 * k) % 128, 1)
            value = moved if k == 0 else jnp.where(lane < 32 * k, value, moved)
        return value

    for block in range(54):
        put(block, jnp.concatenate([piece(block * 96), piece(block * 96 + 48)], axis=0))


def shape(dims, dtype=BF16):
    return jax.ShapeDtypeStruct(dims, dtype)


def call(kernel, outs, *args, scratch=(), smem=(), flops=0, name=None):
    return pl.pallas_call(
        kernel,
        out_shape=outs,
        in_specs=[SMEM if k in smem else VMEM for k in range(len(args))],
        out_specs=jax.tree.map(lambda _: VMEM, outs),
        scratch_shapes=scratch,
        compiler_params=pltpu.CompilerParams(vmem_limit_bytes=LIMIT),
        cost_estimate=pl.CostEstimate(flops=flops, bytes_accessed=1 << 20, transcendentals=0),
        name=name,
    )(*args)


def staged_sum(own, send):
    core_pairs = [(g, g ^ 1) for g in range(8)]

    def x_pairs(k):
        return [(x * 8 + z, (x + k) % 4 * 8 + z) for x in range(4) for z in range(8)]

    def y_pairs(k):
        return [(y * 2 + c, (y + k) % 4 * 2 + c) for y in range(4) for c in range(2)]

    def z_pairs(k):
        return [(x * 8 + z, x * 8 + (z + k) % 8) for x in range(4) for z in range(8)]

    def at_x():
        return lax.axis_index("dev") // 8

    def at_y():
        return lax.axis_index("group") // 2

    def at_z():
        return lax.rem(lax.axis_index("dev"), 8)

    def part(arrived, count, axis_of, name):
        rows = arrived[0].shape[0]
        return call(
            lambda *refs: part_kernel(count, axis_of, *refs),
            [shape((rows // count, 128))] * count,
            *arrived,
            scratch=[pltpu.VMEM((rows, 128), BF16)],
            name=name,
        )

    def join(arrived, count, axis_of, name):
        return call(
            lambda *refs: join_kernel(count, axis_of, *refs),
            shape((arrived[0].shape[0] * count, 128)),
            *arrived,
            name=name,
        )

    got = lax.ppermute(send, "group", core_pairs)
    parts = part([own, got], 4, at_x, "sum_core")
    arrived = [parts[0]] + [lax.ppermute(parts[k], "dev", x_pairs(k)) for k in range(1, 4)]
    parts = part(arrived, 4, at_y, "sum_x")
    arrived = [parts[0]] + [lax.ppermute(parts[k], "group", y_pairs(k)) for k in range(1, 4)]
    (mine,) = part(arrived, 1, at_y, "sum_y")
    arrived = [mine] + [lax.ppermute(mine, "dev", z_pairs(k)) for k in range(1, 8)]
    mine = call(
        lambda *refs: total_kernel(8, at_z, *refs),
        shape(mine.shape),
        *arrived,
        scratch=[pltpu.VMEM((8,) + mine.shape, BF16)],
        name="sum_z",
    )
    arrived = [mine] + [lax.ppermute(mine, "group", y_pairs(k)) for k in range(1, 4)]
    mine = join(arrived, 4, at_y, "join_y")
    arrived = [mine] + [lax.ppermute(mine, "dev", x_pairs(k)) for k in range(1, 4)]
    mine = join(arrived, 4, at_x, "join_x")
    return mine, lax.ppermute(mine, "group", core_pairs)


def dev_shift(value, step):
    count = lax.axis_size("dev")
    pairs = [(i, i + step) for i in range(count) if 0 <= i + step < count]
    return lax.ppermute(value, "dev", pairs)


def per_device(features_in, occupancy, cotangent, kernel_one, kernel_two, neighbours):
    occ = occupancy.reshape(1, 1024)
    w1 = kernel_one.reshape(27 * CH, CH)
    w2 = kernel_two.reshape(27 * CH, CH)
    low, high = call(
        rim_kernel, [shape((2 * CH, 128))] * 2, features_in, cotangent, occ, name="rims"
    )
    upper = dev_shift(low, -1)
    lower = dev_shift(high, 1)
    a, g, zp, gp, w1t, wb, w2t, sel, mask = call(
        prep_kernel,
        [
            shape((K9, 1024)), shape((K9, 1024)), shape((CH, 1024), F32), shape((CH, 1024), F32),
            shape((3, CH, K9)), shape((3, CH, K9)), shape((3, CH, K9)),
            shape((3, 128, 1152)), shape((1, 1024), F32),
        ],
        features_in, cotangent, occ, w1, w2, neighbours,
        scratch=[pltpu.VMEM((8, 2 * CH, 128), BF16)],
        smem=(5,),
        flops=4 << 30,
        name="prep",
    )
    own, send, a1, a1_low, a1_high = call(
        main_kernel,
        [
            shape((ROWS // 2, 128)), shape((ROWS // 2, 128)), shape((CH, 1024)),
            shape((CH, 128)), shape((CH, 128)),
        ],
        a, g, zp, gp, w1t, wb, sel, mask, lower, upper,
        scratch=[pltpu.VMEM((54 * CH, 128), F32), pltpu.VMEM((ROWS, 128), BF16)],
        flops=4 << 30,
        name="gradients",
    )
    a1_upper = dev_shift(a1_low, -1)
    a1_lower = dev_shift(a1_high, 1)
    features_out = call(
        out_kernel,
        shape((CH, 1024)),
        a1, a1_lower, a1_upper, sel, w2t, mask,
        scratch=[pltpu.VMEM((K9, 1280), BF16), pltpu.VMEM((8, CH, 128), BF16)],
        flops=4 << 30,
        name="features",
    )
    mine, other = staged_sum(own, send)
    kernel_one_grad, kernel_two_grad = call(
        grads_kernel,
        [shape((27, CH, CH), F32)] * 2,
        mine, other,
        scratch=[pltpu.VMEM((ROWS, 128), F32)],
        name="unpack",
    )
    return (features_out, kernel_one_grad, kernel_two_grad)


def solution(mesh):
    return jax.shard_map(
        per_device,
        mesh=mesh,
        in_specs=(
            P(None, ("group", "dev")),
            P(("group", "dev")),
            P(None, ("group", "dev")),
            P(),
            P(),
            P(("group", "dev"), None),
        ),
        out_specs=(P(None, ("group", "dev")), P(), P()),
        check_vma=False,
    )
```

time: 387 us -> 99.2 us (0.26); the launches traced: 380 us -> 98.7 us
  waiting for transfers between devices: 267 us -> 24 us
  starting transfers between devices: 13.9 us -> 51.6 us
  local copies, waits for them, and re-layouts: 40.5 us -> 6.86 us
  matrix products: 32.9 us -> 0 us
  Pallas kernels: 0 us -> 15.5 us
  between operations: 15.6 us -> 0.76 us
  other arithmetic: 9.84 us -> 0 us
    psum x1 -> x0, waiting for transfers between devices: 265 us -> none  [reduce_grad(): whole = lax.psum(flat, ('group', 'dev'))]
    ppermute x4 -> x25, starting transfers between devices: 13.9 us -> 51.6 us  [the longest x7 12.6 us: staged_sum(): lax.ppermute(mine, 'dev', z_pairs(k))]
    dot_general x45 -> x0, matrix products: 32.9 us -> none  [the longest x18 13.9 us: kernel_terms(): lax.dot_general(stacked, grad, (((1,), (1,)), ((), ())), preferred_elemen...]
    ppermute x4 -> x25, waiting for transfers between devices: 2.39 us -> 24 us  [the longest x3 5.46 us: staged_sum(): lax.ppermute(mine, 'dev', x_pairs(k))]
    gather x5 -> x0, local copies, waits for them, and re-layouts: 17.8 us -> none  [the longest x3 14.7 us: padded_of(): return jnp.take(table, columns.reshape(-1), axis=1)]
    pallas_call x0 -> x11, Pallas kernels: none -> 15.5 us  [call(): pl.pallas_call(kernel, out_shape=outs, in_specs=[SMEM if k in smem else V...]
    slice x9 -> x0, local copies, waits for them, and re-layouts: 8.21 us -> none  [the longest x6 6.39 us: cube_window(): cube[:, :, first:first + 8, second:second + 8, third:third + 8]]
    concatenate x2 -> x0, other arithmetic: 5 us -> none  [padded_of(): jnp.concatenate([values, lower, upper, jnp.zeros((values.shape[0], 1), va...]
  transfers between devices with their start and end apart: 5 -> 25, of which waited for: 3 -> 14; matrix products, arithmetic and copies ran while one was open for 3% -> 0% of each run, Pallas kernels for 0% -> 7%
where the time goes in v1:
time: 99.2 us; the launch traced here: 98.7 us
  starting transfers between devices  51.6 us (52%)
  waiting for transfers between devices  24 us (24%)
  Pallas kernels  15.5 us (16%)
  local copies, waits for them, and re-layouts  6.86 us (7%)
    pallas_call x11, Pallas kernels, call(): pl.pallas_call(kernel, out_shape=outs, in_specs=[SMEM if k in smem else V...  15.5 us
    ppermute x7, starting transfers between devices, staged_sum(): lax.ppermute(mine, 'dev', z_pairs(k))  12.6 us
    ppermute x4, starting transfers between devices, dev_shift(): return lax.ppermute(value, 'dev', pairs)  9.51 us
    ppermute x3, starting transfers between devices, staged_sum(): lax.ppermute(parts[k], 'dev', x_pairs(k))  9.44 us
    ppermute x1, starting transfers between devices, staged_sum(): return (mine, lax.ppermute(mine, 'group', core_pairs))  7.89 us
    unnamed x14, local copies, waits for them, and re-layouts  6.86 us
    ppermute x3, waiting for transfers between devices, staged_sum(): lax.ppermute(mine, 'dev', x_pairs(k))  5.46 us
    ppermute x3, waiting for transfers between devices, staged_sum(): lax.ppermute(parts[k], 'dev', x_pairs(k))  5.19 us
  transfers between devices with their start and end apart: 25, of which 14 were waited for; matrix products, arithmetic and copies ran while one was open for 0% of the time, Pallas kernels for 7%

profile of v1, /device:TPU:1, one launch (start us, length us, event | category | flops | bytes accessed | tf_op | source)
XLA Modules:
  0.0 98.7 jit_solution(15279652777391281993)
XLA Ops:
  0.6 0.9 copy-done
  1.6 0.9 copy-done.1
  2.5 0.7 copy-done.2
  3.3 4.4 %collective-permute-start = (bf16[192,128]{1,0:T(8,128)(2,1)S(1)}, bf16[192,128]{1,0:T(8,128)(2,1)S(1)}, u32[]{:S(2)}, u32[]{:S(2)}) collective-permute-start(bf16[192,128]{1,0:T(8,128)(2,1)S(1)} %get-tuple-element.37), channel_id=1, source_target_pairs={{0,1},{1,2},{2,3},{3,4},{4,5},{5,6},{6,7},{7,8},{8,9},{9,10},{10,1... | collective-permute-start | bytes 147464 | tf_op jit(solution)/shard_map/ppermute | solution.py:340
  7.7 1.3 %collective-permute-start.1 = (bf16[192,128]{1,0:T(8,128)(2,1)S(1)}, bf16[192,128]{1,0:T(8,128)(2,1)S(1)}, u32[]{:S(2)}, u32[]{:S(2)}) collective-permute-start(bf16[192,128]{1,0:T(8,128)(2,1)S(1)} %get-tuple-element.38), channel_id=1, source_target_pairs={{1,0},{2,1},{3,2},{4,3},{5,4},{6,5},{7,6},{8,7},{9,8},{10,9},{11,1... | collective-permute-start | bytes 147464 | tf_op jit(solution)/shard_map/ppermute | solution.py:340
  9.0 1.1 %copy-done.3 = bf16[27,96,96]{2,1,0:T(8,128)(2,1)S(1)} copy-done((bf16[27,96,96]{2,1,0:T(8,128)(2,1)S(1)}, bf16[27,96,96]{2,1,0:T(8,128)(2,1)}, u32[]{:S(2)}) %copy-start.3) | copy-done | bytes 497688
  10.1 1.1 %copy-done.4 = bf16[27,96,96]{2,1,0:T(8,128)(2,1)S(1)} copy-done((bf16[27,96,96]{2,1,0:T(8,128)(2,1)S(1)}, bf16[27,96,96]{2,1,0:T(8,128)(2,1)}, u32[]{:S(2)}) %copy-start.4) | copy-done | bytes 497688
  11.1 0.7 copy-done.5
  11.8 4.9 %prep.1 = (bf16[864,1024]{1,0:T(8,128)(2,1)}, bf16[864,1024]{1,0:T(8,128)(2,1)}, f32[96,1024]{1,0:T(8,128)S(1)}, f32[96,1024]{1,0:T(8,128)S(1)}, bf16[3,96,864]{...) custom-call(bf16[96,1024]{1,0:T(8,128)(2,1)S(1)} %copy-done, ...), custom_call_target="tpu_custom_call" | custom-call | flops 4294967296 | bytes 1048576 | tf_op jit(solution)/shard_map/prep/pallas_call | solution.py:265
  16.7 1.5 %copy-done.6 = bf16[864,1024]{1,0:T(8,128)(2,1)S(1)} copy-done((bf16[864,1024]{1,0:T(8,128)(2,1)S(1)}, bf16[864,1024]{1,0:T(8,128)(2,1)}, u32[]{:S(2)}) %copy-start.6) | copy-done | bytes 1769496
  18.2 5.1 %gradients.1 = (bf16[2048,128]{1,0:T(8,128)(2,1)S(1)}, bf16[2048,128]{1,0:T(8,128)(2,1)S(1)}, bf16[96,1024]{1,0:T(8,128)(2,1)S(1)}, bf16[96,128]{1,0:T(8,128)(2,1)S(1)}, bf16[96,128]{1,0:T(8,128)(2,1)S(1)}) custom-call(bf16[864,1024]{1,0:T(8,128)(2,1)S(1)} %copy-done.6, bf16[864,1024]{1,0:T(8,128)(2,1)} %get-tuple-element.30.g_ref, ...), custom_call_target="tpu_custom_call" | custom-call | flops 4294967296 | bytes 1048576 | tf_op jit(solution)/shard_map/gradients/pallas_call | solution.py:265
  23.3 1.1 %collective-permute-start.4 = (bf16[2048,128]{1,0:T(8,128)(2,1)S(1)}, bf16[2048,128]{1,0:T(8,128)(2,1)S(1)}, u32[]{:S(2)}, u32[]{:S(2)}) collective-permute-start(bf16[2048,128]{1,0:T(8,128)(2,1)S(1)} %get-tuple-element.44), channel_id=1, source_target_pairs={{0,32},{32,0},{64,96},{96,64},{128,160},{160,128},{192,224},{224,1... | collective-permute-start | bytes 1572872 | tf_op jit(solution)/shard_map/ppermute | solution.py:316
  24.4 1.5 %collective-permute-done.4.refs_1_ = bf16[2048,128]{1,0:T(8,128)(2,1)S(1)} collective-permute-done((bf16[2048,128]{1,0:T(8,128)(2,1)S(1)}, bf16[2048,128]{1,0:T(8,128)(2,1)S(1)}, u32[]{:S(2)}, u32[]{:S(2)}) %collective-permute-start.4) | collective-permute-done | bytes 524320 | tf_op jit(solution)/shard_map/ppermute | solution.py:316
  25.9 0.3 sum_core.1
  26.2 5.8 %collective-permute-start.5 = (bf16[512,128]{1,0:T(8,128)(2,1)S(1)}, bf16[512,128]{1,0:T(8,128)(2,1)S(1)}, u32[]{:S(2)}, u32[]{:S(2)}) collective-permute-start(bf16[512,128]{1,0:T(8,128)(2,1)S(1)} %get-tuple-element.46), channel_id=1, source_target_pairs={{0,8},{1,9},{2,10},{3,11},{4,12},{5,13},{6,14},{7,15},{8,16},{9,17... | collective-permute-start | bytes 393224 | tf_op jit(solution)/shard_map/ppermute | solution.py:318
  32.0 2.7 %collective-permute-start.6 = (bf16[512,128]{1,0:T(8,128)(2,1)S(1)}, bf16[512,128]{1,0:T(8,128)(2,1)S(1)}, u32[]{:S(2)}, u32[]{:S(2)}) collective-permute-start(bf16[512,128]{1,0:T(8,128)(2,1)S(1)} %get-tuple-element.47), channel_id=1, source_target_pairs={{0,16},{1,17},{2,18},{3,19},{4,20},{5,21},{6,22},{7,23},{8,24},{9,... | collective-permute-start | bytes 393224 | tf_op jit(solution)/shard_map/ppermute | solution.py:318
  34.8 0.9 collective-permute-start.7
  35.7 1.5 %collective-permute-done.5.refs_1_ = bf16[512,128]{1,0:T(8,128)(2,1)S(1)} collective-permute-done((bf16[512,128]{1,0:T(8,128)(2,1)S(1)}, bf16[512,128]{1,0:T(8,128)(2,1)S(1)}, u32[]{:S(2)}, u32[]{:S(2)}) %collective-permute-start.5) | collective-permute-done | bytes 131104 | tf_op jit(solution)/shard_map/ppermute | solution.py:318
  37.2 3.7 %collective-permute-done.6.refs_2_ = bf16[512,128]{1,0:T(8,128)(2,1)S(1)} collective-permute-done((bf16[512,128]{1,0:T(8,128)(2,1)S(1)}, bf16[512,128]{1,0:T(8,128)(2,1)S(1)}, u32[]{:S(2)}, u32[]{:S(2)}) %collective-permute-start.6) | collective-permute-done | bytes 131104 | tf_op jit(solution)/shard_map/ppermute | solution.py:318
  41.0 1.4 %collective-permute-start.8 = (bf16[128,128]{1,0:T(8,128)(2,1)S(1)}, bf16[128,128]{1,0:T(8,128)(2,1)S(1)}, u32[]{:S(2)}, u32[]{:S(2)}) collective-permute-start(bf16[128,128]{1,0:T(8,128)(2,1)S(1)} %get-tuple-element.50), channel_id=1, source_target_pairs={{0,64},{32,96},{64,128},{96,160},{128,192},{160,224},{192,0},{224,... | collective-permute-start | bytes 98312 | tf_op jit(solution)/shard_map/ppermute | solution.py:320
  42.3 2.6 %collective-permute-start.9 = (bf16[128,128]{1,0:T(8,128)(2,1)S(1)}, bf16[128,128]{1,0:T(8,128)(2,1)S(1)}, u32[]{:S(2)}, u32[]{:S(2)}) collective-permute-start(bf16[128,128]{1,0:T(8,128)(2,1)S(1)} %get-tuple-element.51), channel_id=1, source_target_pairs={{0,128},{32,160},{64,192},{96,224},{128,0},{160,32},{192,64},{224,... | collective-permute-start | bytes 98312 | tf_op jit(solution)/shard_map/ppermute | solution.py:320
  45.0 1.1 %collective-permute-start.10 = (bf16[128,128]{1,0:T(8,128)(2,1)S(1)}, bf16[128,128]{1,0:T(8,128)(2,1)S(1)}, u32[]{:S(2)}, u32[]{:S(2)}) collective-permute-start(bf16[128,128]{1,0:T(8,128)(2,1)S(1)} %get-tuple-element.52), channel_id=1, source_target_pairs={{0,192},{32,224},{64,0},{96,32},{128,64},{160,96},{192,128},{224,1... | collective-permute-start | bytes 98312 | tf_op jit(solution)/shard_map/ppermute | solution.py:320
  46.0 0.6 collective-permute-done.9.refs_2_
  46.6 1.5 %collective-permute-done.10.refs_3_ = bf16[128,128]{1,0:T(8,128)(2,1)S(1)} collective-permute-done((bf16[128,128]{1,0:T(8,128)(2,1)S(1)}, bf16[128,128]{1,0:T(8,128)(2,1)S(1)}, u32[]{:S(2)}, u32[]{:S(2)}) %collective-permute-start.10) | collective-permute-done | bytes 32800 | tf_op jit(solution)/shard_map/ppermute | solution.py:320
  48.2 1.7 %collective-permute-start.17 = (bf16[128,128]{1,0:T(8,128)(2,1)S(1)}, bf16[128,128]{1,0:T(8,128)(2,1)S(1)}, u32[]{:S(2)}, u32[]{:S(2)}) collective-permute-start(bf16[128,128]{1,0:T(8,128)(2,1)S(1)} %sum_y.1.refs_0_), channel_id=1, source_target_pairs={{0,7},{1,0},{2,1},{3,2},{4,3},{5,4},{6,5},{7,6},{8,15},{9,8},{10,9... | collective-permute-start | bytes 98312 | tf_op jit(solution)/shard_map/ppermute | solution.py:322
  49.9 1.2 %collective-permute-start.16 = (bf16[128,128]{1,0:T(8,128)(2,1)S(1)}, bf16[128,128]{1,0:T(8,128)(2,1)S(1)}, u32[]{:S(2)}, u32[]{:S(2)}) collective-permute-start(bf16[128,128]{1,0:T(8,128)(2,1)S(1)} %sum_y.1.refs_0_), channel_id=1, source_target_pairs={{0,6},{1,7},{2,0},{3,1},{4,2},{5,3},{6,4},{7,5},{8,14},{9,15},{10,... | collective-permute-start | bytes 98312 | tf_op jit(solution)/shard_map/ppermute | solution.py:322
  51.1 1.7 %collective-permute-start.15 = (bf16[128,128]{1,0:T(8,128)(2,1)S(1)}, bf16[128,128]{1,0:T(8,128)(2,1)S(1)}, u32[]{:S(2)}, u32[]{:S(2)}) collective-permute-start(bf16[128,128]{1,0:T(8,128)(2,1)S(1)} %sum_y.1.refs_0_), channel_id=1, source_target_pairs={{0,5},{1,6},{2,7},{3,0},{4,1},{5,2},{6,3},{7,4},{8,13},{9,14},{10,... | collective-permute-start | bytes 98312 | tf_op jit(solution)/shard_map/ppermute | solution.py:322
  52.8 3.3 %collective-permute-start.14 = (bf16[128,128]{1,0:T(8,128)(2,1)S(1)}, bf16[128,128]{1,0:T(8,128)(2,1)S(1)}, u32[]{:S(2)}, u32[]{:S(2)}) collective-permute-start(bf16[128,128]{1,0:T(8,128)(2,1)S(1)} %sum_y.1.refs_0_), channel_id=1, source_target_pairs={{0,4},{1,5},{2,6},{3,7},{4,0},{5,1},{6,2},{7,3},{8,12},{9,13},{10,... | collective-permute-start | bytes 98312 | tf_op jit(solution)/shard_map/ppermute | solution.py:322
  56.0 3.4 %collective-permute-start.12 = (bf16[128,128]{1,0:T(8,128)(2,1)S(1)}, bf16[128,128]{1,0:T(8,128)(2,1)S(1)}, u32[]{:S(2)}, u32[]{:S(2)}) collective-permute-start(bf16[128,128]{1,0:T(8,128)(2,1)S(1)} %sum_y.1.refs_0_), channel_id=1, source_target_pairs={{0,2},{1,3},{2,4},{3,5},{4,6},{5,7},{6,0},{7,1},{8,10},{9,11},{10,... | collective-permute-start | bytes 98312 | tf_op jit(solution)/shard_map/ppermute | solution.py:322
  59.4 1.4 %collective-permute-start.11 = (bf16[128,128]{1,0:T(8,128)(2,1)S(1)}, bf16[128,128]{1,0:T(8,128)(2,1)S(1)}, u32[]{:S(2)}, u32[]{:S(2)}) collective-permute-start(bf16[128,128]{1,0:T(8,128)(2,1)S(1)} %sum_y.1.refs_0_), channel_id=1, source_target_pairs={{0,1},{1,2},{2,3},{3,4},{4,5},{5,6},{6,7},{7,0},{8,9},{9,10},{10,1... | collective-permute-start | bytes 98312 | tf_op jit(solution)/shard_map/ppermute | solution.py:322
  60.8 1.0 %collective-permute-done.13.refs_3_ = bf16[128,128]{1,0:T(8,128)(2,1)S(1)} collective-permute-done((bf16[128,128]{1,0:T(8,128)(2,1)S(1)}, bf16[128,128]{1,0:T(8,128)(2,1)S(1)}, u32[]{:S(2)}, u32[]{:S(2)}) %collective-permute-start.13) | collective-permute-done | bytes 32800 | tf_op jit(solution)/shard_map/ppermute | solution.py:322
  61.8 1.0 %collective-permute-done.12.refs_2_ = bf16[128,128]{1,0:T(8,128)(2,1)S(1)} collective-permute-done((bf16[128,128]{1,0:T(8,128)(2,1)S(1)}, bf16[128,128]{1,0:T(8,128)(2,1)S(1)}, u32[]{:S(2)}, u32[]{:S(2)}) %collective-permute-start.12) | collective-permute-done | bytes 32800 | tf_op jit(solution)/shard_map/ppermute | solution.py:322
  62.8 0.9 collective-permute-done.11.refs_1_
  63.8 2.3 %collective-permute-start.20 = (bf16[128,128]{1,0:T(8,128)(2,1)S(1)}, bf16[128,128]{1,0:T(8,128)(2,1)S(1)}, u32[]{:S(2)}, u32[]{:S(2)}) collective-permute-start(bf16[128,128]{1,0:T(8,128)(2,1)S(1)} %sum_z.1.refs_0_), channel_id=1, source_target_pairs={{0,192},{32,224},{64,0},{96,32},{128,64},{160,96},{192,128},{224,1... | collective-permute-start | bytes 98312 | tf_op jit(solution)/shard_map/ppermute | solution.py:330
  66.1 0.7 collective-permute-start.18
  66.8 0.3 collective-permute-done.20.refs_3_
  67.1 3.3 %collective-permute-done.19.refs_2_ = bf16[128,128]{1,0:T(8,128)(2,1)S(1)} collective-permute-done((bf16[128,128]{1,0:T(8,128)(2,1)S(1)}, bf16[128,128]{1,0:T(8,128)(2,1)S(1)}, u32[]{:S(2)}, u32[]{:S(2)}) %collective-permute-start.19) | collective-permute-done | bytes 32800 | tf_op jit(solution)/shard_map/ppermute | solution.py:330
  70.4 1.9 %collective-permute-start.23 = (bf16[512,128]{1,0:T(8,128)(2,1)S(1)}, bf16[512,128]{1,0:T(8,128)(2,1)S(1)}, u32[]{:S(2)}, u32[]{:S(2)}) collective-permute-start(bf16[512,128]{1,0:T(8,128)(2,1)S(1)} %join_y.1.refs_0_), channel_id=1, source_target_pairs={{0,24},{1,25},{2,26},{3,27},{4,28},{5,29},{6,30},{7,31},{8,0},{9,1... | collective-permute-start | bytes 393224 | tf_op jit(solution)/shard_map/ppermute | solution.py:332
  72.3 1.1 %collective-permute-start.22 = (bf16[512,128]{1,0:T(8,128)(2,1)S(1)}, bf16[512,128]{1,0:T(8,128)(2,1)S(1)}, u32[]{:S(2)}, u32[]{:S(2)}) collective-permute-start(bf16[512,128]{1,0:T(8,128)(2,1)S(1)} %join_y.1.refs_0_), channel_id=1, source_target_pairs={{0,16},{1,17},{2,18},{3,19},{4,20},{5,21},{6,22},{7,23},{8,24},{9,... | collective-permute-start | bytes 393224 | tf_op jit(solution)/shard_map/ppermute | solution.py:332
  73.6 2.1 %collective-permute-done.23.refs_3_ = bf16[512,128]{1,0:T(8,128)(2,1)S(1)} collective-permute-done((bf16[512,128]{1,0:T(8,128)(2,1)S(1)}, bf16[512,128]{1,0:T(8,128)(2,1)S(1)}, u32[]{:S(2)}, u32[]{:S(2)}) %collective-permute-start.23) | collective-permute-done | bytes 131104 | tf_op jit(solution)/shard_map/ppermute | solution.py:332
  75.6 2.1 %collective-permute-done.22.refs_2_ = bf16[512,128]{1,0:T(8,128)(2,1)S(1)} collective-permute-done((bf16[512,128]{1,0:T(8,128)(2,1)S(1)}, bf16[512,128]{1,0:T(8,128)(2,1)S(1)}, u32[]{:S(2)}, u32[]{:S(2)}) %collective-permute-start.22) | collective-permute-done | bytes 131104 | tf_op jit(solution)/shard_map/ppermute | solution.py:332
  77.7 1.3 %collective-permute-done.21.refs_1_ = bf16[512,128]{1,0:T(8,128)(2,1)S(1)} collective-permute-done((bf16[512,128]{1,0:T(8,128)(2,1)S(1)}, bf16[512,128]{1,0:T(8,128)(2,1)S(1)}, u32[]{:S(2)}, u32[]{:S(2)}) %collective-permute-start.21) | collective-permute-done | bytes 131104 | tf_op jit(solution)/shard_map/ppermute | solution.py:332
  79.1 7.9 %collective-permute-start.24 = (bf16[2048,128]{1,0:T(8,128)(2,1)S(1)}, bf16[2048,128]{1,0:T(8,128)(2,1)S(1)}, u32[]{:S(2)}, u32[]{:S(2)}) collective-permute-start(bf16[2048,128]{1,0:T(8,128)(2,1)S(1)} %join_x.1.own_ref), channel_id=1, source_target_pairs={{0,32},{32,0},{64,96},{96,64},{128,160},{160,128},{192,224},{224,1... | collective-permute-start | bytes 1572872 | tf_op jit(solution)/shard_map/ppermute | solution.py:334
  87.0 2.3 %collective-permute-start.2 = (bf16[96,128]{1,0:T(8,128)(2,1)S(1)}, bf16[96,128]{1,0:T(8,128)(2,1)S(1)}, u32[]{:S(2)}, u32[]{:S(2)}) collective-permute-start(bf16[96,128]{1,0:T(8,128)(2,1)S(1)} %get-tuple-element.40), channel_id=1, source_target_pairs={{0,1},{1,2},{2,3},{3,4},{4,5},{5,6},{6,7},{7,8},{8,9},{9,10},{10,1... | collective-permute-start | bytes 73736 | tf_op jit(solution)/shard_map/ppermute | solution.py:340
  89.3 1.5 %collective-permute-start.3 = (bf16[96,128]{1,0:T(8,128)(2,1)S(1)}, bf16[96,128]{1,0:T(8,128)(2,1)S(1)}, u32[]{:S(2)}, u32[]{:S(2)}) collective-permute-start(bf16[96,128]{1,0:T(8,128)(2,1)S(1)} %get-tuple-element.41), channel_id=1, source_target_pairs={{1,0},{2,1},{3,2},{4,3},{5,4},{6,5},{7,6},{8,7},{9,8},{10,9},{11,1... | collective-permute-start | bytes 73736 | tf_op jit(solution)/shard_map/ppermute | solution.py:340
  90.8 3.0 %collective-permute-done.3.high_ref = bf16[96,128]{1,0:T(8,128)(2,1)S(1)} collective-permute-done((bf16[96,128]{1,0:T(8,128)(2,1)S(1)}, bf16[96,128]{1,0:T(8,128)(2,1)S(1)}, u32[]{:S(2)}, u32[]{:S(2)}) %collective-permute-start.3) | collective-permute-done | bytes 24608 | tf_op jit(solution)/shard_map/ppermute | solution.py:340
  93.9 2.4 %features.1 = bf16[96,1024]{1,0:T(8,128)(2,1)} custom-call(bf16[96,1024]{1,0:T(8,128)(2,1)S(1)} %get-tuple-element.39.a1_ref, bf16[96,128]{1,0:T(8,128)(2,1)S(1)} %collective-permute-done.2.low_ref, bf16[96,128]{1,0:T(8,128)(2,1)S(1)} %collective-permute-done.3.high_ref, bf16[3,128,1152]{2,1,0:T(8,128)(2,1)S(1)} %get-tuple-element.35.sel_ref, ...), custom_call_target="tpu_custom_call" | custom-call | flops 4294967296 | bytes 1048576 | tf_op jit(solution)/shard_map/features/pallas_call | solution.py:265
  96.3 2.5 %unpack.1 = (f32[27,96,96]{2,1,0:T(8,128)}, f32[27,96,96]{2,1,0:T(8,128)}) custom-call(bf16[2048,128]{1,0:T(8,128)(2,1)S(1)} %join_x.1.own_ref, bf16[2048,128]{1,0:T(8,128)(2,1)S(1)} %collective-permute-done.24.other_ref), custom_call_target="tpu_custom_call" | custom-call | bytes 1048576 | tf_op jit(solution)/shard_map/unpack/pallas_call | solution.py:265
  (27 shorter events, 0.6 us)
Async XLA Ops:
  0.6 0.9 copy-start
  1.6 0.9 copy-start.1
  2.5 0.7 copy-start.2
  3.3 13.5 %collective-permute-start = (bf16[192,128]{1,0:T(8,128)(2,1)S(1)}, bf16[192,128]{1,0:T(8,128)(2,1)S(1)}, u32[]{:S(2)}, u32[]{:S(2)}) collective-permute-start(bf16[192,128]{1,0:T(8,128)(2,1)S(1)} %get-tuple-element.37), channel_id=1, source_target_pairs={{0,1},{1,2},{2,3},{3,4},{4,5},{5,6},{6,7},{7,8},{8,9},{9,10},{10,1... | collective-permute-start | bytes 147464 | tf_op jit(solution)/shard_map/ppermute | solution.py:340
  7.7 9.1 %collective-permute-start.1 = (bf16[192,128]{1,0:T(8,128)(2,1)S(1)}, bf16[192,128]{1,0:T(8,128)(2,1)S(1)}, u32[]{:S(2)}, u32[]{:S(2)}) collective-permute-start(bf16[192,128]{1,0:T(8,128)(2,1)S(1)} %get-tuple-element.38), channel_id=1, source_target_pairs={{1,0},{2,1},{3,2},{4,3},{5,4},{6,5},{7,6},{8,7},{9,8},{10,9},{11,1... | collective-permute-start | bytes 147464 | tf_op jit(solution)/shard_map/ppermute | solution.py:340
  9.0 1.1 %copy-start.3 = (bf16[27,96,96]{2,1,0:T(8,128)(2,1)S(1)}, bf16[27,96,96]{2,1,0:T(8,128)(2,1)}, u32[]{:S(2)}) copy-start(bf16[27,96,96]{2,1,0:T(8,128)(2,1)} %param.9) | copy-start | bytes 1492996
  10.1 1.1 %copy-start.4 = (bf16[27,96,96]{2,1,0:T(8,128)(2,1)S(1)}, bf16[27,96,96]{2,1,0:T(8,128)(2,1)}, u32[]{:S(2)}) copy-start(bf16[27,96,96]{2,1,0:T(8,128)(2,1)} %param.10) | copy-start | bytes 1492996
  11.1 0.7 copy-start.5
  16.7 1.5 %copy-start.6 = (bf16[864,1024]{1,0:T(8,128)(2,1)S(1)}, bf16[864,1024]{1,0:T(8,128)(2,1)}, u32[]{:S(2)}) copy-start(bf16[864,1024]{1,0:T(8,128)(2,1)} %get-tuple-element.29.a_ref) | copy-start | bytes 5308420
  23.3 2.6 %collective-permute-start.4 = (bf16[2048,128]{1,0:T(8,128)(2,1)S(1)}, bf16[2048,128]{1,0:T(8,128)(2,1)S(1)}, u32[]{:S(2)}, u32[]{:S(2)}) collective-permute-start(bf16[2048,128]{1,0:T(8,128)(2,1)S(1)} %get-tuple-element.44), channel_id=1, source_target_pairs={{0,32},{32,0},{64,96},{96,64},{128,160},{160,128},{192,224},{224,1... | collective-permute-start | bytes 1572872 | tf_op jit(solution)/shard_map/ppermute | solution.py:316
  26.2 11.0 %collective-permute-start.5 = (bf16[512,128]{1,0:T(8,128)(2,1)S(1)}, bf16[512,128]{1,0:T(8,128)(2,1)S(1)}, u32[]{:S(2)}, u32[]{:S(2)}) collective-permute-start(bf16[512,128]{1,0:T(8,128)(2,1)S(1)} %get-tuple-element.46), channel_id=1, source_target_pairs={{0,8},{1,9},{2,10},{3,11},{4,12},{5,13},{6,14},{7,15},{8,16},{9,17... | collective-permute-start | bytes 393224 | tf_op jit(solution)/shard_map/ppermute | solution.py:318
  32.0 8.8 %collective-permute-start.6 = (bf16[512,128]{1,0:T(8,128)(2,1)S(1)}, bf16[512,128]{1,0:T(8,128)(2,1)S(1)}, u32[]{:S(2)}, u32[]{:S(2)}) collective-permute-start(bf16[512,128]{1,0:T(8,128)(2,1)S(1)} %get-tuple-element.47), channel_id=1, source_target_pairs={{0,16},{1,17},{2,18},{3,19},{4,20},{5,21},{6,22},{7,23},{8,24},{9,... | collective-permute-start | bytes 393224 | tf_op jit(solution)/shard_map/ppermute | solution.py:318
  34.8 6.1 %collective-permute-start.7 = (bf16[512,128]{1,0:T(8,128)(2,1)S(1)}, bf16[512,128]{1,0:T(8,128)(2,1)S(1)}, u32[]{:S(2)}, u32[]{:S(2)}) collective-permute-start(bf16[512,128]{1,0:T(8,128)(2,1)S(1)} %get-tuple-element.48), channel_id=1, source_target_pairs={{0,24},{1,25},{2,26},{3,27},{4,28},{5,29},{6,30},{7,31},{8,0},{9,1... | collective-permute-start | bytes 393224 | tf_op jit(solution)/shard_map/ppermute | solution.py:318
  41.0 5.1 %collective-permute-start.8 = (bf16[128,128]{1,0:T(8,128)(2,1)S(1)}, bf16[128,128]{1,0:T(8,128)(2,1)S(1)}, u32[]{:S(2)}, u32[]{:S(2)}) collective-permute-start(bf16[128,128]{1,0:T(8,128)(2,1)S(1)} %get-tuple-element.50), channel_id=1, source_target_pairs={{0,64},{32,96},{64,128},{96,160},{128,192},{160,224},{192,0},{224,... | collective-permute-start | bytes 98312 | tf_op jit(solution)/shard_map/ppermute | solution.py:320
  42.3 4.3 %collective-permute-start.9 = (bf16[128,128]{1,0:T(8,128)(2,1)S(1)}, bf16[128,128]{1,0:T(8,128)(2,1)S(1)}, u32[]{:S(2)}, u32[]{:S(2)}) collective-permute-start(bf16[128,128]{1,0:T(8,128)(2,1)S(1)} %get-tuple-element.51), channel_id=1, source_target_pairs={{0,128},{32,160},{64,192},{96,224},{128,0},{160,32},{192,64},{224,... | collective-permute-start | bytes 98312 | tf_op jit(solution)/shard_map/ppermute | solution.py:320
  45.0 3.2 %collective-permute-start.10 = (bf16[128,128]{1,0:T(8,128)(2,1)S(1)}, bf16[128,128]{1,0:T(8,128)(2,1)S(1)}, u32[]{:S(2)}, u32[]{:S(2)}) collective-permute-start(bf16[128,128]{1,0:T(8,128)(2,1)S(1)} %get-tuple-element.52), channel_id=1, source_target_pairs={{0,192},{32,224},{64,0},{96,32},{128,64},{160,96},{192,128},{224,1... | collective-permute-start | bytes 98312 | tf_op jit(solution)/shard_map/ppermute | solution.py:320
  48.2 7.8 %collective-permute-start.17 = (bf16[128,128]{1,0:T(8,128)(2,1)S(1)}, bf16[128,128]{1,0:T(8,128)(2,1)S(1)}, u32[]{:S(2)}, u32[]{:S(2)}) collective-permute-start(bf16[128,128]{1,0:T(8,128)(2,1)S(1)} %sum_y.1.refs_0_), channel_id=1, source_target_pairs={{0,7},{1,0},{2,1},{3,2},{4,3},{5,4},{6,5},{7,6},{8,15},{9,8},{10,9... | collective-permute-start | bytes 98312 | tf_op jit(solution)/shard_map/ppermute | solution.py:322
  49.9 9.5 %collective-permute-start.16 = (bf16[128,128]{1,0:T(8,128)(2,1)S(1)}, bf16[128,128]{1,0:T(8,128)(2,1)S(1)}, u32[]{:S(2)}, u32[]{:S(2)}) collective-permute-start(bf16[128,128]{1,0:T(8,128)(2,1)S(1)} %sum_y.1.refs_0_), channel_id=1, source_target_pairs={{0,6},{1,7},{2,0},{3,1},{4,2},{5,3},{6,4},{7,5},{8,14},{9,15},{10,... | collective-permute-start | bytes 98312 | tf_op jit(solution)/shard_map/ppermute | solution.py:322
  51.1 9.7 %collective-permute-start.15 = (bf16[128,128]{1,0:T(8,128)(2,1)S(1)}, bf16[128,128]{1,0:T(8,128)(2,1)S(1)}, u32[]{:S(2)}, u32[]{:S(2)}) collective-permute-start(bf16[128,128]{1,0:T(8,128)(2,1)S(1)} %sum_y.1.refs_0_), channel_id=1, source_target_pairs={{0,5},{1,6},{2,7},{3,0},{4,1},{5,2},{6,3},{7,4},{8,13},{9,14},{10,... | collective-permute-start | bytes 98312 | tf_op jit(solution)/shard_map/ppermute | solution.py:322
  52.8 8.0 %collective-permute-start.14 = (bf16[128,128]{1,0:T(8,128)(2,1)S(1)}, bf16[128,128]{1,0:T(8,128)(2,1)S(1)}, u32[]{:S(2)}, u32[]{:S(2)}) collective-permute-start(bf16[128,128]{1,0:T(8,128)(2,1)S(1)} %sum_y.1.refs_0_), channel_id=1, source_target_pairs={{0,4},{1,5},{2,6},{3,7},{4,0},{5,1},{6,2},{7,3},{8,12},{9,13},{10,... | collective-permute-start | bytes 98312 | tf_op jit(solution)/shard_map/ppermute | solution.py:322
  56.0 5.8 %collective-permute-start.13 = (bf16[128,128]{1,0:T(8,128)(2,1)S(1)}, bf16[128,128]{1,0:T(8,128)(2,1)S(1)}, u32[]{:S(2)}, u32[]{:S(2)}) collective-permute-start(bf16[128,128]{1,0:T(8,128)(2,1)S(1)} %sum_y.1.refs_0_), channel_id=1, source_target_pairs={{0,3},{1,4},{2,5},{3,6},{4,7},{5,0},{6,1},{7,2},{8,11},{9,12},{10,... | collective-permute-start | bytes 98312 | tf_op jit(solution)/shard_map/ppermute | solution.py:322
  56.0 6.8 %collective-permute-start.12 = (bf16[128,128]{1,0:T(8,128)(2,1)S(1)}, bf16[128,128]{1,0:T(8,128)(2,1)S(1)}, u32[]{:S(2)}, u32[]{:S(2)}) collective-permute-start(bf16[128,128]{1,0:T(8,128)(2,1)S(1)} %sum_y.1.refs_0_), channel_id=1, source_target_pairs={{0,2},{1,3},{2,4},{3,5},{4,6},{5,7},{6,0},{7,1},{8,10},{9,11},{10,... | collective-permute-start | bytes 98312 | tf_op jit(solution)/shard_map/ppermute | solution.py:322
  59.4 4.3 %collective-permute-start.11 = (bf16[128,128]{1,0:T(8,128)(2,1)S(1)}, bf16[128,128]{1,0:T(8,128)(2,1)S(1)}, u32[]{:S(2)}, u32[]{:S(2)}) collective-permute-start(bf16[128,128]{1,0:T(8,128)(2,1)S(1)} %sum_y.1.refs_0_), channel_id=1, source_target_pairs={{0,1},{1,2},{2,3},{3,4},{4,5},{5,6},{6,7},{7,0},{8,9},{9,10},{10,1... | collective-permute-start | bytes 98312 | tf_op jit(solution)/shard_map/ppermute | solution.py:322
  63.8 3.3 %collective-permute-start.20 = (bf16[128,128]{1,0:T(8,128)(2,1)S(1)}, bf16[128,128]{1,0:T(8,128)(2,1)S(1)}, u32[]{:S(2)}, u32[]{:S(2)}) collective-permute-start(bf16[128,128]{1,0:T(8,128)(2,1)S(1)} %sum_z.1.refs_0_), channel_id=1, source_target_pairs={{0,192},{32,224},{64,0},{96,32},{128,64},{160,96},{192,128},{224,1... | collective-permute-start | bytes 98312 | tf_op jit(solution)/shard_map/ppermute | solution.py:330
  66.1 4.3 %collective-permute-start.19 = (bf16[128,128]{1,0:T(8,128)(2,1)S(1)}, bf16[128,128]{1,0:T(8,128)(2,1)S(1)}, u32[]{:S(2)}, u32[]{:S(2)}) collective-permute-start(bf16[128,128]{1,0:T(8,128)(2,1)S(1)} %sum_z.1.refs_0_), channel_id=1, source_target_pairs={{0,128},{32,160},{64,192},{96,224},{128,0},{160,32},{192,64},{224,... | collective-permute-start | bytes 98312 | tf_op jit(solution)/shard_map/ppermute | solution.py:330
  66.1 4.3 %collective-permute-start.18 = (bf16[128,128]{1,0:T(8,128)(2,1)S(1)}, bf16[128,128]{1,0:T(8,128)(2,1)S(1)}, u32[]{:S(2)}, u32[]{:S(2)}) collective-permute-start(bf16[128,128]{1,0:T(8,128)(2,1)S(1)} %sum_z.1.refs_0_), channel_id=1, source_target_pairs={{0,64},{32,96},{64,128},{96,160},{128,192},{160,224},{192,0},{224,... | collective-permute-start | bytes 98312 | tf_op jit(solution)/shard_map/ppermute | solution.py:330
  70.4 5.2 %collective-permute-start.23 = (bf16[512,128]{1,0:T(8,128)(2,1)S(1)}, bf16[512,128]{1,0:T(8,128)(2,1)S(1)}, u32[]{:S(2)}, u32[]{:S(2)}) collective-permute-start(bf16[512,128]{1,0:T(8,128)(2,1)S(1)} %join_y.1.refs_0_), channel_id=1, source_target_pairs={{0,24},{1,25},{2,26},{3,27},{4,28},{5,29},{6,30},{7,31},{8,0},{9,1... | collective-permute-start | bytes 393224 | tf_op jit(solution)/shard_map/ppermute | solution.py:332
  72.3 5.4 %collective-permute-start.22 = (bf16[512,128]{1,0:T(8,128)(2,1)S(1)}, bf16[512,128]{1,0:T(8,128)(2,1)S(1)}, u32[]{:S(2)}, u32[]{:S(2)}) collective-permute-start(bf16[512,128]{1,0:T(8,128)(2,1)S(1)} %join_y.1.refs_0_), channel_id=1, source_target_pairs={{0,16},{1,17},{2,18},{3,19},{4,20},{5,21},{6,22},{7,23},{8,24},{9,... | collective-permute-start | bytes 393224 | tf_op jit(solution)/shard_map/ppermute | solution.py:332
  73.4 5.6 %collective-permute-start.21 = (bf16[512,128]{1,0:T(8,128)(2,1)S(1)}, bf16[512,128]{1,0:T(8,128)(2,1)S(1)}, u32[]{:S(2)}, u32[]{:S(2)}) collective-permute-start(bf16[512,128]{1,0:T(8,128)(2,1)S(1)} %join_y.1.refs_0_), channel_id=1, source_target_pairs={{0,8},{1,9},{2,10},{3,11},{4,12},{5,13},{6,14},{7,15},{8,16},{9,17... | collective-permute-start | bytes 393224 | tf_op jit(solution)/shard_map/ppermute | solution.py:332
  79.1 17.2 %collective-permute-start.24 = (bf16[2048,128]{1,0:T(8,128)(2,1)S(1)}, bf16[2048,128]{1,0:T(8,128)(2,1)S(1)}, u32[]{:S(2)}, u32[]{:S(2)}) collective-permute-start(bf16[2048,128]{1,0:T(8,128)(2,1)S(1)} %join_x.1.own_ref), channel_id=1, source_target_pairs={{0,32},{32,0},{64,96},{96,64},{128,160},{160,128},{192,224},{224,1... | collective-permute-start | bytes 1572872 | tf_op jit(solution)/shard_map/ppermute | solution.py:334
  87.0 3.9 %collective-permute-start.2 = (bf16[96,128]{1,0:T(8,128)(2,1)S(1)}, bf16[96,128]{1,0:T(8,128)(2,1)S(1)}, u32[]{:S(2)}, u32[]{:S(2)}) collective-permute-start(bf16[96,128]{1,0:T(8,128)(2,1)S(1)} %get-tuple-element.40), channel_id=1, source_target_pairs={{0,1},{1,2},{2,3},{3,4},{4,5},{5,6},{6,7},{7,8},{8,9},{9,10},{10,1... | collective-permute-start | bytes 73736 | tf_op jit(solution)/shard_map/ppermute | solution.py:340
  89.3 4.6 %collective-permute-start.3 = (bf16[96,128]{1,0:T(8,128)(2,1)S(1)}, bf16[96,128]{1,0:T(8,128)(2,1)S(1)}, u32[]{:S(2)}, u32[]{:S(2)}) collective-permute-start(bf16[96,128]{1,0:T(8,128)(2,1)S(1)} %get-tuple-element.41), channel_id=1, source_target_pairs={{1,0},{2,1},{3,2},{4,3},{5,4},{6,5},{7,6},{8,7},{9,8},{10,9},{11,1... | collective-permute-start | bytes 73736 | tf_op jit(solution)/shard_map/ppermute | solution.py:340

commit v2 on v1

v2 whole, which is shorter than its diff:
```python
import jax
import jax.numpy as jnp
from jax import lax
from jax.experimental import pallas as pl
from jax.experimental.pallas import tpu as pltpu
from jax.sharding import PartitionSpec as P

CH = 96
PAIRS = [(dy, dz) for dy in (-1, 0, 1) for dz in (-1, 0, 1)]
K9 = 9 * CH
F32 = jnp.float32
BF16 = jnp.bfloat16
NN = (((1,), (0,)), ((), ()))
NT = (((1,), (1,)), ((), ()))
VMEM = pl.BlockSpec(memory_space=pltpu.VMEM)
SMEM = pl.BlockSpec(memory_space=pltpu.SMEM)
ANY = pl.BlockSpec(memory_space=pl.ANY)
HBM = pl.BlockSpec(memory_space=pltpu.HBM)
BOTH = ("group", "dev")
ROWS = 4096
HALF = ROWS // 2
PACKED = 648
AROUND = 32
INPUTS = [pltpu.VMEM((CH, 1024), BF16), pltpu.VMEM((CH, 1024), BF16), pltpu.VMEM((1, 1024), jnp.int32)]


def dot(a, b, dims=NN):
    return lax.dot_general(a, b, dims, preferred_element_type=F32)


def lanes_low(rows):
    return lax.broadcasted_iota(jnp.int32, (rows, 128), 1) < 64


def pair_planes(first, second):
    low = lanes_low(first.shape[0])
    even = jnp.where(low, first, pltpu.roll(second, 64, 1))
    odd = jnp.where(low, pltpu.roll(first, 64, 1), second)
    return even, odd


def to_planes(ref, x):
    first = ref[:, x * 64 : x * 64 + 128].astype(F32)
    second = ref[:, 512 + x * 64 : 640 + x * 64].astype(F32)
    return pair_planes(first, second)


def selection(nb_ref, face):
    base = {0: 0, -1: 2, 1: 4}[face]
    lane = lax.broadcasted_iota(jnp.int32, (1, 128), 1)
    source = lax.broadcasted_iota(jnp.int32, (128, 128), 0)
    y = (lane // 8) % 8
    z = lane % 8
    pieces = []
    for dy, dz in PAIRS:
        far_y = y + dy
        far_z = z + dz
        out_y = (far_y < 0) | (far_y > 7)
        out_z = (far_z < 0) | (far_z > 7)

        def entry(block):
            def at(sy, sz):
                return nb_ref[block, (face + 1) * 9 + (sy + 1) * 3 + sz + 1] - base

            return jnp.where(
                out_y,
                jnp.where(out_z, at(dy, dz), at(dy, 0)),
                jnp.where(out_z, at(0, dz), at(0, 0)),
            )

        found = jnp.where(lane < 64, entry(0), entry(1))
        column = found * 64 + (far_y & 7) * 8 + (far_z & 7)
        column = jnp.where(found < 0, -1, column)
        pieces.append(jnp.where(source == column, 1.0, 0.0).astype(BF16))
    return pieces


def fetch(sources, targets, sems):
    copies = [
        pltpu.make_async_copy(source, target, sems.at[k])
        for k, (source, target) in enumerate(zip(sources, targets))
    ]
    for copy in copies:
        copy.start()
    return copies


def rim_kernel(feat_hbm, cot_hbm, occ_hbm, low_ref, high_ref, feat_ref, cot_ref, occ_ref, sems):
    for copy in fetch((feat_hbm, cot_hbm, occ_hbm), (feat_ref, cot_ref, occ_ref), sems):
        copy.wait()
    for x, pick, out_ref in ((0, 0, low_ref), (6, 1, high_ref)):
        mask = to_planes(occ_ref, x)[pick] > 0
        for row, ref in ((0, feat_ref), (CH, cot_ref)):
            plane = to_planes(ref, x)[pick]
            out_ref[row : row + CH, :] = jnp.where(mask, plane, 0.0).astype(BF16)


def turned(w_ref, d):
    return w_ref[d * K9 : (d + 1) * K9, :].astype(F32).T.astype(BF16)


def prep_kernel(
    feat_hbm, cot_hbm, occ_hbm, w1_hbm, w2_hbm, nb_ref,
    a_ref, g_ref, zp_ref, gp_ref, w1t_ref, wb_ref, sel_ref, mask_ref,
    feat_ref, cot_ref, occ_ref, w1_ref, w2_ref, planes_ref, sems,
):
    copies = fetch(
        (occ_hbm, feat_hbm, cot_hbm, w1_hbm, w2_hbm), (occ_ref, feat_ref, cot_ref, w1_ref, w2_ref), sems
    )
    for index, face in enumerate((-1, 0, 1)):
        for j, piece in enumerate(selection(nb_ref, face)):
            sel_ref[index, :, j * 128 : (j + 1) * 128] = piece
    for copy in copies[:3]:
        copy.wait()
    for x in range(0, 8, 2):
        masks = to_planes(occ_ref, x)
        for k in range(2):
            mask_ref[:, (x + k) * 128 : (x + k + 1) * 128] = masks[k]
        for row, ref in ((0, feat_ref), (CH, cot_ref)):
            both = to_planes(ref, x)
            for k in range(2):
                planes_ref[x + k, row : row + CH, :] = jnp.where(masks[k] > 0, both[k], 0.0).astype(BF16)
    stacked = planes_ref[...].reshape(8 * 2 * CH, 128)
    for j in range(9):
        spread = dot(stacked, sel_ref[1, :, j * 128 : (j + 1) * 128]).astype(BF16)
        for x in range(8):
            a_ref[j * CH : (j + 1) * CH, x * 128 : (x + 1) * 128] = spread[x * 2 * CH : x * 2 * CH + CH]
            g_ref[j * CH : (j + 1) * CH, x * 128 : (x + 1) * 128] = spread[x * 2 * CH + CH : (x + 1) * 2 * CH]
    for copy in copies[3:]:
        copy.wait()
    for d in range(3):
        w1t_ref[d] = turned(w1_ref, d)
        wb_ref[d] = jnp.concatenate(
            [w2_ref[(26 - d * 9 - j) * CH : (27 - d * 9 - j) * CH, :] for j in range(9)], axis=1
        )
    for w_ref, v_ref, out_ref in ((w1t_ref, a_ref, zp_ref), (wb_ref, g_ref, gp_ref)):
        out_ref[...] = dot(w_ref[1], v_ref[...])
        out_ref[:, 128:] += dot(w_ref[0], v_ref[:, :896])
        out_ref[:, :896] += dot(w_ref[2], v_ref[:, 128:])


def spread_rim(rim, sel_ref, index, rows):
    full = dot(rim, sel_ref[index]).astype(BF16)
    parts = []
    for r in range(0, rows, CH):
        parts.append(
            jnp.concatenate([full[r : r + CH, j * 128 : (j + 1) * 128] for j in range(9)], axis=0)
        )
    return parts


def main_kernel(
    a_ref, g_ref, zp_ref, gp_ref, w1t_ref, wb_ref, sel_ref, mask_ref, low_ref, high_ref,
    own_ref, send_ref, a1_ref, a1_low_ref, a1_high_ref,
    grad_ref, packed_ref,
):
    scale = 262144.0 ** -0.5
    a_low, g_low = spread_rim(low_ref[...], sel_ref, 0, 2 * CH)
    a_high, g_high = spread_rim(high_ref[...], sel_ref, 2, 2 * CH)

    def finish(partial_ref, w_ref, low, high):
        first = partial_ref[:, :128] + dot(w_ref[0], low)
        last = partial_ref[:, 896:] + dot(w_ref[2], high)
        return mask_ref[...] * jnp.concatenate([first, partial_ref[:, 128:896], last], axis=1)

    z = finish(zp_ref, w1t_ref, a_low, a_high)
    ga = finish(gp_ref, wb_ref, g_low, g_high)
    sigma = 1.0 / (1.0 + jnp.exp(-z))
    a1 = (z * sigma).astype(BF16)
    gz = (ga * sigma * (1.0 + z * (1.0 - sigma))).astype(BF16)
    a1_ref[...] = a1
    a1_low_ref[...] = a1[:, :128]
    a1_high_ref[...] = a1[:, 896:]

    def terms(v_ref, low, high, grad, start):
        zero = jnp.zeros((K9, 32), F32)

        def put(d, value):
            r = start + d * K9
            grad_ref[r : r + K9, :] = jnp.concatenate([value * scale, zero], axis=1)

        put(0, dot(v_ref[:, :896], grad[:, 128:], NT) + dot(low, grad[:, :128], NT))
        put(1, dot(v_ref[...], grad, NT))
        put(2, dot(v_ref[:, 128:], grad[:, :896], NT) + dot(high, grad[:, 896:], NT))

    terms(g_ref, g_low, g_high, a1, 27 * CH)
    terms(a_ref, a_low, a_high, gz, 0)
    lane = lax.broadcasted_iota(jnp.int32, (PACKED, 128), 1)
    for grad in range(2):
        rows = grad * 27 * CH
        base = grad * HALF
        spare = grad_ref[rows + 3 * PACKED : rows + 4 * PACKED, :]
        for k in range(3):
            kept = grad_ref[rows + k * PACKED : rows + (k + 1) * PACKED, :]
            packed_ref[base + k * PACKED : base + (k + 1) * PACKED, :] = jnp.where(
                lane < 96, kept, pltpu.roll(spare, 96 - 32 * k, 1)
            )
        packed_ref[base + 3 * PACKED : base + HALF, :] = jnp.zeros((HALF - 3 * PACKED, 128), F32)
    core = core_index()
    own_ref[...] = packed_ref[pl.ds(pl.multiple_of(core * HALF, HALF), HALF), :]
    send_ref[...] = packed_ref[pl.ds(pl.multiple_of((1 - core) * HALF, HALF), HALF), :].astype(BF16)


def out_kernel(a1_ref, low_ref, high_ref, sel_ref, w2_ref, mask_ref, after_ref, out_ref, v_ref, planes_ref):
    for x in range(8):
        planes_ref[x] = a1_ref[:, x * 128 : (x + 1) * 128]
    stacked = planes_ref[...].reshape(8 * CH, 128)
    for j in range(9):
        spread = dot(stacked, sel_ref[1, :, j * 128 : (j + 1) * 128]).astype(BF16)
        for x in range(8):
            v_ref[j * CH : (j + 1) * CH, (x + 1) * 128 : (x + 2) * 128] = spread[x * CH : (x + 1) * CH]
    v_ref[:, :128] = spread_rim(low_ref[...], sel_ref, 0, CH)[0]
    v_ref[:, 1152:] = spread_rim(high_ref[...], sel_ref, 2, CH)[0]
    total = dot(turned(w2_ref, 0), v_ref[:, :1024])
    total += dot(turned(w2_ref, 1), v_ref[:, 128:1152])
    total += dot(turned(w2_ref, 2), v_ref[:, 256:])
    total = mask_ref[...] * total
    for x in range(0, 8, 2):
        even = total[:, x * 128 : (x + 1) * 128]
        odd = total[:, (x + 1) * 128 : (x + 2) * 128]
        first, second = pair_planes(even, odd)
        out_ref[:, x * 64 : x * 64 + 128] = first.astype(BF16)
        out_ref[:, 512 + x * 64 : 640 + x * 64] = second.astype(BF16)


def core_index():
    return lax.rem(lax.axis_index("group"), 2)


def add_kernel(own_ref, got_ref, out_ref):
    out_ref[...] = (own_ref[...] + got_ref[...].astype(F32)).astype(BF16)


def rows_kernel(got_ref, low_ref, high_ref, out_ref):
    total = got_ref[0].astype(F32)
    for k in range(1, AROUND):
        total += got_ref[k].astype(F32)
    out_ref[...] = total.astype(BF16)


def total_kernel(*refs):
    out_ref, slots_ref = refs[-2:]
    me = lax.rem(lax.axis_index("dev"), 8) // 2
    for k in range(4):
        slots_ref[lax.rem(me + 4 - k, 4)] = refs[k][...]
    total = slots_ref[0].astype(F32)
    for k in range(1, 4):
        total += slots_ref[k].astype(F32)
    total = total.astype(BF16)
    for k in range(AROUND):
        out_ref[k] = total


def grads_kernel(own_ref, other_ref, one_hbm, two_hbm, packed_ref, one_ref, two_ref, sems):
    core = core_index()
    packed_ref[pl.ds(pl.multiple_of(core * HALF, HALF), HALF), :] = own_ref[...].astype(F32)
    packed_ref[pl.ds(pl.multiple_of((1 - core) * HALF, HALF), HALF), :] = other_ref[...].astype(F32)
    lane = lax.broadcasted_iota(jnp.int32, (24, 128), 1)

    def piece(grad, start):
        base = grad * HALF
        if start < 3 * PACKED:
            return packed_ref[base + start : base + start + 24, :]
        r = base + start - 3 * PACKED
        value = pltpu.roll(packed_ref[r : r + 24, :], 32, 1)
        for k in (1, 2):
            moved = pltpu.roll(packed_ref[r + k * PACKED : r + k * PACKED + 24, :], (32 + 32 * k) % 128, 1)
            value = jnp.where(lane < 32 * k, value, moved)
        return value

    def block_of(grad, block):
        return jnp.concatenate([piece(grad, block * CH + 24 * q) for q in range(4)], axis=0)

    copies = []
    for first in range(0, 27, 9):
        for block in range(first, first + 9):
            one_ref[block] = block_of(0, block)[:, :CH]
        part = pl.ds(first, 9)
        copies.append(pltpu.make_async_copy(one_ref.at[part], one_hbm.at[part], sems.at[len(copies)]))
        copies[-1].start()
    for first in range(18, -1, -9):
        for tap in range(first, first + 9):
            wide = jnp.concatenate([block_of(1, 26 - tap), jnp.zeros((32, 128), F32)], axis=0)
            two_ref[tap] = wide.T[:CH, :CH]
        part = pl.ds(first, 9)
        copies.append(pltpu.make_async_copy(two_ref.at[part], two_hbm.at[part], sems.at[len(copies)]))
        copies[-1].start()
    for copy in copies:
        copy.wait()


def shape(dims, dtype=BF16):
    return jax.ShapeDtypeStruct(dims, dtype)


def call(kernel, outs, *args, scratch=(), specs=None, out_specs=None, limit=8, flops=0, name=None):
    specs = specs or {}
    return pl.pallas_call(
        kernel,
        out_shape=outs,
        in_specs=[specs.get(k, VMEM) for k in range(len(args))],
        out_specs=out_specs or jax.tree.map(lambda _: VMEM, outs),
        scratch_shapes=scratch,
        compiler_params=pltpu.CompilerParams(vmem_limit_bytes=limit << 20),
        cost_estimate=pl.CostEstimate(flops=flops, bytes_accessed=1 << 20, transcendentals=0),
        name=name,
    )(*args)


def device_pairs(move):
    pairs = []
    for index in range(256):
        group, dev = index // 32, index % 32
        x, y, z, core = move(dev // 8, group // 2, dev % 8, group % 2)
        pairs.append((index, (y * 2 + core) * 32 + x * 8 + z))
    return pairs


def around_groups():
    return [
        [(y * 2 + core) * 32 + x * 8 + pair * 2 + z for y in range(4) for x in range(4) for z in range(2)]
        for core in range(2)
        for pair in range(4)
    ]


def all_to_all(value):
    return lax.all_to_all(value, BOTH, 0, 0, axis_index_groups=around_groups(), tiled=True)


def swap_core(value):
    return lax.ppermute(value, BOTH, device_pairs(lambda x, y, z, core: (x, y, z, 1 - core)))


def swap_z(value, k):
    return lax.ppermute(value, BOTH, device_pairs(lambda x, y, z, core: (x, y, (z + 2 * k) % 8, core)))


def dev_shift(value, step):
    count = lax.axis_size("dev")
    pairs = [(i, i + step) for i in range(count) if 0 <= i + step < count]
    return lax.ppermute(value, "dev", pairs)


def per_device(features_in, occupancy, cotangent, kernel_one, kernel_two, neighbours):
    occ = occupancy.reshape(1, 1024)
    w1 = kernel_one.reshape(27 * CH, CH)
    w2 = kernel_two.reshape(27 * CH, CH)
    low, high = call(
        rim_kernel,
        [shape((2 * CH, 128))] * 2,
        features_in, cotangent, occ,
        specs={0: HBM, 1: HBM, 2: HBM},
        scratch=INPUTS + [pltpu.SemaphoreType.DMA((3,))],
        name="rims",
    )
    upper = dev_shift(low, -1)
    lower = dev_shift(high, 1)
    a, g, zp, gp, w1t, wb, sel, mask = call(
        prep_kernel,
        [
            shape((K9, 1024)), shape((K9, 1024)), shape((CH, 1024), F32), shape((CH, 1024), F32),
            shape((3, CH, K9)), shape((3, CH, K9)), shape((3, 128, 1152)), shape((1, 1024), F32),
        ],
        features_in, cotangent, occ, w1, w2, neighbours,
        specs={0: HBM, 1: HBM, 2: HBM, 3: HBM, 4: HBM, 5: SMEM},
        scratch=INPUTS + [
            pltpu.VMEM((27 * CH, CH), BF16), pltpu.VMEM((27 * CH, CH), BF16),
            pltpu.VMEM((8, 2 * CH, 128), BF16), pltpu.SemaphoreType.DMA((5,)),
        ],
        limit=16,
        flops=4 << 30,
        name="prep",
    )
    own, send, a1, a1_low, a1_high = call(
        main_kernel,
        [
            shape((HALF, 128), F32), shape((HALF, 128)), shape((CH, 1024)),
            shape((CH, 128)), shape((CH, 128)),
        ],
        a, g, zp, gp, w1t, wb, sel, mask, lower, upper,
        scratch=[pltpu.VMEM((54 * CH, 128), F32), pltpu.VMEM((ROWS, 128), F32)],
        limit=16,
        flops=4 << 30,
        name="gradients",
    )
    got = swap_core(send)
    a1_upper = dev_shift(a1_low, -1)
    a1_lower = dev_shift(a1_high, 1)
    value = call(add_kernel, shape((HALF, 128)), own, got, name="sum_core")
    value = all_to_all(value.reshape(AROUND, HALF // AROUND, 128))
    value = call(
        rows_kernel, shape((HALF // AROUND, 128)), value, a1_lower, a1_upper,
        specs={1: ANY, 2: ANY}, name="sum_around",
    )
    arrived = [value] + [swap_z(value, k) for k in range(1, 4)]
    features_out = call(
        out_kernel,
        shape((CH, 1024)),
        a1, a1_lower, a1_upper, sel, w2, mask, value,
        specs={6: ANY},
        scratch=[pltpu.VMEM((K9, 1280), BF16), pltpu.VMEM((8, CH, 128), BF16)],
        limit=16,
        flops=4 << 30,
        name="features",
    )
    value = call(
        total_kernel, shape((AROUND, HALF // AROUND, 128)), *arrived, features_out,
        specs={4: ANY},
        scratch=[pltpu.VMEM((4, HALF // AROUND, 128), BF16)],
        name="sum_z",
    )
    mine = all_to_all(value).reshape(HALF, 128)
    kernel_one_grad, kernel_two_grad = call(
        grads_kernel,
        [shape((27, CH, CH), F32)] * 2,
        mine, swap_core(mine),
        out_specs=[HBM, HBM],
        scratch=[
            pltpu.VMEM((ROWS, 128), F32), pltpu.VMEM((27, CH, CH), F32), pltpu.VMEM((27, CH, CH), F32),
            pltpu.SemaphoreType.DMA((6,)),
        ],
        limit=16,
        name="unpack",
    )
    return (features_out, kernel_one_grad, kernel_two_grad)


def solution(mesh):
    return jax.shard_map(
        per_device,
        mesh=mesh,
        in_specs=(
            P(None, ("group", "dev")),
            P(("group", "dev")),
            P(None, ("group", "dev")),
            P(),
            P(),
            P(("group", "dev"), None),
        ),
        out_specs=(P(None, ("group", "dev")), P(), P()),
        check_vma=False,
    )
```

time: 99.2 us -> 86.8 us (0.88)
  starting transfers between devices: 51.6 us -> 34.9 us
  blocking collectives: 0 us -> 15.5 us
  waiting for transfers between devices: 24 us -> 10.8 us
  local copies, waits for them, and re-layouts: 6.86 us -> 8.86 us
    ppermute x21 -> x5, starting transfers between devices: 42.1 us -> 13.2 us  [the longest x3 6.72 us: swap_z(): lax.ppermute(value, BOTH, device_pairs(lambda x, y, z, core: (x, y, (z +...]
    ppermute x21 -> x5, waiting for transfers between devices: 20.9 us -> 3.87 us  [the longest x2 3.07 us: swap_core(): lax.ppermute(value, BOTH, device_pairs(lambda x, y, z, core: (x, y, z, 1...]
    all_to_all x0 -> x1, blocking collectives: none -> 15.5 us  [all_to_all(): lax.all_to_all(value, BOTH, 0, 0, axis_index_groups=around_groups(), tile...]
    all_to_all x0 -> x1, starting transfers between devices: none -> 11.6 us  [all_to_all(): lax.all_to_all(value, BOTH, 0, 0, axis_index_groups=around_groups(), tile...]
    all_to_all x0 -> x1, waiting for transfers between devices: none -> 3.05 us  [all_to_all(): lax.all_to_all(value, BOTH, 0, 0, axis_index_groups=around_groups(), tile...]
    unnamed x14 -> x22, local copies, waits for them, and re-layouts: 6.86 us -> 8.86 us
    pallas_call x11 -> x8, Pallas kernels: 15.5 us -> 15.2 us  [call(): pl.pallas_call(kernel, out_shape=outs, in_specs=[specs.get(k, VMEM) for k...]
  transfers between devices with their start and end apart: 25 -> 10, of which waited for: 14 -> 7; matrix products, arithmetic and copies ran while one was open for 0% -> 0% of each run, Pallas kernels for 7% -> 9%
where the time goes in v2:
time: 86.8 us; the launch traced here: 86.2 us
  starting transfers between devices  34.9 us (40%)
  blocking collectives  15.5 us (18%)
  Pallas kernels  15.2 us (18%)
  waiting for transfers between devices  10.8 us (12%)
  local copies, waits for them, and re-layouts  8.86 us (10%)
  between operations  0.91 us (1%)
    all_to_all x1, blocking collectives, all_to_all(): lax.all_to_all(value, BOTH, 0, 0, axis_index_groups=around_groups(), tile...  15.5 us
    pallas_call x8, Pallas kernels, call(): pl.pallas_call(kernel, out_shape=outs, in_specs=[specs.get(k, VMEM) for k...  15.2 us
    all_to_all x1, starting transfers between devices, all_to_all(): lax.all_to_all(value, BOTH, 0, 0, axis_index_groups=around_groups(), tile...  11.6 us
    ppermute x4, starting transfers between devices, dev_shift(): return lax.ppermute(value, 'dev', pairs)  10.1 us
    unnamed x22, local copies, waits for them, and re-layouts  8.86 us
    ppermute x3, starting transfers between devices, swap_z(): lax.ppermute(value, BOTH, device_pairs(lambda x, y, z, core: (x, y, (z +...  6.72 us
    ppermute x2, starting transfers between devices, swap_core(): lax.ppermute(value, BOTH, device_pairs(lambda x, y, z, core: (x, y, z, 1...  6.51 us
    ppermute x4, waiting for transfers between devices, dev_shift(): return lax.ppermute(value, 'dev', pairs)  3.9 us
  transfers between devices with their start and end apart: 10, of which 7 were waited for; matrix products, arithmetic and copies ran while one was open for 0% of the time, Pallas kernels for 9%

profile of v2, /device:TPU:1, one launch (start us, length us, event | category | flops | bytes accessed | tf_op | source)
XLA Modules:
  0.0 86.2 jit_solution(15820894741277725210)
XLA Ops:
  0.6 0.0 copy-start
  0.6 0.9 %copy-done = bf16[96,1024]{1,0:T(8,128)(2,1)S(1)} copy-done((bf16[96,1024]{1,0:T(8,128)(2,1)S(1)}, bf16[96,1024]{1,0:T(8,128)(2,1)}, u32[]{:S(2)}) %copy-start) | copy-done | bytes 196632
  1.6 0.0 copy-start.2
  1.6 0.9 %copy-done.2 = bf16[96,1024]{1,0:T(8,128)(2,1)S(1)} copy-done((bf16[96,1024]{1,0:T(8,128)(2,1)S(1)}, bf16[96,1024]{1,0:T(8,128)(2,1)}, u32[]{:S(2)}) %copy-start.2) | copy-done | bytes 196632
  2.5 0.0 copy-start.5
  2.5 0.7 copy-done.5
  3.2 0.6 rims.1
  3.8 4.4 %collective-permute-start = (bf16[192,128]{1,0:T(8,128)(2,1)S(1)}, bf16[192,128]{1,0:T(8,128)(2,1)S(1)}, u32[]{:S(2)}, u32[]{:S(2)}) collective-permute-start(bf16[192,128]{1,0:T(8,128)(2,1)S(1)} %get-tuple-element.28), channel_id=1, source_target_pairs={{0,1},{1,2},{2,3},{3,4},{4,5},{5,6},{6,7},{7,8},{8,9},{9,10},{10,1... | collective-permute-start | bytes 147464 | tf_op jit(solution)/shard_map/ppermute | solution.py:342
  8.2 1.3 %collective-permute-start.1 = (bf16[192,128]{1,0:T(8,128)(2,1)S(1)}, bf16[192,128]{1,0:T(8,128)(2,1)S(1)}, u32[]{:S(2)}, u32[]{:S(2)}) collective-permute-start(bf16[192,128]{1,0:T(8,128)(2,1)S(1)} %get-tuple-element.29), channel_id=1, source_target_pairs={{1,0},{2,1},{3,2},{4,3},{5,4},{6,5},{7,6},{8,7},{9,8},{10,9},{11,1... | collective-permute-start | bytes 147464 | tf_op jit(solution)/shard_map/ppermute | solution.py:342
  9.5 0.0 copy-start.1
  9.5 0.9 %copy-done.1 = bf16[96,1024]{1,0:T(8,128)(2,1)S(1)} copy-done((bf16[96,1024]{1,0:T(8,128)(2,1)S(1)}, bf16[96,1024]{1,0:T(8,128)(2,1)}, u32[]{:S(2)}) %copy-start.1) | copy-done | bytes 196632
  10.4 0.0 copy-start.3
  10.4 0.9 %copy-done.3 = bf16[96,1024]{1,0:T(8,128)(2,1)S(1)} copy-done((bf16[96,1024]{1,0:T(8,128)(2,1)S(1)}, bf16[96,1024]{1,0:T(8,128)(2,1)}, u32[]{:S(2)}) %copy-start.3) | copy-done | bytes 196632
  11.3 0.0 copy-start.6
  11.3 0.7 copy-done.6
  12.0 0.0 copy-start.7
  12.0 1.1 %copy-done.7 = bf16[27,96,96]{2,1,0:T(8,128)(2,1)S(1)} copy-done((bf16[27,96,96]{2,1,0:T(8,128)(2,1)S(1)}, bf16[27,96,96]{2,1,0:T(8,128)(2,1)}, u32[]{:S(2)}) %copy-start.7) | copy-done | bytes 497688
  13.1 0.0 copy-start.8
  13.1 1.1 %copy-done.8 = bf16[27,96,96]{2,1,0:T(8,128)(2,1)S(1)} copy-done((bf16[27,96,96]{2,1,0:T(8,128)(2,1)S(1)}, bf16[27,96,96]{2,1,0:T(8,128)(2,1)}, u32[]{:S(2)}) %copy-start.8) | copy-done | bytes 497688
  14.2 0.7 copy-done.10
  14.9 5.2 %prep.1 = (bf16[864,1024]{1,0:T(8,128)(2,1)S(1)}, bf16[864,1024]{1,0:T(8,128)(2,1)S(1)}, f32[96,1024]{1,0:T(8,128)S(1)}, f32[96,1024]{1,0:T(8,128)S(1)}, bf16[3,...) custom-call(bf16[96,1024]{1,0:T(8,128)(2,1)S(1)} %copy-done.1, ...), custom_call_target="tpu_custom_call" | custom-call | flops 4294967296 | bytes 1048576 | tf_op jit(solution)/shard_map/prep/pallas_call | solution.py:298
  20.0 0.0 collective-permute-done.low_ref
  20.1 0.0 collective-permute-done.1.high_ref
  20.1 4.0 %gradients.1 = (f32[2048,128]{1,0:T(8,128)S(1)}, bf16[2048,128]{1,0:T(8,128)(2,1)S(1)}, bf16[96,1024]{1,0:T(8,128)(2,1)S(1)}, bf16[96,128]{1,0:T(8,128)(2,1)S(1)}, bf16[96,128]{1,0:T(8,128)(2,1)S(1)}) custom-call(bf16[864,1024]{1,0:T(8,128)(2,1)S(1)} %get-tuple-element.20.a_ref, bf16[864,1024]{1,0:T(8,128)(2,1)S(1)} %get-tuple-element.21.g_ref, ...), custom_call_target="tpu_custom_call" | custom-call | flops 4294967296 | bytes 1048576 | tf_op jit(solution)/shard_map/gradients/pallas_call | solution.py:298
  24.1 1.1 %collective-permute-start.4 = (bf16[2048,128]{1,0:T(8,128)(2,1)S(1)}, bf16[2048,128]{1,0:T(8,128)(2,1)S(1)}, u32[]{:S(2)}, u32[]{:S(2)}) collective-permute-start(bf16[2048,128]{1,0:T(8,128)(2,1)S(1)} %get-tuple-element.34), channel_id=1, source_target_pairs={{0,32},{1,33},{2,34},{3,35},{4,36},{5,37},{6,38},{7,39},{8,40},{9,... | collective-permute-start | bytes 1572872 | tf_op jit(solution)/shard_map/ppermute | solution.py:332
  25.1 1.5 %collective-permute-done.4.got_ref = bf16[2048,128]{1,0:T(8,128)(2,1)S(1)} collective-permute-done((bf16[2048,128]{1,0:T(8,128)(2,1)S(1)}, bf16[2048,128]{1,0:T(8,128)(2,1)S(1)}, u32[]{:S(2)}, u32[]{:S(2)}) %collective-permute-start.4) | collective-permute-done | bytes 524320 | tf_op jit(solution)/shard_map/ppermute | solution.py:332
  26.7 0.9 %sum_core.1 = bf16[2048,128]{1,0:T(8,128)(2,1)} custom-call(f32[2048,128]{1,0:T(8,128)S(1)} %get-tuple-element.33.own_ref, bf16[2048,128]{1,0:T(8,128)(2,1)S(1)} %collective-permute-done.4.got_ref), custom_call_target="tpu_custom_call" | custom-call | bytes 1048576 | tf_op jit(solution)/shard_map/sum_core/pallas_call | solution.py:298
  27.6 11.6 %all-to-all-start = ((bf16[32,64,128]{2,1,0:T(8,128)(2,1)}), bf16[32,64,128]{2,1,0:T(8,128)(2,1)S(1)}, u32[]{:S(2)}, u32[]{:S(2)}) async-start(bf16[32,64,128]{2,1,0:T(8,128)(2,1)} %bitcast.3), calls=%async_computation | async-start | bytes 1048576 | tf_op jit(solution)/shard_map/all_to_all | solution.py:328
  39.2 3.1 %collective-permute-start.2 = (bf16[96,128]{1,0:T(8,128)(2,1)S(1)}, bf16[96,128]{1,0:T(8,128)(2,1)S(1)}, u32[]{:S(2)}, u32[]{:S(2)}) collective-permute-start(bf16[96,128]{1,0:T(8,128)(2,1)S(1)} %get-tuple-element.31), channel_id=1, source_target_pairs={{0,1},{1,2},{2,3},{3,4},{4,5},{5,6},{6,7},{7,8},{8,9},{9,10},{10,1... | collective-permute-start | bytes 73736 | tf_op jit(solution)/shard_map/ppermute | solution.py:342
  42.3 1.3 %collective-permute-start.3 = (bf16[96,128]{1,0:T(8,128)(2,1)S(1)}, bf16[96,128]{1,0:T(8,128)(2,1)S(1)}, u32[]{:S(2)}, u32[]{:S(2)}) collective-permute-start(bf16[96,128]{1,0:T(8,128)(2,1)S(1)} %get-tuple-element.32), channel_id=1, source_target_pairs={{1,0},{2,1},{3,2},{4,3},{5,4},{6,5},{7,6},{8,7},{9,8},{10,9},{11,1... | collective-permute-start | bytes 73736 | tf_op jit(solution)/shard_map/ppermute | solution.py:342
  43.6 1.4 %collective-permute-done.2.low_ref = bf16[96,128]{1,0:T(8,128)(2,1)S(1)} collective-permute-done((bf16[96,128]{1,0:T(8,128)(2,1)S(1)}, bf16[96,128]{1,0:T(8,128)(2,1)S(1)}, u32[]{:S(2)}, u32[]{:S(2)}) %collective-permute-start.2) | collective-permute-done | bytes 24608 | tf_op jit(solution)/shard_map/ppermute | solution.py:342
  45.0 2.5 %collective-permute-done.3.high_ref = bf16[96,128]{1,0:T(8,128)(2,1)S(1)} collective-permute-done((bf16[96,128]{1,0:T(8,128)(2,1)S(1)}, bf16[96,128]{1,0:T(8,128)(2,1)S(1)}, u32[]{:S(2)}, u32[]{:S(2)}) %collective-permute-start.3) | collective-permute-done | bytes 24608 | tf_op jit(solution)/shard_map/ppermute | solution.py:342
  47.5 3.0 %all-to-all-done.got_ref = bf16[32,64,128]{2,1,0:T(8,128)(2,1)S(1)} async-done(((bf16[32,64,128]{2,1,0:T(8,128)(2,1)}), bf16[32,64,128]{2,1,0:T(8,128)(2,1)S(1)}, u32[]{:S(2)}, u32[]{:S(2)}) %all-to-all-start) | async-done | bytes 524320 | tf_op jit(solution)/shard_map/all_to_all | solution.py:328
  50.6 0.1 sum_around.1.after_ref.refs_0_
  50.7 2.7 %collective-permute-start.7 = (bf16[64,128]{1,0:T(8,128)(2,1)S(1)}, bf16[64,128]{1,0:T(8,128)(2,1)S(1)}, u32[]{:S(2)}, u32[]{:S(2)}) collective-permute-start(bf16[64,128]{1,0:T(8,128)(2,1)S(1)} %sum_around.1.after_ref.refs_0_), channel_id=1, source_target_pairs={{0,6},{1,7},{2,0},{3,1},{4,2},{5,3},{6,4},{7,5},{8,14},{9,15},{10,... | collective-permute-start | bytes 49160 | tf_op jit(solution)/shard_map/ppermute | solution.py:336
  53.4 2.3 %collective-permute-start.6 = (bf16[64,128]{1,0:T(8,128)(2,1)S(1)}, bf16[64,128]{1,0:T(8,128)(2,1)S(1)}, u32[]{:S(2)}, u32[]{:S(2)}) collective-permute-start(bf16[64,128]{1,0:T(8,128)(2,1)S(1)} %sum_around.1.after_ref.refs_0_), channel_id=1, source_target_pairs={{0,4},{1,5},{2,6},{3,7},{4,0},{5,1},{6,2},{7,3},{8,12},{9,13},{10,... | collective-permute-start | bytes 49160 | tf_op jit(solution)/shard_map/ppermute | solution.py:336
  55.7 1.7 %collective-permute-start.5 = (bf16[64,128]{1,0:T(8,128)(2,1)S(1)}, bf16[64,128]{1,0:T(8,128)(2,1)S(1)}, u32[]{:S(2)}, u32[]{:S(2)}) collective-permute-start(bf16[64,128]{1,0:T(8,128)(2,1)S(1)} %sum_around.1.after_ref.refs_0_), channel_id=1, source_target_pairs={{0,2},{1,3},{2,4},{3,5},{4,6},{5,7},{6,0},{7,1},{8,10},{9,11},{10,... | collective-permute-start | bytes 49160 | tf_op jit(solution)/shard_map/ppermute | solution.py:336
  57.4 0.0 copy-done.9
  57.4 2.3 %features.1.refs_4_ = bf16[96,1024]{1,0:T(8,128)(2,1)} custom-call(bf16[96,1024]{1,0:T(8,128)(2,1)S(1)} %get-tuple-element.30.a1_ref, bf16[96,128]{1,0:T(8,128)(2,1)S(1)} %collective-permute-done.2.low_ref, bf16[96,128]{1,0:T(8,128)(2,1)S(1)} %collective-permute-done.3.high_ref, bf16[3,128,1152]{2,1,0:T(8,128)(2,1)S(1)} %get-tuple-element.26.sel_ref, ...), custom_call_target="tpu_custom_call" | custom-call | flops 4294967296 | bytes 1048576 | tf_op jit(solution)/shard_map/features/pallas_call | solution.py:298
  59.7 0.0 collective-permute-done.7.refs_3_
  59.7 0.2 collective-permute-done.6.refs_2_
  59.9 0.6 collective-permute-done.5.refs_1_
  60.5 0.9 %copy-done.4 = bf16[96,1024]{1,0:T(8,128)(2,1)S(1)} copy-done((bf16[96,1024]{1,0:T(8,128)(2,1)S(1)}, bf16[96,1024]{1,0:T(8,128)(2,1)}, u32[]{:S(2)}) %copy-start.4) | copy-done | bytes 196632
  61.4 0.1 sum_z.1
  61.5 15.5 %all_to_all.10 = bf16[32,64,128]{2,1,0:T(8,128)(2,1)S(1)} all-to-all(bf16[32,64,128]{2,1,0:T(8,128)(2,1)S(1)} %sum_z.1), channel_id=1, replica_groups={{0,1,8,9,16,17,24,25,64,65,72,73,80,81,88,89,128,129,136,137,144,145,15..., dimensions={0} | all-to-all | bytes 1048576 | tf_op jit(solution)/shard_map/all_to_all | solution.py:328
  77.0 5.5 %collective-permute-start.8 = (bf16[2048,128]{1,0:T(8,128)(2,1)S(1)}, bf16[2048,128]{1,0:T(8,128)(2,1)S(1)}, u32[]{:S(2)}, u32[]{:S(2)}) collective-permute-start(bf16[2048,128]{1,0:T(8,128)(2,1)S(1)} %bitcast.5), channel_id=1, source_target_pairs={{0,32},{1,33},{2,34},{3,35},{4,36},{5,37},{6,38},{7,39},{8,40},{9,... | collective-permute-start | bytes 1572872 | tf_op jit(solution)/shard_map/ppermute | solution.py:332
  82.4 1.5 %collective-permute-done.8.other_ref = bf16[2048,128]{1,0:T(8,128)(2,1)S(1)} collective-permute-done((bf16[2048,128]{1,0:T(8,128)(2,1)S(1)}, bf16[2048,128]{1,0:T(8,128)(2,1)S(1)}, u32[]{:S(2)}, u32[]{:S(2)}) %collective-permute-start.8) | collective-permute-done | bytes 524320 | tf_op jit(solution)/shard_map/ppermute | solution.py:332
  84.0 2.0 %unpack.1 = (f32[27,96,96]{2,1,0:T(8,128)}, f32[27,96,96]{2,1,0:T(8,128)}) custom-call(bf16[2048,128]{1,0:T(8,128)(2,1)S(1)} %bitcast.6, bf16[2048,128]{1,0:T(8,128)(2,1)S(1)} %collective-permute-done.8.other_ref), custom_call_target="tpu_custom_call" | custom-call | bytes 1048576 | tf_op jit(solution)/shard_map/unpack/pallas_call | solution.py:298
  (3 shorter events, 0.0 us)
Async XLA Ops:
  0.6 0.9 %copy-start = (bf16[96,1024]{1,0:T(8,128)(2,1)S(1)}, bf16[96,1024]{1,0:T(8,128)(2,1)}, u32[]{:S(2)}) copy-start(bf16[96,1024]{1,0:T(8,128)(2,1)} %feat_hbm.3) | copy-start | bytes 589828
  1.6 0.9 %copy-start.2 = (bf16[96,1024]{1,0:T(8,128)(2,1)S(1)}, bf16[96,1024]{1,0:T(8,128)(2,1)}, u32[]{:S(2)}) copy-start(bf16[96,1024]{1,0:T(8,128)(2,1)} %cot_hbm.3) | copy-start | bytes 589828
  2.5 0.7 copy-start.5
  3.8 16.3 %collective-permute-start = (bf16[192,128]{1,0:T(8,128)(2,1)S(1)}, bf16[192,128]{1,0:T(8,128)(2,1)S(1)}, u32[]{:S(2)}, u32[]{:S(2)}) collective-permute-start(bf16[192,128]{1,0:T(8,128)(2,1)S(1)} %get-tuple-element.28), channel_id=1, source_target_pairs={{0,1},{1,2},{2,3},{3,4},{4,5},{5,6},{6,7},{7,8},{8,9},{9,10},{10,1... | collective-permute-start | bytes 147464 | tf_op jit(solution)/shard_map/ppermute | solution.py:342
  8.2 11.9 %collective-permute-start.1 = (bf16[192,128]{1,0:T(8,128)(2,1)S(1)}, bf16[192,128]{1,0:T(8,128)(2,1)S(1)}, u32[]{:S(2)}, u32[]{:S(2)}) collective-permute-start(bf16[192,128]{1,0:T(8,128)(2,1)S(1)} %get-tuple-element.29), channel_id=1, source_target_pairs={{1,0},{2,1},{3,2},{4,3},{5,4},{6,5},{7,6},{8,7},{9,8},{10,9},{11,1... | collective-permute-start | bytes 147464 | tf_op jit(solution)/shard_map/ppermute | solution.py:342
  9.5 0.9 %copy-start.1 = (bf16[96,1024]{1,0:T(8,128)(2,1)S(1)}, bf16[96,1024]{1,0:T(8,128)(2,1)}, u32[]{:S(2)}) copy-start(bf16[96,1024]{1,0:T(8,128)(2,1)} %feat_hbm.3) | copy-start | bytes 589828
  10.4 0.9 %copy-start.3 = (bf16[96,1024]{1,0:T(8,128)(2,1)S(1)}, bf16[96,1024]{1,0:T(8,128)(2,1)}, u32[]{:S(2)}) copy-start(bf16[96,1024]{1,0:T(8,128)(2,1)} %cot_hbm.3) | copy-start | bytes 589828
  11.3 0.7 copy-start.6
  12.0 1.1 %copy-start.7 = (bf16[27,96,96]{2,1,0:T(8,128)(2,1)S(1)}, bf16[27,96,96]{2,1,0:T(8,128)(2,1)}, u32[]{:S(2)}) copy-start(bf16[27,96,96]{2,1,0:T(8,128)(2,1)} %param.9) | copy-start | bytes 1492996
  13.1 1.1 %copy-start.8 = (bf16[27,96,96]{2,1,0:T(8,128)(2,1)S(1)}, bf16[27,96,96]{2,1,0:T(8,128)(2,1)}, u32[]{:S(2)}) copy-start(bf16[27,96,96]{2,1,0:T(8,128)(2,1)} %param.10) | copy-start | bytes 1492996
  14.2 0.7 copy-start.10
  24.1 2.6 %collective-permute-start.4 = (bf16[2048,128]{1,0:T(8,128)(2,1)S(1)}, bf16[2048,128]{1,0:T(8,128)(2,1)S(1)}, u32[]{:S(2)}, u32[]{:S(2)}) collective-permute-start(bf16[2048,128]{1,0:T(8,128)(2,1)S(1)} %get-tuple-element.34), channel_id=1, source_target_pairs={{0,32},{1,33},{2,34},{3,35},{4,36},{5,37},{6,38},{7,39},{8,40},{9,... | collective-permute-start | bytes 1572872 | tf_op jit(solution)/shard_map/ppermute | solution.py:332
  26.7 30.7 %copy-start.9 = (bf16[27,96,96]{2,1,0:T(8,128)(2,1)S(1)}, bf16[27,96,96]{2,1,0:T(8,128)(2,1)}, u32[]{:S(2)}) copy-start(bf16[27,96,96]{2,1,0:T(8,128)(2,1)} %param.10) | copy-start | bytes 1492996
  27.6 23.0 %all-to-all-start = ((bf16[32,64,128]{2,1,0:T(8,128)(2,1)}), bf16[32,64,128]{2,1,0:T(8,128)(2,1)S(1)}, u32[]{:S(2)}, u32[]{:S(2)}) async-start(bf16[32,64,128]{2,1,0:T(8,128)(2,1)} %bitcast.3), calls=%async_computation | async-start | bytes 1048576 | tf_op jit(solution)/shard_map/all_to_all | solution.py:328
  39.2 5.8 %collective-permute-start.2 = (bf16[96,128]{1,0:T(8,128)(2,1)S(1)}, bf16[96,128]{1,0:T(8,128)(2,1)S(1)}, u32[]{:S(2)}, u32[]{:S(2)}) collective-permute-start(bf16[96,128]{1,0:T(8,128)(2,1)S(1)} %get-tuple-element.31), channel_id=1, source_target_pairs={{0,1},{1,2},{2,3},{3,4},{4,5},{5,6},{6,7},{7,8},{8,9},{9,10},{10,1... | collective-permute-start | bytes 73736 | tf_op jit(solution)/shard_map/ppermute | solution.py:342
  42.3 5.2 %collective-permute-start.3 = (bf16[96,128]{1,0:T(8,128)(2,1)S(1)}, bf16[96,128]{1,0:T(8,128)(2,1)S(1)}, u32[]{:S(2)}, u32[]{:S(2)}) collective-permute-start(bf16[96,128]{1,0:T(8,128)(2,1)S(1)} %get-tuple-element.32), channel_id=1, source_target_pairs={{1,0},{2,1},{3,2},{4,3},{5,4},{6,5},{7,6},{8,7},{9,8},{10,9},{11,1... | collective-permute-start | bytes 73736 | tf_op jit(solution)/shard_map/ppermute | solution.py:342
  50.7 9.1 %collective-permute-start.7 = (bf16[64,128]{1,0:T(8,128)(2,1)S(1)}, bf16[64,128]{1,0:T(8,128)(2,1)S(1)}, u32[]{:S(2)}, u32[]{:S(2)}) collective-permute-start(bf16[64,128]{1,0:T(8,128)(2,1)S(1)} %sum_around.1.after_ref.refs_0_), channel_id=1, source_target_pairs={{0,6},{1,7},{2,0},{3,1},{4,2},{5,3},{6,4},{7,5},{8,14},{9,15},{10,... | collective-permute-start | bytes 49160 | tf_op jit(solution)/shard_map/ppermute | solution.py:336
  53.4 6.5 %collective-permute-start.6 = (bf16[64,128]{1,0:T(8,128)(2,1)S(1)}, bf16[64,128]{1,0:T(8,128)(2,1)S(1)}, u32[]{:S(2)}, u32[]{:S(2)}) collective-permute-start(bf16[64,128]{1,0:T(8,128)(2,1)S(1)} %sum_around.1.after_ref.refs_0_), channel_id=1, source_target_pairs={{0,4},{1,5},{2,6},{3,7},{4,0},{5,1},{6,2},{7,3},{8,12},{9,13},{10,... | collective-permute-start | bytes 49160 | tf_op jit(solution)/shard_map/ppermute | solution.py:336
  55.7 4.9 %collective-permute-start.5 = (bf16[64,128]{1,0:T(8,128)(2,1)S(1)}, bf16[64,128]{1,0:T(8,128)(2,1)S(1)}, u32[]{:S(2)}, u32[]{:S(2)}) collective-permute-start(bf16[64,128]{1,0:T(8,128)(2,1)S(1)} %sum_around.1.after_ref.refs_0_), channel_id=1, source_target_pairs={{0,2},{1,3},{2,4},{3,5},{4,6},{5,7},{6,0},{7,1},{8,10},{9,11},{10,... | collective-permute-start | bytes 49160 | tf_op jit(solution)/shard_map/ppermute | solution.py:336
  60.5 0.9 %copy-start.4 = (bf16[96,1024]{1,0:T(8,128)(2,1)S(1)}, bf16[96,1024]{1,0:T(8,128)(2,1)}, u32[]{:S(2)}) copy-start(bf16[96,1024]{1,0:T(8,128)(2,1)} %features.1.refs_4_) | copy-start | bytes 589828
  77.0 7.0 %collective-permute-start.8 = (bf16[2048,128]{1,0:T(8,128)(2,1)S(1)}, bf16[2048,128]{1,0:T(8,128)(2,1)S(1)}, u32[]{:S(2)}, u32[]{:S(2)}) collective-permute-start(bf16[2048,128]{1,0:T(8,128)(2,1)S(1)} %bitcast.5), channel_id=1, source_target_pairs={{0,32},{1,33},{2,34},{3,35},{4,36},{5,37},{6,38},{7,39},{8,40},{9,... | collective-permute-start | bytes 1572872 | tf_op jit(solution)/shard_map/ppermute | solution.py:332

commit v3 on v2

--- a/solution.py
+++ b/solution.py
@@ -1,3 +1,5 @@
+import functools
+
 import jax
 import jax.numpy as jnp
 from jax import lax
@@ -100,17 +102,20 @@
 
 
 def prep_kernel(
-    feat_hbm, cot_hbm, occ_hbm, w1_hbm, w2_hbm, nb_ref,
-    a_ref, g_ref, zp_ref, gp_ref, w1t_ref, wb_ref, sel_ref, mask_ref,
-    feat_ref, cot_ref, occ_ref, w1_ref, w2_ref, planes_ref, sems,
+    feat_hbm, cot_hbm, occ_hbm, w1_hbm, w2_hbm, nb_hbm,
+    v_ref, part_ref, w1t_ref, wb_ref, sel_ref, mask_ref,
+    feat_ref, cot_ref, occ_ref, w1_ref, w2_ref, nb_ref, planes_ref, sems,
 ):
     copies = fetch(
-        (occ_hbm, feat_hbm, cot_hbm, w1_hbm, w2_hbm), (occ_ref, feat_ref, cot_ref, w1_ref, w2_ref), sems
-    )
+        (nb_hbm, occ_hbm, feat_hbm, cot_hbm, w1_hbm, w2_hbm),
+        (nb_ref, occ_ref, feat_ref, cot_ref, w1_ref, w2_ref),
+        sems,
+    )
+    copies[0].wait()
     for index, face in enumerate((-1, 0, 1)):
         for j, piece in enumerate(selection(nb_ref, face)):
             sel_ref[index, :, j * 128 : (j + 1) * 128] = piece
-    for copy in copies[:3]:
+    for copy in copies[1:4]:
         copy.wait()
     for x in range(0, 8, 2):
         masks = to_planes(occ_ref, x)
@@ -121,22 +126,33 @@
             for k in range(2):
                 planes_ref[x + k, row : row + CH, :] = jnp.where(masks[k] > 0, both[k], 0.0).astype(BF16)
     stacked = planes_ref[...].reshape(8 * 2 * CH, 128)
-    for j in range(9):
-        spread = dot(stacked, sel_ref[1, :, j * 128 : (j + 1) * 128]).astype(BF16)
+
+    def place(j, spread):
         for x in range(8):
-            a_ref[j * CH : (j + 1) * CH, x * 128 : (x + 1) * 128] = spread[x * 2 * CH : x * 2 * CH + CH]
-            g_ref[j * CH : (j + 1) * CH, x * 128 : (x + 1) * 128] = spread[x * 2 * CH + CH : (x + 1) * 2 * CH]
-    for copy in copies[3:]:
+            for k in range(2):
+                r = (x * 2 + k) * CH
+                v_ref[k, j * CH : (j + 1) * CH, x * 128 : (x + 1) * 128] = spread[r : r + CH]
+
+    spread_planes(stacked, sel_ref, place)
+    for copy in copies[4:]:
         copy.wait()
     for d in range(3):
         w1t_ref[d] = turned(w1_ref, d)
         wb_ref[d] = jnp.concatenate(
             [w2_ref[(26 - d * 9 - j) * CH : (27 - d * 9 - j) * CH, :] for j in range(9)], axis=1
         )
-    for w_ref, v_ref, out_ref in ((w1t_ref, a_ref, zp_ref), (wb_ref, g_ref, gp_ref)):
-        out_ref[...] = dot(w_ref[1], v_ref[...])
-        out_ref[:, 128:] += dot(w_ref[0], v_ref[:, :896])
-        out_ref[:, :896] += dot(w_ref[2], v_ref[:, 128:])
+    for k, w_ref in ((0, w1t_ref), (1, wb_ref)):
+        part_ref[k] = dot(w_ref[1], v_ref[k])
+        part_ref[k, :, 128:] += dot(w_ref[0], v_ref[k, :, :896])
+        part_ref[k, :, :896] += dot(w_ref[2], v_ref[k, :, 128:])
+
+
+def spread_planes(stacked, sel_ref, place):
+    for j in range(0, 9, 2):
+        wide = min(256, 1152 - j * 128)
+        spread = dot(stacked, sel_ref[1, :, j * 128 : j * 128 + wide]).astype(BF16)
+        for k in range(wide // 128):
+            place(j + k, spread[:, k * 128 : (k + 1) * 128])
 
 
 def spread_rim(rim, sel_ref, index, rows):
@@ -149,68 +165,70 @@
     return parts
 
 
-def main_kernel(
-    a_ref, g_ref, zp_ref, gp_ref, w1t_ref, wb_ref, sel_ref, mask_ref, low_ref, high_ref,
-    own_ref, send_ref, a1_ref, a1_low_ref, a1_high_ref,
-    grad_ref, packed_ref,
+def point_kernel(
+    part_ref, w1t_ref, wb_ref, sel_ref, mask_ref, low_ref, high_ref,
+    grad_ref, rim_ref, a1_low_ref, a1_high_ref,
 ):
-    scale = 262144.0 ** -0.5
-    a_low, g_low = spread_rim(low_ref[...], sel_ref, 0, 2 * CH)
-    a_high, g_high = spread_rim(high_ref[...], sel_ref, 2, 2 * CH)
-
-    def finish(partial_ref, w_ref, low, high):
-        first = partial_ref[:, :128] + dot(w_ref[0], low)
-        last = partial_ref[:, 896:] + dot(w_ref[2], high)
-        return mask_ref[...] * jnp.concatenate([first, partial_ref[:, 128:896], last], axis=1)
-
-    z = finish(zp_ref, w1t_ref, a_low, a_high)
-    ga = finish(gp_ref, wb_ref, g_low, g_high)
+    lows = spread_rim(low_ref[...], sel_ref, 0, 2 * CH)
+    highs = spread_rim(high_ref[...], sel_ref, 2, 2 * CH)
+    for k in range(2):
+        rim_ref[k, 0] = lows[k]
+        rim_ref[k, 1] = highs[k]
+
+    def finish(k, w_ref):
+        first = part_ref[k, :, :128] + dot(w_ref[0], lows[k])
+        last = part_ref[k, :, 896:] + dot(w_ref[2], highs[k])
+        return mask_ref[...] * jnp.concatenate([first, part_ref[k, :, 128:896], last], axis=1)
+
+    z = finish(0, w1t_ref)
     sigma = 1.0 / (1.0 + jnp.exp(-z))
     a1 = (z * sigma).astype(BF16)
-    gz = (ga * sigma * (1.0 + z * (1.0 - sigma))).astype(BF16)
-    a1_ref[...] = a1
+    grad_ref[1] = a1
     a1_low_ref[...] = a1[:, :128]
     a1_high_ref[...] = a1[:, 896:]
-
-    def terms(v_ref, low, high, grad, start):
-        zero = jnp.zeros((K9, 32), F32)
-
-        def put(d, value):
-            r = start + d * K9
-            grad_ref[r : r + K9, :] = jnp.concatenate([value * scale, zero], axis=1)
-
-        put(0, dot(v_ref[:, :896], grad[:, 128:], NT) + dot(low, grad[:, :128], NT))
-        put(1, dot(v_ref[...], grad, NT))
-        put(2, dot(v_ref[:, 128:], grad[:, :896], NT) + dot(high, grad[:, 896:], NT))
-
-    terms(g_ref, g_low, g_high, a1, 27 * CH)
-    terms(a_ref, a_low, a_high, gz, 0)
+    ga = finish(1, wb_ref)
+    grad_ref[0] = (ga * sigma * (1.0 + z * (1.0 - sigma))).astype(BF16)
+
+
+def term_kernel(kept, v_ref, rim_ref, grad_ref, out_ref, terms_ref):
+    which = core_index() if kept else 1 - core_index()
+    grad = grad_ref[which]
+    inner = v_ref[which]
+    scale = 262144.0 ** -0.5
+    zero = jnp.zeros((K9, 32), F32)
+    views = (
+        jnp.concatenate([rim_ref[which, 0], inner[:, :896]], axis=1),
+        inner,
+        jnp.concatenate([inner[:, 128:], rim_ref[which, 1]], axis=1),
+    )
+    for d, view in enumerate(views):
+        value = dot(view, grad, NT) * scale
+        terms_ref[d * K9 : (d + 1) * K9, :] = jnp.concatenate([value, zero], axis=1)
     lane = lax.broadcasted_iota(jnp.int32, (PACKED, 128), 1)
-    for grad in range(2):
-        rows = grad * 27 * CH
-        base = grad * HALF
-        spare = grad_ref[rows + 3 * PACKED : rows + 4 * PACKED, :]
-        for k in range(3):
-            kept = grad_ref[rows + k * PACKED : rows + (k + 1) * PACKED, :]
-            packed_ref[base + k * PACKED : base + (k + 1) * PACKED, :] = jnp.where(
-                lane < 96, kept, pltpu.roll(spare, 96 - 32 * k, 1)
-            )
-        packed_ref[base + 3 * PACKED : base + HALF, :] = jnp.zeros((HALF - 3 * PACKED, 128), F32)
-    core = core_index()
-    own_ref[...] = packed_ref[pl.ds(pl.multiple_of(core * HALF, HALF), HALF), :]
-    send_ref[...] = packed_ref[pl.ds(pl.multiple_of((1 - core) * HALF, HALF), HALF), :].astype(BF16)
-
-
-def out_kernel(a1_ref, low_ref, high_ref, sel_ref, w2_ref, mask_ref, after_ref, out_ref, v_ref, planes_ref):
+    spare = terms_ref[3 * PACKED : 4 * PACKED, :]
+    for k in range(3):
+        value = jnp.where(
+            lane < 96, terms_ref[k * PACKED : (k + 1) * PACKED, :], pltpu.roll(spare, 96 - 32 * k, 1)
+        )
+        out_ref[k * PACKED : (k + 1) * PACKED, :] = value.astype(out_ref.dtype)
+    out_ref[3 * PACKED : HALF, :] = jnp.zeros((HALF - 3 * PACKED, 128), out_ref.dtype)
+
+
+def out_kernel(
+    grad_ref, low_ref, high_ref, sel_ref, w2_hbm, mask_ref, after_ref, out_ref, w2_ref, v_ref, planes_ref, sems
+):
+    (copy,) = fetch((w2_hbm,), (w2_ref,), sems)
     for x in range(8):
-        planes_ref[x] = a1_ref[:, x * 128 : (x + 1) * 128]
-    stacked = planes_ref[...].reshape(8 * CH, 128)
-    for j in range(9):
-        spread = dot(stacked, sel_ref[1, :, j * 128 : (j + 1) * 128]).astype(BF16)
+        planes_ref[x] = grad_ref[1, :, x * 128 : (x + 1) * 128]
+
+    def place(j, spread):
         for x in range(8):
             v_ref[j * CH : (j + 1) * CH, (x + 1) * 128 : (x + 2) * 128] = spread[x * CH : (x + 1) * CH]
+
+    spread_planes(planes_ref[...].reshape(8 * CH, 128), sel_ref, place)
     v_ref[:, :128] = spread_rim(low_ref[...], sel_ref, 0, CH)[0]
     v_ref[:, 1152:] = spread_rim(high_ref[...], sel_ref, 2, CH)[0]
+    copy.wait()
     total = dot(turned(w2_ref, 0), v_ref[:, :1024])
     total += dot(turned(w2_ref, 1), v_ref[:, 128:1152])
     total += dot(turned(w2_ref, 2), v_ref[:, 256:])
@@ -227,11 +245,11 @@
     return lax.rem(lax.axis_index("group"), 2)
 
 
-def add_kernel(own_ref, got_ref, out_ref):
+def add_kernel(own_ref, got_ref, low_ref, high_ref, out_ref):
     out_ref[...] = (own_ref[...] + got_ref[...].astype(F32)).astype(BF16)
 
 
-def rows_kernel(got_ref, low_ref, high_ref, out_ref):
+def rows_kernel(got_ref, after_ref, out_ref):
     total = got_ref[0].astype(F32)
     for k in range(1, AROUND):
         total += got_ref[k].astype(F32)
@@ -342,10 +360,17 @@
     return lax.ppermute(value, "dev", pairs)
 
 
+def in_hbm(value):
+    return pltpu.with_memory_space_constraint(value, pltpu.HBM)
+
+
 def per_device(features_in, occupancy, cotangent, kernel_one, kernel_two, neighbours):
-    occ = occupancy.reshape(1, 1024)
-    w1 = kernel_one.reshape(27 * CH, CH)
-    w2 = kernel_two.reshape(27 * CH, CH)
+    features_in = in_hbm(features_in)
+    cotangent = in_hbm(cotangent)
+    occ = in_hbm(occupancy.reshape(1, 1024))
+    w1 = in_hbm(kernel_one.reshape(27 * CH, CH))
+    w2 = in_hbm(kernel_two.reshape(27 * CH, CH))
+    neighbours = in_hbm(neighbours)
     low, high = call(
         rim_kernel,
         [shape((2 * CH, 128))] * 2,
@@ -356,57 +381,70 @@
     )
     upper = dev_shift(low, -1)
     lower = dev_shift(high, 1)
-    a, g, zp, gp, w1t, wb, sel, mask = call(
+    v, part, w1t, wb, sel, mask = call(
         prep_kernel,
         [
-            shape((K9, 1024)), shape((K9, 1024)), shape((CH, 1024), F32), shape((CH, 1024), F32),
+            shape((2, K9, 1024)), shape((2, CH, 1024), F32),
             shape((3, CH, K9)), shape((3, CH, K9)), shape((3, 128, 1152)), shape((1, 1024), F32),
         ],
         features_in, cotangent, occ, w1, w2, neighbours,
-        specs={0: HBM, 1: HBM, 2: HBM, 3: HBM, 4: HBM, 5: SMEM},
+        specs={k: HBM for k in range(6)},
         scratch=INPUTS + [
-            pltpu.VMEM((27 * CH, CH), BF16), pltpu.VMEM((27 * CH, CH), BF16),
-            pltpu.VMEM((8, 2 * CH, 128), BF16), pltpu.SemaphoreType.DMA((5,)),
+            pltpu.VMEM((27 * CH, CH), BF16), pltpu.VMEM((27 * CH, CH), BF16), pltpu.SMEM((2, 27), jnp.int32),
+            pltpu.VMEM((8, 2 * CH, 128), BF16), pltpu.SemaphoreType.DMA((6,)),
         ],
         limit=16,
         flops=4 << 30,
         name="prep",
     )
-    own, send, a1, a1_low, a1_high = call(
-        main_kernel,
-        [
-            shape((HALF, 128), F32), shape((HALF, 128)), shape((CH, 1024)),
-            shape((CH, 128)), shape((CH, 128)),
-        ],
-        a, g, zp, gp, w1t, wb, sel, mask, lower, upper,
-        scratch=[pltpu.VMEM((54 * CH, 128), F32), pltpu.VMEM((ROWS, 128), F32)],
+    grad, rim, a1_low, a1_high = call(
+        point_kernel,
+        [shape((2, CH, 1024)), shape((2, 2, K9, 128)), shape((CH, 128)), shape((CH, 128))],
+        part, w1t, wb, sel, mask, lower, upper,
         limit=16,
-        flops=4 << 30,
-        name="gradients",
-    )
-    got = swap_core(send)
+        flops=1 << 30,
+        name="points",
+    )
     a1_upper = dev_shift(a1_low, -1)
     a1_lower = dev_shift(a1_high, 1)
-    value = call(add_kernel, shape((HALF, 128)), own, got, name="sum_core")
-    value = all_to_all(value.reshape(AROUND, HALF // AROUND, 128))
+
+    def terms(kept):
+        return call(
+            functools.partial(term_kernel, kept),
+            shape((HALF, 128), F32 if kept else BF16),
+            v, rim, grad,
+            scratch=[pltpu.VMEM((27 * CH, 128), F32)],
+            limit=16,
+            flops=2 << 30,
+            name="terms_kept" if kept else "terms_sent",
+        )
+
+    got = swap_core(terms(False))
     value = call(
-        rows_kernel, shape((HALF // AROUND, 128)), value, a1_lower, a1_upper,
-        specs={1: ANY, 2: ANY}, name="sum_around",
-    )
-    arrived = [value] + [swap_z(value, k) for k in range(1, 4)]
+        add_kernel, shape((HALF, 128)), terms(True), got, a1_lower, a1_upper,
+        specs={2: ANY, 3: ANY}, name="sum_core",
+    )
+    moved = all_to_all(value.reshape(AROUND, HALF // AROUND, 128))
     features_out = call(
         out_kernel,
         shape((CH, 1024)),
-        a1, a1_lower, a1_upper, sel, w2, mask, value,
-        specs={6: ANY},
-        scratch=[pltpu.VMEM((K9, 1280), BF16), pltpu.VMEM((8, CH, 128), BF16)],
+        grad, a1_lower, a1_upper, sel, w2, mask, in_hbm(value),
+        specs={4: HBM, 6: HBM},
+        scratch=[
+            pltpu.VMEM((27 * CH, CH), BF16), pltpu.VMEM((K9, 1280), BF16), pltpu.VMEM((8, CH, 128), BF16),
+            pltpu.SemaphoreType.DMA((1,)),
+        ],
         limit=16,
-        flops=4 << 30,
+        flops=3 << 30,
         name="features",
     )
     value = call(
-        total_kernel, shape((AROUND, HALF // AROUND, 128)), *arrived, features_out,
-        specs={4: ANY},
+        rows_kernel, shape((HALF // AROUND, 128)), moved, in_hbm(features_out),
+        specs={1: HBM}, name="sum_around",
+    )
+    arrived = [value] + [swap_z(value, k) for k in range(1, 4)]
+    value = call(
+        total_kernel, shape((AROUND, HALF // AROUND, 128)), *arrived,
         scratch=[pltpu.VMEM((4, HALF // AROUND, 128), BF16)],
         name="sum_z",
     )

time: 86.8 us -> 81.4 us (0.938)
  local copies, waits for them, and re-layouts: 8.86 us -> 0 us
  waiting for transfers between devices: 10.8 us -> 16.3 us
  blocking collectives: 15.5 us -> 12.8 us
  Pallas kernels: 15.2 us -> 16.1 us
    unnamed x22 -> x0, local copies, waits for them, and re-layouts: 8.86 us -> none
    all_to_all x1, waiting for transfers between devices: 3.05 us -> 7.65 us  [all_to_all(): lax.all_to_all(value, BOTH, 0, 0, axis_index_groups=around_groups(), tile...]
    ppermute x3, waiting for transfers between devices: 0.79 us -> 4.69 us  [swap_z(): lax.ppermute(value, BOTH, device_pairs(lambda x, y, z, core: (x, y, (z +...]
    all_to_all x1, blocking collectives: 15.5 us -> 12.8 us  [all_to_all(): lax.all_to_all(value, BOTH, 0, 0, axis_index_groups=around_groups(), tile...]
    ppermute x2, waiting for transfers between devices: 3.07 us -> 1.54 us  [swap_core(): lax.ppermute(value, BOTH, device_pairs(lambda x, y, z, core: (x, y, z, 1...]
    ppermute x4, waiting for transfers between devices: 3.9 us -> 2.42 us  [dev_shift(): return lax.ppermute(value, 'dev', pairs)]
    pallas_call x8 -> x10, Pallas kernels: 15.2 us -> 16.1 us  [call(): pl.pallas_call(kernel, out_shape=outs, in_specs=[specs.get(k, VMEM) for k...]
    ppermute x3, starting transfers between devices: 6.72 us -> 5.8 us  [swap_z(): lax.ppermute(value, BOTH, device_pairs(lambda x, y, z, core: (x, y, (z +...]
  transfers between devices with their start and end apart: 10 -> 10, of which waited for: 7 -> 5; matrix products, arithmetic and copies ran while one was open for 0% -> 0% of each run, Pallas kernels for 9% -> 12%
where the time goes in v3:
time: 81.4 us; the launch traced here: 81 us
  starting transfers between devices  35.1 us (43%)
  waiting for transfers between devices  16.3 us (20%)
  Pallas kernels  16.1 us (20%)
  blocking collectives  12.8 us (16%)
    pallas_call x10, Pallas kernels, call(): pl.pallas_call(kernel, out_shape=outs, in_specs=[specs.get(k, VMEM) for k...  16.1 us
    all_to_all x1, blocking collectives, all_to_all(): lax.all_to_all(value, BOTH, 0, 0, axis_index_groups=around_groups(), tile...  12.8 us
    all_to_all x1, starting transfers between devices, all_to_all(): lax.all_to_all(value, BOTH, 0, 0, axis_index_groups=around_groups(), tile...  11.1 us
    ppermute x4, starting transfers between devices, dev_shift(): return lax.ppermute(value, 'dev', pairs)  11 us
    all_to_all x1, waiting for transfers between devices, all_to_all(): lax.all_to_all(value, BOTH, 0, 0, axis_index_groups=around_groups(), tile...  7.65 us
    ppermute x2, starting transfers between devices, swap_core(): lax.ppermute(value, BOTH, device_pairs(lambda x, y, z, core: (x, y, z, 1...  7.29 us
    ppermute x3, starting transfers between devices, swap_z(): lax.ppermute(value, BOTH, device_pairs(lambda x, y, z, core: (x, y, (z +...  5.8 us
    ppermute x3, waiting for transfers between devices, swap_z(): lax.ppermute(value, BOTH, device_pairs(lambda x, y, z, core: (x, y, (z +...  4.69 us
  transfers between devices with their start and end apart: 10, of which 5 were waited for; matrix products, arithmetic and copies ran while one was open for 0% of the time, Pallas kernels for 12%

profile of v3, /device:TPU:1, one launch (start us, length us, event | category | flops | bytes accessed | tf_op | source)
XLA Modules:
  0.0 81.0 jit_solution(1120326857402027606)
XLA Ops:
  0.6 1.2 %rims.1 = (bf16[192,128]{1,0:T(8,128)(2,1)S(1)}, bf16[192,128]{1,0:T(8,128)(2,1)S(1)}) custom-call(bf16[96,1024]{1,0:T(8,128)(2,1)} %feat_hbm.3, bf16[96,1024]{1,0:T(8,128)(2,1)} %cot_hbm.3, s32[1,1024]{1,0:T(1,128)} %bitcast.7), custom_call_target="tpu_custom_call" | custom-call | bytes 1048576 | tf_op jit(solution)/shard_map/rims/pallas_call | solution.py:316
  1.8 4.4 %collective-permute-start = (bf16[192,128]{1,0:T(8,128)(2,1)S(1)}, bf16[192,128]{1,0:T(8,128)(2,1)S(1)}, u32[]{:S(2)}, u32[]{:S(2)}) collective-permute-start(bf16[192,128]{1,0:T(8,128)(2,1)S(1)} %get-tuple-element.22), channel_id=1, source_target_pairs={{0,1},{1,2},{2,3},{3,4},{4,5},{5,6},{6,7},{7,8},{8,9},{9,10},{10,1... | collective-permute-start | bytes 147464 | tf_op jit(solution)/shard_map/ppermute | solution.py:360
  6.2 1.3 %collective-permute-start.1 = (bf16[192,128]{1,0:T(8,128)(2,1)S(1)}, bf16[192,128]{1,0:T(8,128)(2,1)S(1)}, u32[]{:S(2)}, u32[]{:S(2)}) collective-permute-start(bf16[192,128]{1,0:T(8,128)(2,1)S(1)} %get-tuple-element.23), channel_id=1, source_target_pairs={{1,0},{2,1},{3,2},{4,3},{5,4},{6,5},{7,6},{8,7},{9,8},{10,9},{11,1... | collective-permute-start | bytes 147464 | tf_op jit(solution)/shard_map/ppermute | solution.py:360
  7.5 4.4 %prep.1 = (bf16[2,864,1024]{2,1,0:T(8,128)(2,1)S(1)}, f32[2,96,1024]{2,1,0:T(8,128)S(1)}, bf16[3,96,864]{2,1,0:T(8,128)(2,1)S(1)}, bf16[3,96,864]{2,1,0:T(8,128)...) custom-call(bf16[96,1024]{1,0:T(8,128)(2,1)} %feat_hbm.3, bf16[96,1024]{1,0:T(8,128)(2,1)} %cot_hbm.3, ...), custom_call_target="tpu_custom_call" | custom-call | flops 4294967296 | bytes 1048576 | tf_op jit(solution)/shard_map/prep/pallas_call | solution.py:316
  11.9 0.0 collective-permute-done.low_ref
  11.9 0.0 collective-permute-done.1.high_ref
  11.9 0.7 points.1
  12.6 1.6 %terms_sent.1 = bf16[2048,128]{1,0:T(8,128)(2,1)S(1)} custom-call(bf16[2,864,1024]{2,1,0:T(8,128)(2,1)S(1)} %get-tuple-element.27.v_ref, bf16[2,2,864,128]{3,2,1,0:T(8,128)(2,1)S(1)} %get-tuple-element.28.rim_ref, bf16[2,96,1024]{2,1,0:T(8,128)(2,1)S(1)} %get-tuple-element.24.grad_ref), custom_call_target="tpu_custom_call" | custom-call | flops 2147483648 | bytes 1048576 | tf_op jit(solution)/shard_map/terms_sent/pallas_call | solution.py:316
  14.2 1.3 %collective-permute-start.4 = (bf16[2048,128]{1,0:T(8,128)(2,1)S(1)}, bf16[2048,128]{1,0:T(8,128)(2,1)S(1)}, u32[]{:S(2)}, u32[]{:S(2)}) collective-permute-start(bf16[2048,128]{1,0:T(8,128)(2,1)S(1)} %terms_sent.1), channel_id=1, source_target_pairs={{0,32},{1,33},{2,34},{3,35},{4,36},{5,37},{6,38},{7,39},{8,40},{9,... | collective-permute-start | bytes 1572872 | tf_op jit(solution)/shard_map/ppermute | solution.py:350
  15.5 4.0 %collective-permute-start.2 = (bf16[96,128]{1,0:T(8,128)(2,1)S(1)}, bf16[96,128]{1,0:T(8,128)(2,1)S(1)}, u32[]{:S(2)}, u32[]{:S(2)}) collective-permute-start(bf16[96,128]{1,0:T(8,128)(2,1)S(1)} %get-tuple-element.25), channel_id=1, source_target_pairs={{0,1},{1,2},{2,3},{3,4},{4,5},{5,6},{6,7},{7,8},{8,9},{9,10},{10,1... | collective-permute-start | bytes 73736 | tf_op jit(solution)/shard_map/ppermute | solution.py:360
  19.5 1.3 %collective-permute-start.3 = (bf16[96,128]{1,0:T(8,128)(2,1)S(1)}, bf16[96,128]{1,0:T(8,128)(2,1)S(1)}, u32[]{:S(2)}, u32[]{:S(2)}) collective-permute-start(bf16[96,128]{1,0:T(8,128)(2,1)S(1)} %get-tuple-element.26), channel_id=1, source_target_pairs={{1,0},{2,1},{3,2},{4,3},{5,4},{6,5},{7,6},{8,7},{9,8},{10,9},{11,1... | collective-permute-start | bytes 73736 | tf_op jit(solution)/shard_map/ppermute | solution.py:360
  20.8 1.7 %terms_kept.1.own_ref = f32[2048,128]{1,0:T(8,128)S(1)} custom-call(bf16[2,864,1024]{2,1,0:T(8,128)(2,1)S(1)} %get-tuple-element.27.v_ref, bf16[2,2,864,128]{3,2,1,0:T(8,128)(2,1)S(1)} %get-tuple-element.28.rim_ref, bf16[2,96,1024]{2,1,0:T(8,128)(2,1)S(1)} %get-tuple-element.24.grad_ref), custom_call_target="tpu_custom_call" | custom-call | flops 2147483648 | bytes 1048576 | tf_op jit(solution)/shard_map/terms_kept/pallas_call | solution.py:316
  22.5 0.0 collective-permute-done.2.low_ref
  22.5 2.4 %collective-permute-done.3.high_ref = bf16[96,128]{1,0:T(8,128)(2,1)S(1)} collective-permute-done((bf16[96,128]{1,0:T(8,128)(2,1)S(1)}, bf16[96,128]{1,0:T(8,128)(2,1)S(1)}, u32[]{:S(2)}, u32[]{:S(2)}) %collective-permute-start.3) | collective-permute-done | bytes 24608 | tf_op jit(solution)/shard_map/ppermute | solution.py:360
  24.9 0.0 collective-permute-done.4.got_ref
  25.0 0.9 %sum_core.1.after_ref = bf16[2048,128]{1,0:T(8,128)(2,1)} custom-call(f32[2048,128]{1,0:T(8,128)S(1)} %terms_kept.1.own_ref, bf16[2048,128]{1,0:T(8,128)(2,1)S(1)} %collective-permute-done.4.got_ref, bf16[96,128]{1,0:T(8,128)(2,1)S(1)} %collective-permute-done.2.low_ref, bf16[96,128]{1,0:T(8,128)(2,1)S(1)} %collective-permute-done.3.high_ref), custom_call_target="tpu_custom_call" | custom-call | bytes 1048576 | tf_op jit(solution)/shard_map/sum_core/pallas_call | solution.py:316
  25.8 11.1 %all-to-all-start = ((bf16[32,64,128]{2,1,0:T(8,128)(2,1)}), bf16[32,64,128]{2,1,0:T(8,128)(2,1)S(1)}, u32[]{:S(2)}, u32[]{:S(2)}) async-start(bf16[32,64,128]{2,1,0:T(8,128)(2,1)} %bitcast.3), calls=%async_computation | async-start | bytes 1048576 | tf_op jit(solution)/shard_map/all_to_all | solution.py:346
  36.9 3.5 %features.1.after_ref = bf16[96,1024]{1,0:T(8,128)(2,1)} custom-call(bf16[2,96,1024]{2,1,0:T(8,128)(2,1)S(1)} %get-tuple-element.24.grad_ref, bf16[96,128]{1,0:T(8,128)(2,1)S(1)} %collective-permute-done.2.low_ref, bf16[96,128]{1,0:T(8,128)(2,1)S(1)} %collective-permute-done.3.high_ref, bf16[3,128,1152]{2,1,0:T(8,128)(2,1)S(1)} %get-tuple-element.20.sel_ref, ...), custom_call_target="tpu_custom_call" | custom-call | flops 3221225472 | bytes 1048576 | tf_op jit(solution)/shard_map/features/pallas_call | solution.py:316
  40.4 7.6 %all-to-all-done.got_ref = bf16[32,64,128]{2,1,0:T(8,128)(2,1)S(1)} async-done(((bf16[32,64,128]{2,1,0:T(8,128)(2,1)}), bf16[32,64,128]{2,1,0:T(8,128)(2,1)S(1)}, u32[]{:S(2)}, u32[]{:S(2)}) %all-to-all-start) | async-done | bytes 524320 | tf_op jit(solution)/shard_map/all_to_all | solution.py:346
  48.1 0.1 sum_around.1.refs_0_
  48.2 3.3 %collective-permute-start.7 = (bf16[64,128]{1,0:T(8,128)(2,1)S(1)}, bf16[64,128]{1,0:T(8,128)(2,1)S(1)}, u32[]{:S(2)}, u32[]{:S(2)}) collective-permute-start(bf16[64,128]{1,0:T(8,128)(2,1)S(1)} %sum_around.1.refs_0_), channel_id=1, source_target_pairs={{0,6},{1,7},{2,0},{3,1},{4,2},{5,3},{6,4},{7,5},{8,14},{9,15},{10,... | collective-permute-start | bytes 49160 | tf_op jit(solution)/shard_map/ppermute | solution.py:354
  51.5 2.5 %collective-permute-start.6 = (bf16[64,128]{1,0:T(8,128)(2,1)S(1)}, bf16[64,128]{1,0:T(8,128)(2,1)S(1)}, u32[]{:S(2)}, u32[]{:S(2)}) collective-permute-start(bf16[64,128]{1,0:T(8,128)(2,1)S(1)} %sum_around.1.refs_0_), channel_id=1, source_target_pairs={{0,4},{1,5},{2,6},{3,7},{4,0},{5,1},{6,2},{7,3},{8,12},{9,13},{10,... | collective-permute-start | bytes 49160 | tf_op jit(solution)/shard_map/ppermute | solution.py:354
  54.0 0.0 collective-permute-start.5
  54.0 0.0 collective-permute-done.7.refs_3_
  54.0 4.0 %collective-permute-done.6.refs_2_ = bf16[64,128]{1,0:T(8,128)(2,1)S(1)} collective-permute-done((bf16[64,128]{1,0:T(8,128)(2,1)S(1)}, bf16[64,128]{1,0:T(8,128)(2,1)S(1)}, u32[]{:S(2)}, u32[]{:S(2)}) %collective-permute-start.6) | collective-permute-done | bytes 16416 | tf_op jit(solution)/shard_map/ppermute | solution.py:354
  58.0 0.7 collective-permute-done.5.refs_1_
  58.7 0.1 sum_z.1
  58.7 12.8 %all_to_all.10 = bf16[32,64,128]{2,1,0:T(8,128)(2,1)S(1)} all-to-all(bf16[32,64,128]{2,1,0:T(8,128)(2,1)S(1)} %sum_z.1), channel_id=1, replica_groups={{0,1,8,9,16,17,24,25,64,65,72,73,80,81,88,89,128,129,136,137,144,145,15..., dimensions={0} | all-to-all | bytes 1048576 | tf_op jit(solution)/shard_map/all_to_all | solution.py:346
  71.5 6.0 %collective-permute-start.8 = (bf16[2048,128]{1,0:T(8,128)(2,1)S(1)}, bf16[2048,128]{1,0:T(8,128)(2,1)S(1)}, u32[]{:S(2)}, u32[]{:S(2)}) collective-permute-start(bf16[2048,128]{1,0:T(8,128)(2,1)S(1)} %bitcast.5), channel_id=1, source_target_pairs={{0,32},{1,33},{2,34},{3,35},{4,36},{5,37},{6,38},{7,39},{8,40},{9,... | collective-permute-start | bytes 1572872 | tf_op jit(solution)/shard_map/ppermute | solution.py:350
  77.5 1.5 %collective-permute-done.8.other_ref = bf16[2048,128]{1,0:T(8,128)(2,1)S(1)} collective-permute-done((bf16[2048,128]{1,0:T(8,128)(2,1)S(1)}, bf16[2048,128]{1,0:T(8,128)(2,1)S(1)}, u32[]{:S(2)}, u32[]{:S(2)}) %collective-permute-start.8) | collective-permute-done | bytes 524320 | tf_op jit(solution)/shard_map/ppermute | solution.py:350
  79.0 2.0 %unpack.1 = (f32[27,96,96]{2,1,0:T(8,128)}, f32[27,96,96]{2,1,0:T(8,128)}) custom-call(bf16[2048,128]{1,0:T(8,128)(2,1)S(1)} %bitcast.6, bf16[2048,128]{1,0:T(8,128)(2,1)S(1)} %collective-permute-done.8.other_ref), custom_call_target="tpu_custom_call" | custom-call | bytes 1048576 | tf_op jit(solution)/shard_map/unpack/pallas_call | solution.py:316
Async XLA Ops:
  1.8 10.1 %collective-permute-start = (bf16[192,128]{1,0:T(8,128)(2,1)S(1)}, bf16[192,128]{1,0:T(8,128)(2,1)S(1)}, u32[]{:S(2)}, u32[]{:S(2)}) collective-permute-start(bf16[192,128]{1,0:T(8,128)(2,1)S(1)} %get-tuple-element.22), channel_id=1, source_target_pairs={{0,1},{1,2},{2,3},{3,4},{4,5},{5,6},{6,7},{7,8},{8,9},{9,10},{10,1... | collective-permute-start | bytes 147464 | tf_op jit(solution)/shard_map/ppermute | solution.py:360
  6.2 5.7 %collective-permute-start.1 = (bf16[192,128]{1,0:T(8,128)(2,1)S(1)}, bf16[192,128]{1,0:T(8,128)(2,1)S(1)}, u32[]{:S(2)}, u32[]{:S(2)}) collective-permute-start(bf16[192,128]{1,0:T(8,128)(2,1)S(1)} %get-tuple-element.23), channel_id=1, source_target_pairs={{1,0},{2,1},{3,2},{4,3},{5,4},{6,5},{7,6},{8,7},{9,8},{10,9},{11,1... | collective-permute-start | bytes 147464 | tf_op jit(solution)/shard_map/ppermute | solution.py:360
  14.2 10.7 %collective-permute-start.4 = (bf16[2048,128]{1,0:T(8,128)(2,1)S(1)}, bf16[2048,128]{1,0:T(8,128)(2,1)S(1)}, u32[]{:S(2)}, u32[]{:S(2)}) collective-permute-start(bf16[2048,128]{1,0:T(8,128)(2,1)S(1)} %terms_sent.1), channel_id=1, source_target_pairs={{0,32},{1,33},{2,34},{3,35},{4,36},{5,37},{6,38},{7,39},{8,40},{9,... | collective-permute-start | bytes 1572872 | tf_op jit(solution)/shard_map/ppermute | solution.py:350
  15.5 7.0 %collective-permute-start.2 = (bf16[96,128]{1,0:T(8,128)(2,1)S(1)}, bf16[96,128]{1,0:T(8,128)(2,1)S(1)}, u32[]{:S(2)}, u32[]{:S(2)}) collective-permute-start(bf16[96,128]{1,0:T(8,128)(2,1)S(1)} %get-tuple-element.25), channel_id=1, source_target_pairs={{0,1},{1,2},{2,3},{3,4},{4,5},{5,6},{6,7},{7,8},{8,9},{9,10},{10,1... | collective-permute-start | bytes 73736 | tf_op jit(solution)/shard_map/ppermute | solution.py:360
  19.5 5.4 %collective-permute-start.3 = (bf16[96,128]{1,0:T(8,128)(2,1)S(1)}, bf16[96,128]{1,0:T(8,128)(2,1)S(1)}, u32[]{:S(2)}, u32[]{:S(2)}) collective-permute-start(bf16[96,128]{1,0:T(8,128)(2,1)S(1)} %get-tuple-element.26), channel_id=1, source_target_pairs={{1,0},{2,1},{3,2},{4,3},{5,4},{6,5},{7,6},{8,7},{9,8},{10,9},{11,1... | collective-permute-start | bytes 73736 | tf_op jit(solution)/shard_map/ppermute | solution.py:360
  25.8 22.3 %all-to-all-start = ((bf16[32,64,128]{2,1,0:T(8,128)(2,1)}), bf16[32,64,128]{2,1,0:T(8,128)(2,1)S(1)}, u32[]{:S(2)}, u32[]{:S(2)}) async-start(bf16[32,64,128]{2,1,0:T(8,128)(2,1)} %bitcast.3), calls=%async_computation | async-start | bytes 1048576 | tf_op jit(solution)/shard_map/all_to_all | solution.py:346
  48.2 5.8 %collective-permute-start.7 = (bf16[64,128]{1,0:T(8,128)(2,1)S(1)}, bf16[64,128]{1,0:T(8,128)(2,1)S(1)}, u32[]{:S(2)}, u32[]{:S(2)}) collective-permute-start(bf16[64,128]{1,0:T(8,128)(2,1)S(1)} %sum_around.1.refs_0_), channel_id=1, source_target_pairs={{0,6},{1,7},{2,0},{3,1},{4,2},{5,3},{6,4},{7,5},{8,14},{9,15},{10,... | collective-permute-start | bytes 49160 | tf_op jit(solution)/shard_map/ppermute | solution.py:354
  51.5 6.5 %collective-permute-start.6 = (bf16[64,128]{1,0:T(8,128)(2,1)S(1)}, bf16[64,128]{1,0:T(8,128)(2,1)S(1)}, u32[]{:S(2)}, u32[]{:S(2)}) collective-permute-start(bf16[64,128]{1,0:T(8,128)(2,1)S(1)} %sum_around.1.refs_0_), channel_id=1, source_target_pairs={{0,4},{1,5},{2,6},{3,7},{4,0},{5,1},{6,2},{7,3},{8,12},{9,13},{10,... | collective-permute-start | bytes 49160 | tf_op jit(solution)/shard_map/ppermute | solution.py:354
  54.0 4.7 %collective-permute-start.5 = (bf16[64,128]{1,0:T(8,128)(2,1)S(1)}, bf16[64,128]{1,0:T(8,128)(2,1)S(1)}, u32[]{:S(2)}, u32[]{:S(2)}) collective-permute-start(bf16[64,128]{1,0:T(8,128)(2,1)S(1)} %sum_around.1.refs_0_), channel_id=1, source_target_pairs={{0,2},{1,3},{2,4},{3,5},{4,6},{5,7},{6,0},{7,1},{8,10},{9,11},{10,... | collective-permute-start | bytes 49160 | tf_op jit(solution)/shard_map/ppermute | solution.py:354
  71.5 7.5 %collective-permute-start.8 = (bf16[2048,128]{1,0:T(8,128)(2,1)S(1)}, bf16[2048,128]{1,0:T(8,128)(2,1)S(1)}, u32[]{:S(2)}, u32[]{:S(2)}) collective-permute-start(bf16[2048,128]{1,0:T(8,128)(2,1)S(1)} %bitcast.5), channel_id=1, source_target_pairs={{0,32},{1,33},{2,34},{3,35},{4,36},{5,37},{6,38},{7,39},{8,40},{9,... | collective-permute-start | bytes 1572872 | tf_op jit(solution)/shard_map/ppermute | solution.py:350

commit v4 on v3

--- a/solution.py
+++ b/solution.py
@@ -21,7 +21,6 @@
 BOTH = ("group", "dev")
 ROWS = 4096
 HALF = ROWS // 2
-PACKED = 648
 AROUND = 32
 INPUTS = [pltpu.VMEM((CH, 1024), BF16), pltpu.VMEM((CH, 1024), BF16), pltpu.VMEM((1, 1024), jnp.int32)]
 
@@ -47,13 +46,12 @@
     return pair_planes(first, second)
 
 
-def selection(nb_ref, face):
+def source_lanes(nb_ref, face):
     base = {0: 0, -1: 2, 1: 4}[face]
     lane = lax.broadcasted_iota(jnp.int32, (1, 128), 1)
-    source = lax.broadcasted_iota(jnp.int32, (128, 128), 0)
     y = (lane // 8) % 8
     z = lane % 8
-    pieces = []
+    rows = []
     for dy, dz in PAIRS:
         far_y = y + dy
         far_z = z + dz
@@ -72,9 +70,13 @@
 
         found = jnp.where(lane < 64, entry(0), entry(1))
         column = found * 64 + (far_y & 7) * 8 + (far_z & 7)
-        column = jnp.where(found < 0, -1, column)
-        pieces.append(jnp.where(source == column, 1.0, 0.0).astype(BF16))
-    return pieces
+        rows.append(jnp.where(found < 0, -1, column).astype(F32))
+    return rows
+
+
+def selection(rows):
+    source = lax.broadcasted_iota(jnp.int32, (128, 128), 0).astype(F32)
+    return jnp.concatenate([jnp.where(source == row, 1.0, 0.0).astype(BF16) for row in rows], axis=1)
 
 
 def fetch(sources, targets, sems):
@@ -87,14 +89,23 @@
     return copies
 
 
-def rim_kernel(feat_hbm, cot_hbm, occ_hbm, low_ref, high_ref, feat_ref, cot_ref, occ_ref, sems):
-    for copy in fetch((feat_hbm, cot_hbm, occ_hbm), (feat_ref, cot_ref, occ_ref), sems):
+def rim_kernel(
+    feat_hbm, cot_hbm, occ_hbm, nb_hbm, low_ref, high_ref, feat_ref, cot_ref, occ_ref, nb_ref, sems
+):
+    copies = fetch((nb_hbm, occ_hbm, feat_hbm, cot_hbm), (nb_ref, occ_ref, feat_ref, cot_ref), sems)
+    copies[0].wait()
+    inner = source_lanes(nb_ref, 0)
+    sides = [inner + source_lanes(nb_ref, face) for face in (-1, 1)]
+    for copy in copies[1:]:
         copy.wait()
-    for x, pick, out_ref in ((0, 0, low_ref), (6, 1, high_ref)):
-        mask = to_planes(occ_ref, x)[pick] > 0
-        for row, ref in ((0, feat_ref), (CH, cot_ref)):
-            plane = to_planes(ref, x)[pick]
-            out_ref[row : row + CH, :] = jnp.where(mask, plane, 0.0).astype(BF16)
+    for x, edge, rows, out_ref in ((0, 0, sides[0], low_ref), (6, 1, sides[1], high_ref)):
+        masks = to_planes(occ_ref, x)
+        planes = [jnp.where(m > 0, p, 0.0) for m, p in zip(masks, to_planes(feat_ref, x))]
+        out_ref[:CH, :] = planes[edge].astype(BF16)
+        out_ref[CH : 2 * CH, :] = jnp.where(masks[edge] > 0, to_planes(cot_ref, x)[edge], 0.0).astype(BF16)
+        out_ref[2 * CH : 3 * CH, :] = planes[1 - edge].astype(BF16)
+        table = jnp.concatenate([masks[edge]] + rows + [jnp.zeros((13, 128), F32)], axis=0)
+        out_ref[3 * CH :, :] = table.astype(BF16)
 
 
 def turned(w_ref, d):
@@ -113,8 +124,7 @@
     )
     copies[0].wait()
     for index, face in enumerate((-1, 0, 1)):
-        for j, piece in enumerate(selection(nb_ref, face)):
-            sel_ref[index, :, j * 128 : (j + 1) * 128] = piece
+        sel_ref[index] = selection(source_lanes(nb_ref, face))
     for copy in copies[1:4]:
         copy.wait()
     for x in range(0, 8, 2):
@@ -137,14 +147,15 @@
     for copy in copies[4:]:
         copy.wait()
     for d in range(3):
-        w1t_ref[d] = turned(w1_ref, d)
-        wb_ref[d] = jnp.concatenate(
+        w1t_ref[d * CH : (d + 1) * CH, :] = turned(w1_ref, d)
+        wb_ref[d * CH : (d + 1) * CH, :] = jnp.concatenate(
             [w2_ref[(26 - d * 9 - j) * CH : (27 - d * 9 - j) * CH, :] for j in range(9)], axis=1
         )
     for k, w_ref in ((0, w1t_ref), (1, wb_ref)):
-        part_ref[k] = dot(w_ref[1], v_ref[k])
-        part_ref[k, :, 128:] += dot(w_ref[0], v_ref[k, :, :896])
-        part_ref[k, :, :896] += dot(w_ref[2], v_ref[k, :, 128:])
+        full = dot(w_ref[...], v_ref[k])
+        part_ref[k] = full[CH : 2 * CH]
+        part_ref[k, :, 128:] += full[:CH, :896]
+        part_ref[k, :, :896] += full[2 * CH :, 128:]
 
 
 def spread_planes(stacked, sel_ref, place):
@@ -155,67 +166,76 @@
             place(j + k, spread[:, k * 128 : (k + 1) * 128])
 
 
-def spread_rim(rim, sel_ref, index, rows):
-    full = dot(rim, sel_ref[index]).astype(BF16)
-    parts = []
-    for r in range(0, rows, CH):
-        parts.append(
-            jnp.concatenate([full[r : r + CH, j * 128 : (j + 1) * 128] for j in range(9)], axis=0)
-        )
-    return parts
-
-
-def point_kernel(
-    part_ref, w1t_ref, wb_ref, sel_ref, mask_ref, low_ref, high_ref,
-    grad_ref, rim_ref, a1_low_ref, a1_high_ref,
-):
-    lows = spread_rim(low_ref[...], sel_ref, 0, 2 * CH)
-    highs = spread_rim(high_ref[...], sel_ref, 2, 2 * CH)
+def spread_rim(rim, select):
+    full = dot(rim, select).astype(BF16)
+    return [
+        jnp.concatenate([full[r : r + CH, j * 128 : (j + 1) * 128] for j in range(9)], axis=0)
+        for r in range(0, rim.shape[0], CH)
+    ]
+
+
+def point_kernel(part_ref, w1t_ref, wb_ref, sel_ref, mask_ref, low_ref, high_ref, grad_ref, rim_ref):
+    lows = spread_rim(low_ref[: 2 * CH, :], sel_ref[0])
+    highs = spread_rim(high_ref[: 2 * CH, :], sel_ref[2])
     for k in range(2):
-        rim_ref[k, 0] = lows[k]
-        rim_ref[k, 1] = highs[k]
+        rim_ref[k, :, :128] = lows[k]
+        rim_ref[k, :, 128:] = highs[k]
 
     def finish(k, w_ref):
-        first = part_ref[k, :, :128] + dot(w_ref[0], lows[k])
-        last = part_ref[k, :, 896:] + dot(w_ref[2], highs[k])
+        first = part_ref[k, :, :128] + dot(w_ref[:CH, :], lows[k])
+        last = part_ref[k, :, 896:] + dot(w_ref[2 * CH :, :], highs[k])
         return mask_ref[...] * jnp.concatenate([first, part_ref[k, :, 128:896], last], axis=1)
 
     z = finish(0, w1t_ref)
     sigma = 1.0 / (1.0 + jnp.exp(-z))
-    a1 = (z * sigma).astype(BF16)
-    grad_ref[1] = a1
-    a1_low_ref[...] = a1[:, :128]
-    a1_high_ref[...] = a1[:, 896:]
+    grad_ref[1] = (z * sigma).astype(BF16)
     ga = finish(1, wb_ref)
     grad_ref[0] = (ga * sigma * (1.0 + z * (1.0 - sigma))).astype(BF16)
 
 
-def term_kernel(kept, v_ref, rim_ref, grad_ref, out_ref, terms_ref):
+def term_kernel(kept, v_ref, rim_ref, grad_ref, out_ref):
     which = core_index() if kept else 1 - core_index()
     grad = grad_ref[which]
-    inner = v_ref[which]
-    scale = 262144.0 ** -0.5
-    zero = jnp.zeros((K9, 32), F32)
-    views = (
-        jnp.concatenate([rim_ref[which, 0], inner[:, :896]], axis=1),
-        inner,
-        jnp.concatenate([inner[:, 128:], rim_ref[which, 1]], axis=1),
-    )
-    for d, view in enumerate(views):
-        value = dot(view, grad, NT) * scale
-        terms_ref[d * K9 : (d + 1) * K9, :] = jnp.concatenate([value, zero], axis=1)
-    lane = lax.broadcasted_iota(jnp.int32, (PACKED, 128), 1)
-    spare = terms_ref[3 * PACKED : 4 * PACKED, :]
-    for k in range(3):
-        value = jnp.where(
-            lane < 96, terms_ref[k * PACKED : (k + 1) * PACKED, :], pltpu.roll(spare, 96 - 32 * k, 1)
-        )
-        out_ref[k * PACKED : (k + 1) * PACKED, :] = value.astype(out_ref.dtype)
-    out_ref[3 * PACKED : HALF, :] = jnp.zeros((HALF - 3 * PACKED, 128), out_ref.dtype)
+    gap = jnp.zeros((CH, 128), BF16)
+    inner = jnp.concatenate(
+        [
+            jnp.concatenate([grad[:, 128:], gap], axis=1),
+            grad,
+            jnp.concatenate([gap, grad[:, :896]], axis=1),
+        ],
+        axis=0,
+    )
+    sides = jnp.concatenate(
+        [
+            jnp.concatenate([grad[:, :128], gap], axis=1),
+            jnp.concatenate([gap, gap], axis=1),
+            jnp.concatenate([gap, grad[:, 896:]], axis=1),
+        ],
+        axis=0,
+    )
+    value = (dot(inner, v_ref[which], NT) + dot(sides, rim_ref[which], NT)) * (262144.0 ** -0.5)
+    value = jnp.concatenate([value, jnp.zeros((3 * CH, 32), F32)], axis=1).astype(out_ref.dtype)
+    for k in range(7):
+        out_ref[k * 3 * CH : (k + 1) * 3 * CH, :] = value[:, k * 128 : (k + 1) * 128]
+    out_ref[21 * CH :, :] = jnp.zeros((HALF - 21 * CH, 128), out_ref.dtype)
+
+
+def beside(payload_ref, own, below, w1t_ref):
+    table = payload_ref[3 * CH :, :].astype(F32)
+    inner = selection([table[1 + j : 2 + j] for j in range(9)])
+    across = selection([table[10 + j : 11 + j] for j in range(9)])
+    (edge,) = spread_rim(payload_ref[:CH, :], inner)
+    (far,) = spread_rim(payload_ref[2 * CH : 3 * CH, :], inner)
+    (near,) = spread_rim(own, across)
+    before, after = (far, near) if below else (near, far)
+    z = dot(w1t_ref[:CH, :], before) + dot(w1t_ref[CH : 2 * CH, :], edge) + dot(w1t_ref[2 * CH :, :], after)
+    z = table[:1] * z
+    return (z / (1.0 + jnp.exp(-z))).astype(BF16)
 
 
 def out_kernel(
-    grad_ref, low_ref, high_ref, sel_ref, w2_hbm, mask_ref, after_ref, out_ref, w2_ref, v_ref, planes_ref, sems
+    grad_ref, lower_ref, upper_ref, low_ref, high_ref, w1t_ref, sel_ref, w2_hbm, mask_ref, after_ref,
+    out_ref, w2_ref, w2t_ref, v_ref, planes_ref, sems,
 ):
     (copy,) = fetch((w2_hbm,), (w2_ref,), sems)
     for x in range(8):
@@ -226,12 +246,13 @@
             v_ref[j * CH : (j + 1) * CH, (x + 1) * 128 : (x + 2) * 128] = spread[x * CH : (x + 1) * CH]
 
     spread_planes(planes_ref[...].reshape(8 * CH, 128), sel_ref, place)
-    v_ref[:, :128] = spread_rim(low_ref[...], sel_ref, 0, CH)[0]
-    v_ref[:, 1152:] = spread_rim(high_ref[...], sel_ref, 2, CH)[0]
+    v_ref[:, :128] = spread_rim(beside(lower_ref, low_ref[:CH, :], True, w1t_ref), sel_ref[0])[0]
+    v_ref[:, 1152:] = spread_rim(beside(upper_ref, high_ref[:CH, :], False, w1t_ref), sel_ref[2])[0]
     copy.wait()
-    total = dot(turned(w2_ref, 0), v_ref[:, :1024])
-    total += dot(turned(w2_ref, 1), v_ref[:, 128:1152])
-    total += dot(turned(w2_ref, 2), v_ref[:, 256:])
+    for d in range(3):
+        w2t_ref[d * CH : (d + 1) * CH, :] = turned(w2_ref, d)
+    full = dot(w2t_ref[...], v_ref[...])
+    total = full[:CH, :1024] + full[CH : 2 * CH, 128:1152] + full[2 * CH :, 256:]
     total = mask_ref[...] * total
     for x in range(0, 8, 2):
         even = total[:, x * 128 : (x + 1) * 128]
@@ -245,7 +266,7 @@
     return lax.rem(lax.axis_index("group"), 2)
 
 
-def add_kernel(own_ref, got_ref, low_ref, high_ref, out_ref):
+def add_kernel(own_ref, got_ref, out_ref):
     out_ref[...] = (own_ref[...] + got_ref[...].astype(F32)).astype(BF16)
 
 
@@ -273,36 +294,37 @@
     core = core_index()
     packed_ref[pl.ds(pl.multiple_of(core * HALF, HALF), HALF), :] = own_ref[...].astype(F32)
     packed_ref[pl.ds(pl.multiple_of((1 - core) * HALF, HALF), HALF), :] = other_ref[...].astype(F32)
-    lane = lax.broadcasted_iota(jnp.int32, (24, 128), 1)
-
-    def piece(grad, start):
-        base = grad * HALF
-        if start < 3 * PACKED:
-            return packed_ref[base + start : base + start + 24, :]
-        r = base + start - 3 * PACKED
-        value = pltpu.roll(packed_ref[r : r + 24, :], 32, 1)
-        for k in (1, 2):
-            moved = pltpu.roll(packed_ref[r + k * PACKED : r + k * PACKED + 24, :], (32 + 32 * k) % 128, 1)
-            value = jnp.where(lane < 32 * k, value, moved)
+    lane = lax.broadcasted_iota(jnp.int32, (CH, 128), 1)
+
+    def block_of(grad, block):
+        d, j = block // 9, block % 9
+        at, off = j * CH // 128, j * CH % 128
+        row = grad * HALF + at * 3 * CH + d * CH
+        value = packed_ref[row : row + CH, :]
+        if off == 0:
+            return value
+        value = pltpu.roll(value, 128 - off, 1)
+        if off > 32:
+            more = pltpu.roll(packed_ref[row + 3 * CH : row + 4 * CH, :], 128 - off, 1)
+            value = jnp.where(lane < 128 - off, value, more)
         return value
 
-    def block_of(grad, block):
-        return jnp.concatenate([piece(grad, block * CH + 24 * q) for q in range(4)], axis=0)
-
     copies = []
-    for first in range(0, 27, 9):
-        for block in range(first, first + 9):
-            one_ref[block] = block_of(0, block)[:, :CH]
+
+    def flush(ref, hbm, first):
         part = pl.ds(first, 9)
-        copies.append(pltpu.make_async_copy(one_ref.at[part], one_hbm.at[part], sems.at[len(copies)]))
+        copies.append(pltpu.make_async_copy(ref.at[part], hbm.at[part], sems.at[len(copies)]))
         copies[-1].start()
+
     for first in range(18, -1, -9):
         for tap in range(first, first + 9):
-            wide = jnp.concatenate([block_of(1, 26 - tap), jnp.zeros((32, 128), F32)], axis=0)
-            two_ref[tap] = wide.T[:CH, :CH]
-        part = pl.ds(first, 9)
-        copies.append(pltpu.make_async_copy(two_ref.at[part], two_hbm.at[part], sems.at[len(copies)]))
-        copies[-1].start()
+            two_ref[tap] = block_of(1, 26 - tap)[:, :CH]
+        flush(two_ref, two_hbm, first)
+    for first in range(0, 27, 9):
+        for tap in range(first, first + 9):
+            wide = jnp.concatenate([block_of(0, tap), jnp.zeros((32, 128), F32)], axis=0)
+            one_ref[tap] = wide.T[:CH, :CH]
+        flush(one_ref, one_hbm, first)
     for copy in copies:
         copy.wait()
 
@@ -373,10 +395,10 @@
     neighbours = in_hbm(neighbours)
     low, high = call(
         rim_kernel,
-        [shape((2 * CH, 128))] * 2,
-        features_in, cotangent, occ,
-        specs={0: HBM, 1: HBM, 2: HBM},
-        scratch=INPUTS + [pltpu.SemaphoreType.DMA((3,))],
+        [shape((3 * CH + 32, 128))] * 2,
+        features_in, cotangent, occ, neighbours,
+        specs={k: HBM for k in range(4)},
+        scratch=INPUTS + [pltpu.SMEM((2, 27), jnp.int32), pltpu.SemaphoreType.DMA((4,))],
         name="rims",
     )
     upper = dev_shift(low, -1)
@@ -385,7 +407,7 @@
         prep_kernel,
         [
             shape((2, K9, 1024)), shape((2, CH, 1024), F32),
-            shape((3, CH, K9)), shape((3, CH, K9)), shape((3, 128, 1152)), shape((1, 1024), F32),
+            shape((3 * CH, K9)), shape((3 * CH, K9)), shape((3, 128, 1152)), shape((1, 1024), F32),
         ],
         features_in, cotangent, occ, w1, w2, neighbours,
         specs={k: HBM for k in range(6)},
@@ -397,41 +419,36 @@
         flops=4 << 30,
         name="prep",
     )
-    grad, rim, a1_low, a1_high = call(
+    grad, rim = call(
         point_kernel,
-        [shape((2, CH, 1024)), shape((2, 2, K9, 128)), shape((CH, 128)), shape((CH, 128))],
+        [shape((2, CH, 1024)), shape((2, K9, 256))],
         part, w1t, wb, sel, mask, lower, upper,
         limit=16,
         flops=1 << 30,
         name="points",
     )
-    a1_upper = dev_shift(a1_low, -1)
-    a1_lower = dev_shift(a1_high, 1)
 
     def terms(kept):
         return call(
             functools.partial(term_kernel, kept),
             shape((HALF, 128), F32 if kept else BF16),
             v, rim, grad,
-            scratch=[pltpu.VMEM((27 * CH, 128), F32)],
             limit=16,
             flops=2 << 30,
             name="terms_kept" if kept else "terms_sent",
         )
 
     got = swap_core(terms(False))
-    value = call(
-        add_kernel, shape((HALF, 128)), terms(True), got, a1_lower, a1_upper,
-        specs={2: ANY, 3: ANY}, name="sum_core",
-    )
+    value = call(add_kernel, shape((HALF, 128)), terms(True), got, name="sum_core")
     moved = all_to_all(value.reshape(AROUND, HALF // AROUND, 128))
     features_out = call(
         out_kernel,
         shape((CH, 1024)),
-        grad, a1_lower, a1_upper, sel, w2, mask, in_hbm(value),
-        specs={4: HBM, 6: HBM},
+        grad, lower, upper, low, high, w1t, sel, w2, mask, in_hbm(value),
+        specs={7: HBM, 9: HBM},
         scratch=[
-            pltpu.VMEM((27 * CH, CH), BF16), pltpu.VMEM((K9, 1280), BF16), pltpu.VMEM((8, CH, 128), BF16),
+            pltpu.VMEM((27 * CH, CH), BF16), pltpu.VMEM((3 * CH, K9), BF16),
+            pltpu.VMEM((K9, 1280), BF16), pltpu.VMEM((8, CH, 128), BF16),
             pltpu.SemaphoreType.DMA((1,)),
         ],
         limit=16,

time: 81.4 us -> 73.1 us (0.90)
  starting transfers between devices: 35.1 us -> 29.1 us
  waiting for transfers between devices: 16.3 us -> 13.8 us
    ppermute x4 -> x2, starting transfers between devices: 11 us -> 5.67 us  [dev_shift(): return lax.ppermute(value, 'dev', pairs)]
    ppermute x4 -> x2, waiting for transfers between devices: 2.42 us -> 0.36 us  [dev_shift(): return lax.ppermute(value, 'dev', pairs)]
    ppermute x3, starting transfers between devices: 5.8 us -> 6.89 us  [swap_z(): lax.ppermute(value, BOTH, device_pairs(lambda x, y, z, core: (x, y, (z +...]
    all_to_all x1, waiting for transfers between devices: 7.65 us -> 6.64 us  [all_to_all(): lax.all_to_all(value, BOTH, 0, 0, axis_index_groups=around_groups(), tile...]
    ppermute x2, starting transfers between devices: 7.29 us -> 6.3 us  [swap_core(): lax.ppermute(value, BOTH, device_pairs(lambda x, y, z, core: (x, y, z, 1...]
    all_to_all x1, blocking collectives: 12.8 us -> 13.6 us  [all_to_all(): lax.all_to_all(value, BOTH, 0, 0, axis_index_groups=around_groups(), tile...]
  transfers between devices with their start and end apart: 10 -> 8, of which waited for: 5 -> 6; matrix products, arithmetic and copies ran while one was open for 0% -> 0% of each run, Pallas kernels for 12% -> 13%
where the time goes in v4:
time: 73.1 us; the launch traced here: 72.8 us
  starting transfers between devices  29.1 us (40%)
  Pallas kernels  15.5 us (21%)
  waiting for transfers between devices  13.8 us (19%)
  blocking collectives  13.6 us (19%)
    pallas_call x10, Pallas kernels, call(): pl.pallas_call(kernel, out_shape=outs, in_specs=[specs.get(k, VMEM) for k...  15.5 us
    all_to_all x1, blocking collectives, all_to_all(): lax.all_to_all(value, BOTH, 0, 0, axis_index_groups=around_groups(), tile...  13.6 us
    all_to_all x1, starting transfers between devices, all_to_all(): lax.all_to_all(value, BOTH, 0, 0, axis_index_groups=around_groups(), tile...  10.3 us
    ppermute x3, starting transfers between devices, swap_z(): lax.ppermute(value, BOTH, device_pairs(lambda x, y, z, core: (x, y, (z +...  6.89 us
    all_to_all x1, waiting for transfers between devices, all_to_all(): lax.all_to_all(value, BOTH, 0, 0, axis_index_groups=around_groups(), tile...  6.64 us
    ppermute x2, starting transfers between devices, swap_core(): lax.ppermute(value, BOTH, device_pairs(lambda x, y, z, core: (x, y, z, 1...  6.3 us
    ppermute x2, starting transfers between devices, dev_shift(): return lax.ppermute(value, 'dev', pairs)  5.67 us
    ppermute x3, waiting for transfers between devices, swap_z(): lax.ppermute(value, BOTH, device_pairs(lambda x, y, z, core: (x, y, (z +...  4.69 us
  transfers between devices with their start and end apart: 8, of which 6 were waited for; matrix products, arithmetic and copies ran while one was open for 0% of the time, Pallas kernels for 13%

profile of v4, /device:TPU:1, one launch (start us, length us, event | category | flops | bytes accessed | tf_op | source)
XLA Modules:
  0.0 72.8 jit_solution(5163332627811240555)
XLA Ops:
  0.6 1.2 %rims.1 = (bf16[320,128]{1,0:T(8,128)(2,1)S(1)}, bf16[320,128]{1,0:T(8,128)(2,1)S(1)}) custom-call(bf16[96,1024]{1,0:T(8,128)(2,1)} %feat_hbm.3, bf16[96,1024]{1,0:T(8,128)(2,1)} %cot_hbm.3, s32[1,1024]{1,0:T(1,128)} %bitcast.7, s32[2,27]{1,0:T(2,128)} %nb_hbm.3), custom_call_target="tpu_custom_call" | custom-call | bytes 1048576 | tf_op jit(solution)/shard_map/rims/pallas_call | solution.py:338
  1.8 4.4 %collective-permute-start = (bf16[320,128]{1,0:T(8,128)(2,1)S(1)}, bf16[320,128]{1,0:T(8,128)(2,1)S(1)}, u32[]{:S(2)}, u32[]{:S(2)}) collective-permute-start(bf16[320,128]{1,0:T(8,128)(2,1)S(1)} %get-tuple-element.20.high_ref), channel_id=1, source_target_pairs={{0,1},{1,2},{2,3},{3,4},{4,5},{5,6},{6,7},{7,8},{8,9},{9,10},{10,1... | collective-permute-start | bytes 245768 | tf_op jit(solution)/shard_map/ppermute | solution.py:382
  6.2 1.3 %collective-permute-start.1 = (bf16[320,128]{1,0:T(8,128)(2,1)S(1)}, bf16[320,128]{1,0:T(8,128)(2,1)S(1)}, u32[]{:S(2)}, u32[]{:S(2)}) collective-permute-start(bf16[320,128]{1,0:T(8,128)(2,1)S(1)} %get-tuple-element.21.low_ref), channel_id=1, source_target_pairs={{1,0},{2,1},{3,2},{4,3},{5,4},{6,5},{7,6},{8,7},{9,8},{10,9},{11,1... | collective-permute-start | bytes 245768 | tf_op jit(solution)/shard_map/ppermute | solution.py:382
  7.5 3.7 %prep.1 = (bf16[2,864,1024]{2,1,0:T(8,128)(2,1)S(1)}, f32[2,96,1024]{2,1,0:T(8,128)S(1)}, bf16[288,864]{1,0:T(8,128)(2,1)S(1)}, bf16[288,864]{1,0:T(8,128)(2,1)S...) custom-call(bf16[96,1024]{1,0:T(8,128)(2,1)} %feat_hbm.3, bf16[96,1024]{1,0:T(8,128)(2,1)} %cot_hbm.3, ...), custom_call_target="tpu_custom_call" | custom-call | flops 4294967296 | bytes 1048576 | tf_op jit(solution)/shard_map/prep/pallas_call | solution.py:338
  11.2 0.0 collective-permute-done.low_ref.lower_ref
  11.2 0.4 collective-permute-done.1.high_ref.upper_ref
  11.6 0.7 points.1
  12.3 1.0 %terms_sent.1 = bf16[2048,128]{1,0:T(8,128)(2,1)S(1)} custom-call(bf16[2,864,1024]{2,1,0:T(8,128)(2,1)S(1)} %get-tuple-element.23.v_ref, bf16[2,864,256]{2,1,0:T(8,128)(2,1)S(1)} %get-tuple-element.24.rim_ref, bf16[2,96,1024]{2,1,0:T(8,128)(2,1)S(1)} %get-tuple-element.22.grad_ref), custom_call_target="tpu_custom_call" | custom-call | flops 2147483648 | bytes 1048576 | tf_op jit(solution)/shard_map/terms_sent/pallas_call | solution.py:338
  13.3 2.0 %collective-permute-start.2 = (bf16[2048,128]{1,0:T(8,128)(2,1)S(1)}, bf16[2048,128]{1,0:T(8,128)(2,1)S(1)}, u32[]{:S(2)}, u32[]{:S(2)}) collective-permute-start(bf16[2048,128]{1,0:T(8,128)(2,1)S(1)} %terms_sent.1), channel_id=1, source_target_pairs={{0,32},{1,33},{2,34},{3,35},{4,36},{5,37},{6,38},{7,39},{8,40},{9,... | collective-permute-start | bytes 1572872 | tf_op jit(solution)/shard_map/ppermute | solution.py:372
  15.3 1.0 %terms_kept.1.own_ref = f32[2048,128]{1,0:T(8,128)S(1)} custom-call(bf16[2,864,1024]{2,1,0:T(8,128)(2,1)S(1)} %get-tuple-element.23.v_ref, bf16[2,864,256]{2,1,0:T(8,128)(2,1)S(1)} %get-tuple-element.24.rim_ref, bf16[2,96,1024]{2,1,0:T(8,128)(2,1)S(1)} %get-tuple-element.22.grad_ref), custom_call_target="tpu_custom_call" | custom-call | flops 2147483648 | bytes 1048576 | tf_op jit(solution)/shard_map/terms_kept/pallas_call | solution.py:338
  16.2 0.6 collective-permute-done.2.got_ref
  16.8 0.9 %sum_core.1.after_ref = bf16[2048,128]{1,0:T(8,128)(2,1)} custom-call(f32[2048,128]{1,0:T(8,128)S(1)} %terms_kept.1.own_ref, bf16[2048,128]{1,0:T(8,128)(2,1)S(1)} %collective-permute-done.2.got_ref), custom_call_target="tpu_custom_call" | custom-call | bytes 1048576 | tf_op jit(solution)/shard_map/sum_core/pallas_call | solution.py:338
  17.7 10.3 %all-to-all-start = ((bf16[32,64,128]{2,1,0:T(8,128)(2,1)}), bf16[32,64,128]{2,1,0:T(8,128)(2,1)S(1)}, u32[]{:S(2)}, u32[]{:S(2)}) async-start(bf16[32,64,128]{2,1,0:T(8,128)(2,1)} %bitcast.3), calls=%async_computation | async-start | bytes 1048576 | tf_op jit(solution)/shard_map/all_to_all | solution.py:368
  28.0 4.7 %features.1.after_ref = bf16[96,1024]{1,0:T(8,128)(2,1)} custom-call(bf16[2,96,1024]{2,1,0:T(8,128)(2,1)S(1)} %get-tuple-element.22.grad_ref, bf16[320,128]{1,0:T(8,128)(2,1)S(1)} %collective-permute-done.low_ref.lower_ref, bf16[320,128]{1,0:T(8,128)(2,1)S(1)} %collective-permute-done.1.high_ref.upper_ref, bf16[320,128]{1,0:T(8,128)(2,1)S(1)} %get-tuple-element.21.low_ref, ...), custom_call_target="tpu_custom_call" | custom-call | flops 3221225472 | bytes 1048576 | tf_op jit(solution)/shard_map/features/pallas_call | solution.py:338
  32.7 6.6 %all-to-all-done.got_ref = bf16[32,64,128]{2,1,0:T(8,128)(2,1)S(1)} async-done(((bf16[32,64,128]{2,1,0:T(8,128)(2,1)}), bf16[32,64,128]{2,1,0:T(8,128)(2,1)S(1)}, u32[]{:S(2)}, u32[]{:S(2)}) %all-to-all-start) | async-done | bytes 524320 | tf_op jit(solution)/shard_map/all_to_all | solution.py:368
  39.4 0.1 sum_around.1.refs_0_
  39.5 3.5 %collective-permute-start.5 = (bf16[64,128]{1,0:T(8,128)(2,1)S(1)}, bf16[64,128]{1,0:T(8,128)(2,1)S(1)}, u32[]{:S(2)}, u32[]{:S(2)}) collective-permute-start(bf16[64,128]{1,0:T(8,128)(2,1)S(1)} %sum_around.1.refs_0_), channel_id=1, source_target_pairs={{0,6},{1,7},{2,0},{3,1},{4,2},{5,3},{6,4},{7,5},{8,14},{9,15},{10,... | collective-permute-start | bytes 49160 | tf_op jit(solution)/shard_map/ppermute | solution.py:376
  43.0 3.4 %collective-permute-start.4 = (bf16[64,128]{1,0:T(8,128)(2,1)S(1)}, bf16[64,128]{1,0:T(8,128)(2,1)S(1)}, u32[]{:S(2)}, u32[]{:S(2)}) collective-permute-start(bf16[64,128]{1,0:T(8,128)(2,1)S(1)} %sum_around.1.refs_0_), channel_id=1, source_target_pairs={{0,4},{1,5},{2,6},{3,7},{4,0},{5,1},{6,2},{7,3},{8,12},{9,13},{10,... | collective-permute-start | bytes 49160 | tf_op jit(solution)/shard_map/ppermute | solution.py:376
  46.4 0.0 collective-permute-start.3
  46.4 0.0 collective-permute-done.5.refs_3_
  46.4 3.1 %collective-permute-done.4.refs_2_ = bf16[64,128]{1,0:T(8,128)(2,1)S(1)} collective-permute-done((bf16[64,128]{1,0:T(8,128)(2,1)S(1)}, bf16[64,128]{1,0:T(8,128)(2,1)S(1)}, u32[]{:S(2)}, u32[]{:S(2)}) %collective-permute-start.4) | collective-permute-done | bytes 16416 | tf_op jit(solution)/shard_map/ppermute | solution.py:376
  49.5 1.6 %collective-permute-done.3.refs_1_ = bf16[64,128]{1,0:T(8,128)(2,1)S(1)} collective-permute-done((bf16[64,128]{1,0:T(8,128)(2,1)S(1)}, bf16[64,128]{1,0:T(8,128)(2,1)S(1)}, u32[]{:S(2)}, u32[]{:S(2)}) %collective-permute-start.3) | collective-permute-done | bytes 16416 | tf_op jit(solution)/shard_map/ppermute | solution.py:376
  51.0 0.1 sum_z.1
  51.1 13.6 %all_to_all.10 = bf16[32,64,128]{2,1,0:T(8,128)(2,1)S(1)} all-to-all(bf16[32,64,128]{2,1,0:T(8,128)(2,1)S(1)} %sum_z.1), channel_id=1, replica_groups={{0,1,8,9,16,17,24,25,64,65,72,73,80,81,88,89,128,129,136,137,144,145,15..., dimensions={0} | all-to-all | bytes 1048576 | tf_op jit(solution)/shard_map/all_to_all | solution.py:368
  64.7 4.3 %collective-permute-start.6 = (bf16[2048,128]{1,0:T(8,128)(2,1)S(1)}, bf16[2048,128]{1,0:T(8,128)(2,1)S(1)}, u32[]{:S(2)}, u32[]{:S(2)}) collective-permute-start(bf16[2048,128]{1,0:T(8,128)(2,1)S(1)} %bitcast.5), channel_id=1, source_target_pairs={{0,32},{1,33},{2,34},{3,35},{4,36},{5,37},{6,38},{7,39},{8,40},{9,... | collective-permute-start | bytes 1572872 | tf_op jit(solution)/shard_map/ppermute | solution.py:372
  69.0 1.5 %collective-permute-done.6.other_ref = bf16[2048,128]{1,0:T(8,128)(2,1)S(1)} collective-permute-done((bf16[2048,128]{1,0:T(8,128)(2,1)S(1)}, bf16[2048,128]{1,0:T(8,128)(2,1)S(1)}, u32[]{:S(2)}, u32[]{:S(2)}) %collective-permute-start.6) | collective-permute-done | bytes 524320 | tf_op jit(solution)/shard_map/ppermute | solution.py:372
  70.5 2.2 %unpack.1 = (f32[27,96,96]{2,1,0:T(8,128)}, f32[27,96,96]{2,1,0:T(8,128)}) custom-call(bf16[2048,128]{1,0:T(8,128)(2,1)S(1)} %bitcast.6, bf16[2048,128]{1,0:T(8,128)(2,1)S(1)} %collective-permute-done.6.other_ref), custom_call_target="tpu_custom_call" | custom-call | bytes 1048576 | tf_op jit(solution)/shard_map/unpack/pallas_call | solution.py:338
Async XLA Ops:
  1.8 9.4 %collective-permute-start = (bf16[320,128]{1,0:T(8,128)(2,1)S(1)}, bf16[320,128]{1,0:T(8,128)(2,1)S(1)}, u32[]{:S(2)}, u32[]{:S(2)}) collective-permute-start(bf16[320,128]{1,0:T(8,128)(2,1)S(1)} %get-tuple-element.20.high_ref), channel_id=1, source_target_pairs={{0,1},{1,2},{2,3},{3,4},{4,5},{5,6},{6,7},{7,8},{8,9},{9,10},{10,1... | collective-permute-start | bytes 245768 | tf_op jit(solution)/shard_map/ppermute | solution.py:382
  6.2 5.4 %collective-permute-start.1 = (bf16[320,128]{1,0:T(8,128)(2,1)S(1)}, bf16[320,128]{1,0:T(8,128)(2,1)S(1)}, u32[]{:S(2)}, u32[]{:S(2)}) collective-permute-start(bf16[320,128]{1,0:T(8,128)(2,1)S(1)} %get-tuple-element.21.low_ref), channel_id=1, source_target_pairs={{1,0},{2,1},{3,2},{4,3},{5,4},{6,5},{7,6},{8,7},{9,8},{10,9},{11,1... | collective-permute-start | bytes 245768 | tf_op jit(solution)/shard_map/ppermute | solution.py:382
  13.3 3.5 %collective-permute-start.2 = (bf16[2048,128]{1,0:T(8,128)(2,1)S(1)}, bf16[2048,128]{1,0:T(8,128)(2,1)S(1)}, u32[]{:S(2)}, u32[]{:S(2)}) collective-permute-start(bf16[2048,128]{1,0:T(8,128)(2,1)S(1)} %terms_sent.1), channel_id=1, source_target_pairs={{0,32},{1,33},{2,34},{3,35},{4,36},{5,37},{6,38},{7,39},{8,40},{9,... | collective-permute-start | bytes 1572872 | tf_op jit(solution)/shard_map/ppermute | solution.py:372
  17.7 21.7 %all-to-all-start = ((bf16[32,64,128]{2,1,0:T(8,128)(2,1)}), bf16[32,64,128]{2,1,0:T(8,128)(2,1)S(1)}, u32[]{:S(2)}, u32[]{:S(2)}) async-start(bf16[32,64,128]{2,1,0:T(8,128)(2,1)} %bitcast.3), calls=%async_computation | async-start | bytes 1048576 | tf_op jit(solution)/shard_map/all_to_all | solution.py:368
  39.5 6.9 %collective-permute-start.5 = (bf16[64,128]{1,0:T(8,128)(2,1)S(1)}, bf16[64,128]{1,0:T(8,128)(2,1)S(1)}, u32[]{:S(2)}, u32[]{:S(2)}) collective-permute-start(bf16[64,128]{1,0:T(8,128)(2,1)S(1)} %sum_around.1.refs_0_), channel_id=1, source_target_pairs={{0,6},{1,7},{2,0},{3,1},{4,2},{5,3},{6,4},{7,5},{8,14},{9,15},{10,... | collective-permute-start | bytes 49160 | tf_op jit(solution)/shard_map/ppermute | solution.py:376
  43.0 6.5 %collective-permute-start.4 = (bf16[64,128]{1,0:T(8,128)(2,1)S(1)}, bf16[64,128]{1,0:T(8,128)(2,1)S(1)}, u32[]{:S(2)}, u32[]{:S(2)}) collective-permute-start(bf16[64,128]{1,0:T(8,128)(2,1)S(1)} %sum_around.1.refs_0_), channel_id=1, source_target_pairs={{0,4},{1,5},{2,6},{3,7},{4,0},{5,1},{6,2},{7,3},{8,12},{9,13},{10,... | collective-permute-start | bytes 49160 | tf_op jit(solution)/shard_map/ppermute | solution.py:376
  46.4 4.7 %collective-permute-start.3 = (bf16[64,128]{1,0:T(8,128)(2,1)S(1)}, bf16[64,128]{1,0:T(8,128)(2,1)S(1)}, u32[]{:S(2)}, u32[]{:S(2)}) collective-permute-start(bf16[64,128]{1,0:T(8,128)(2,1)S(1)} %sum_around.1.refs_0_), channel_id=1, source_target_pairs={{0,2},{1,3},{2,4},{3,5},{4,6},{5,7},{6,0},{7,1},{8,10},{9,11},{10,... | collective-permute-start | bytes 49160 | tf_op jit(solution)/shard_map/ppermute | solution.py:376
  64.7 5.8 %collective-permute-start.6 = (bf16[2048,128]{1,0:T(8,128)(2,1)S(1)}, bf16[2048,128]{1,0:T(8,128)(2,1)S(1)}, u32[]{:S(2)}, u32[]{:S(2)}) collective-permute-start(bf16[2048,128]{1,0:T(8,128)(2,1)S(1)} %bitcast.5), channel_id=1, source_target_pairs={{0,32},{1,33},{2,34},{3,35},{4,36},{5,37},{6,38},{7,39},{8,40},{9,... | collective-permute-start | bytes 1572872 | tf_op jit(solution)/shard_map/ppermute | solution.py:372

commit v5 on v4

--- a/solution.py
+++ b/solution.py
@@ -90,7 +90,7 @@
 
 
 def rim_kernel(
-    feat_hbm, cot_hbm, occ_hbm, nb_hbm, low_ref, high_ref, feat_ref, cot_ref, occ_ref, nb_ref, sems
+    feat_hbm, cot_hbm, occ_hbm, nb_hbm, first_ref, second_ref, feat_ref, cot_ref, occ_ref, nb_ref, both_ref, sems
 ):
     copies = fetch((nb_hbm, occ_hbm, feat_hbm, cot_hbm), (nb_ref, occ_ref, feat_ref, cot_ref), sems)
     copies[0].wait()
@@ -98,7 +98,8 @@
     sides = [inner + source_lanes(nb_ref, face) for face in (-1, 1)]
     for copy in copies[1:]:
         copy.wait()
-    for x, edge, rows, out_ref in ((0, 0, sides[0], low_ref), (6, 1, sides[1], high_ref)):
+    for x, edge, rows in ((0, 0, sides[0]), (6, 1, sides[1])):
+        out_ref = both_ref.at[edge]
         masks = to_planes(occ_ref, x)
         planes = [jnp.where(m > 0, p, 0.0) for m, p in zip(masks, to_planes(feat_ref, x))]
         out_ref[:CH, :] = planes[edge].astype(BF16)
@@ -106,6 +107,20 @@
         out_ref[2 * CH : 3 * CH, :] = planes[1 - edge].astype(BF16)
         table = jnp.concatenate([masks[edge]] + rows + [jnp.zeros((13, 128), F32)], axis=0)
         out_ref[3 * CH :, :] = table.astype(BF16)
+    odd = dev_parity()
+    first_ref[...] = both_ref[1 - odd]
+    second_ref[...] = both_ref[odd]
+
+
+def dev_parity():
+    return lax.rem(lax.axis_index("dev"), 2)
+
+
+def lower_upper(first_ref, second_ref, both_ref):
+    both_ref[0] = first_ref[...]
+    both_ref[1] = second_ref[...]
+    odd = dev_parity()
+    return both_ref.at[1 - odd], both_ref.at[odd]
 
 
 def turned(w_ref, d):
@@ -174,7 +189,8 @@
     ]
 
 
-def point_kernel(part_ref, w1t_ref, wb_ref, sel_ref, mask_ref, low_ref, high_ref, grad_ref, rim_ref):
+def point_kernel(part_ref, w1t_ref, wb_ref, sel_ref, mask_ref, first_ref, second_ref, grad_ref, rim_ref, both_ref):
+    low_ref, high_ref = lower_upper(first_ref, second_ref, both_ref)
     lows = spread_rim(low_ref[: 2 * CH, :], sel_ref[0])
     highs = spread_rim(high_ref[: 2 * CH, :], sel_ref[2])
     for k in range(2):
@@ -234,8 +250,8 @@
 
 
 def out_kernel(
-    grad_ref, lower_ref, upper_ref, low_ref, high_ref, w1t_ref, sel_ref, w2_hbm, mask_ref, after_ref,
-    out_ref, w2_ref, w2t_ref, v_ref, planes_ref, sems,
+    grad_ref, got_first_ref, got_second_ref, first_ref, second_ref, w1t_ref, sel_ref, w2_hbm, mask_ref, after_ref,
+    out_ref, w2_ref, w2t_ref, v_ref, planes_ref, got_ref, own_ref, sems,
 ):
     (copy,) = fetch((w2_hbm,), (w2_ref,), sems)
     for x in range(8):
@@ -246,6 +262,8 @@
             v_ref[j * CH : (j + 1) * CH, (x + 1) * 128 : (x + 2) * 128] = spread[x * CH : (x + 1) * CH]
 
     spread_planes(planes_ref[...].reshape(8 * CH, 128), sel_ref, place)
+    lower_ref, upper_ref = lower_upper(got_first_ref, got_second_ref, got_ref)
+    low_ref, high_ref = lower_upper(first_ref, second_ref, own_ref)
     v_ref[:, :128] = spread_rim(beside(lower_ref, low_ref[:CH, :], True, w1t_ref), sel_ref[0])[0]
     v_ref[:, 1152:] = spread_rim(beside(upper_ref, high_ref[:CH, :], False, w1t_ref), sel_ref[2])[0]
     copy.wait()
@@ -281,7 +299,7 @@
     out_ref, slots_ref = refs[-2:]
     me = lax.rem(lax.axis_index("dev"), 8) // 2
     for k in range(4):
-        slots_ref[lax.rem(me + 4 - k, 4)] = refs[k][...]
+        slots_ref[me ^ k] = refs[k][...]
     total = slots_ref[0].astype(F32)
     for k in range(1, 4):
         total += slots_ref[k].astype(F32)
@@ -290,16 +308,16 @@
         out_ref[k] = total
 
 
-def grads_kernel(own_ref, other_ref, one_hbm, two_hbm, packed_ref, one_ref, two_ref, sems):
-    core = core_index()
-    packed_ref[pl.ds(pl.multiple_of(core * HALF, HALF), HALF), :] = own_ref[...].astype(F32)
-    packed_ref[pl.ds(pl.multiple_of((1 - core) * HALF, HALF), HALF), :] = other_ref[...].astype(F32)
+def unpack_kernel(own, *refs):
+    half_ref = refs[0]
+    one_hbm, two_hbm, packed_ref, out_ref, sems = refs[-5:]
+    packed_ref[...] = half_ref[...].astype(F32)
     lane = lax.broadcasted_iota(jnp.int32, (CH, 128), 1)
 
-    def block_of(grad, block):
+    def block_of(block):
         d, j = block // 9, block % 9
         at, off = j * CH // 128, j * CH % 128
-        row = grad * HALF + at * 3 * CH + d * CH
+        row = at * 3 * CH + d * CH
         value = packed_ref[row : row + CH, :]
         if off == 0:
             return value
@@ -309,31 +327,37 @@
             value = jnp.where(lane < 128 - off, value, more)
         return value
 
-    copies = []
-
-    def flush(ref, hbm, first):
-        part = pl.ds(first, 9)
-        copies.append(pltpu.make_async_copy(ref.at[part], hbm.at[part], sems.at[len(copies)]))
-        copies[-1].start()
-
-    for first in range(18, -1, -9):
-        for tap in range(first, first + 9):
-            two_ref[tap] = block_of(1, 26 - tap)[:, :CH]
-        flush(two_ref, two_hbm, first)
-    for first in range(0, 27, 9):
-        for tap in range(first, first + 9):
-            wide = jnp.concatenate([block_of(0, tap), jnp.zeros((32, 128), F32)], axis=0)
-            one_ref[tap] = wide.T[:CH, :CH]
-        flush(one_ref, one_hbm, first)
-    for copy in copies:
-        copy.wait()
+    def write(hbm, make):
+        copies = []
+        for first in range(0, 27, 9):
+            for tap in range(first, first + 9):
+                out_ref[tap] = make(tap)
+            part = pl.ds(first, 9)
+            copies.append(pltpu.make_async_copy(out_ref.at[part], hbm.at[part], sems.at[len(copies)]))
+            copies[-1].start()
+        for copy in copies:
+            copy.wait()
+
+    def turned_block(tap):
+        wide = jnp.concatenate([block_of(tap), jnp.zeros((32, 128), F32)], axis=0)
+        return wide.T[:CH, :CH]
+
+    core = core_index()
+
+    @pl.when(core == (0 if own else 1))
+    def _():
+        write(one_hbm, turned_block)
+
+    @pl.when(core == (1 if own else 0))
+    def _():
+        write(two_hbm, lambda tap: block_of(26 - tap)[:, :CH])
 
 
 def shape(dims, dtype=BF16):
     return jax.ShapeDtypeStruct(dims, dtype)
 
 
-def call(kernel, outs, *args, scratch=(), specs=None, out_specs=None, limit=8, flops=0, name=None):
+def call(kernel, outs, *args, scratch=(), specs=None, out_specs=None, limit=8, flops=0, aliases=None, name=None):
     specs = specs or {}
     return pl.pallas_call(
         kernel,
@@ -341,6 +365,7 @@
         in_specs=[specs.get(k, VMEM) for k in range(len(args))],
         out_specs=out_specs or jax.tree.map(lambda _: VMEM, outs),
         scratch_shapes=scratch,
+        input_output_aliases=aliases or {},
         compiler_params=pltpu.CompilerParams(vmem_limit_bytes=limit << 20),
         cost_estimate=pl.CostEstimate(flops=flops, bytes_accessed=1 << 20, transcendentals=0),
         name=name,
@@ -373,13 +398,12 @@
 
 
 def swap_z(value, k):
-    return lax.ppermute(value, BOTH, device_pairs(lambda x, y, z, core: (x, y, (z + 2 * k) % 8, core)))
-
-
-def dev_shift(value, step):
-    count = lax.axis_size("dev")
-    pairs = [(i, i + step) for i in range(count) if 0 <= i + step < count]
-    return lax.ppermute(value, "dev", pairs)
+    return lax.ppermute(value, BOTH, device_pairs(lambda x, y, z, core: (x, y, z ^ (2 * k), core)))
+
+
+def dev_swap(value, first):
+    pairs = [(i, i + 1) for i in range(first, lax.axis_size("dev") - 1, 2)]
+    return lax.ppermute(value, "dev", pairs + [(j, i) for i, j in pairs])
 
 
 def in_hbm(value):
@@ -393,16 +417,18 @@
     w1 = in_hbm(kernel_one.reshape(27 * CH, CH))
     w2 = in_hbm(kernel_two.reshape(27 * CH, CH))
     neighbours = in_hbm(neighbours)
-    low, high = call(
+    first, second = call(
         rim_kernel,
         [shape((3 * CH + 32, 128))] * 2,
         features_in, cotangent, occ, neighbours,
         specs={k: HBM for k in range(4)},
-        scratch=INPUTS + [pltpu.SMEM((2, 27), jnp.int32), pltpu.SemaphoreType.DMA((4,))],
+        scratch=INPUTS + [
+            pltpu.SMEM((2, 27), jnp.int32), pltpu.VMEM((2, 3 * CH + 32, 128), BF16), pltpu.SemaphoreType.DMA((4,))
+        ],
         name="rims",
     )
-    upper = dev_shift(low, -1)
-    lower = dev_shift(high, 1)
+    got_first = dev_swap(first, 0)
+    got_second = dev_swap(second, 1)
     v, part, w1t, wb, sel, mask = call(
         prep_kernel,
         [
@@ -422,7 +448,8 @@
     grad, rim = call(
         point_kernel,
         [shape((2, CH, 1024)), shape((2, K9, 256))],
-        part, w1t, wb, sel, mask, lower, upper,
+        part, w1t, wb, sel, mask, got_first, got_second,
+        scratch=[pltpu.VMEM((2, 3 * CH + 32, 128), BF16)],
         limit=16,
         flops=1 << 30,
         name="points",
@@ -444,11 +471,12 @@
     features_out = call(
         out_kernel,
         shape((CH, 1024)),
-        grad, lower, upper, low, high, w1t, sel, w2, mask, in_hbm(value),
-        specs={7: HBM, 9: HBM},
+        grad, got_first, got_second, first, second, w1t, sel, w2, mask, value,
+        specs={7: HBM, 9: ANY},
         scratch=[
             pltpu.VMEM((27 * CH, CH), BF16), pltpu.VMEM((3 * CH, K9), BF16),
             pltpu.VMEM((K9, 1280), BF16), pltpu.VMEM((8, CH, 128), BF16),
+            pltpu.VMEM((2, 3 * CH + 32, 128), BF16), pltpu.VMEM((2, 3 * CH + 32, 128), BF16),
             pltpu.SemaphoreType.DMA((1,)),
         ],
         limit=16,
@@ -466,18 +494,23 @@
         name="sum_z",
     )
     mine = all_to_all(value).reshape(HALF, 128)
-    kernel_one_grad, kernel_two_grad = call(
-        grads_kernel,
-        [shape((27, CH, CH), F32)] * 2,
-        mine, swap_core(mine),
-        out_specs=[HBM, HBM],
-        scratch=[
-            pltpu.VMEM((ROWS, 128), F32), pltpu.VMEM((27, CH, CH), F32), pltpu.VMEM((27, CH, CH), F32),
-            pltpu.SemaphoreType.DMA((6,)),
-        ],
-        limit=16,
-        name="unpack",
-    )
+    other = swap_core(mine)
+    grads = []
+    for own, half in ((True, mine), (False, other)):
+        grads = call(
+            functools.partial(unpack_kernel, own),
+            [shape((27, CH, CH), F32)] * 2,
+            half, *grads,
+            specs={1: HBM, 2: HBM},
+            out_specs=[HBM, HBM],
+            aliases={} if own else {1: 0, 2: 1},
+            scratch=[
+                pltpu.VMEM((HALF, 128), F32), pltpu.VMEM((27, CH, CH), F32), pltpu.SemaphoreType.DMA((3,))
+            ],
+            limit=16,
+            name="unpack_own" if own else "unpack_other",
+        )
+    kernel_one_grad, kernel_two_grad = grads
     return (features_out, kernel_one_grad, kernel_two_grad)
 
 

time: 73.1 us -> 69.9 us (0.956)
  waiting for transfers between devices: 13.8 us -> 11.7 us
  starting transfers between devices: 29.1 us -> 27.6 us
  Pallas kernels: 15.5 us -> 16.4 us
    ppermute x5, starting transfers between devices: 12.6 us -> 8.95 us  [the longest x3 5.74 us: swap_z(): lax.ppermute(value, BOTH, device_pairs(lambda x, y, z, core: (x, y, z ^ 2...]
    all_to_all x1, starting transfers between devices: 10.3 us -> 13.2 us  [all_to_all(): lax.all_to_all(value, BOTH, 0, 0, axis_index_groups=around_groups(), tile...]
    ppermute x2, waiting for transfers between devices: 2.11 us -> 0.76 us  [swap_core(): lax.ppermute(value, BOTH, device_pairs(lambda x, y, z, core: (x, y, z, 1...]
    ppermute x2, starting transfers between devices: 6.3 us -> 5.37 us  [swap_core(): lax.ppermute(value, BOTH, device_pairs(lambda x, y, z, core: (x, y, z, 1...]
    pallas_call x10 -> x11, Pallas kernels: 15.5 us -> 16.4 us  [call(): pl.pallas_call(kernel, out_shape=outs, in_specs=[specs.get(k, VMEM) for k...]
  transfers between devices with their start and end apart: 8 -> 8, of which waited for: 6 -> 4; matrix products, arithmetic and copies ran while one was open for 0% -> 0% of each run, Pallas kernels for 13% -> 15%
where the time goes in v5:
time: 69.9 us; the launch traced here: 69.6 us
  starting transfers between devices  27.6 us (39%)
  Pallas kernels  16.4 us (23%)
  blocking collectives  13.2 us (19%)
  waiting for transfers between devices  11.7 us (17%)
  between operations  0.73 us (1%)
    pallas_call x11, Pallas kernels, call(): pl.pallas_call(kernel, out_shape=outs, in_specs=[specs.get(k, VMEM) for k...  16.4 us
    all_to_all x1, starting transfers between devices, all_to_all(): lax.all_to_all(value, BOTH, 0, 0, axis_index_groups=around_groups(), tile...  13.2 us
    all_to_all x1, blocking collectives, all_to_all(): lax.all_to_all(value, BOTH, 0, 0, axis_index_groups=around_groups(), tile...  13.2 us
    all_to_all x1, waiting for transfers between devices, all_to_all(): lax.all_to_all(value, BOTH, 0, 0, axis_index_groups=around_groups(), tile...  6.62 us
    ppermute x3, starting transfers between devices, swap_z(): lax.ppermute(value, BOTH, device_pairs(lambda x, y, z, core: (x, y, z ^ 2...  5.74 us
    ppermute x2, starting transfers between devices, swap_core(): lax.ppermute(value, BOTH, device_pairs(lambda x, y, z, core: (x, y, z, 1...  5.37 us
    ppermute x3, waiting for transfers between devices, swap_z(): lax.ppermute(value, BOTH, device_pairs(lambda x, y, z, core: (x, y, z ^ 2...  4.35 us
    ppermute x2, starting transfers between devices, dev_swap(): return lax.ppermute(value, 'dev', pairs + [(j, i) for i, j in pairs])  3.21 us
  transfers between devices with their start and end apart: 8, of which 4 were waited for; matrix products, arithmetic and copies ran while one was open for 0% of the time, Pallas kernels for 15%

profile of v5, /device:TPU:1, one launch (start us, length us, event | category | flops | bytes accessed | tf_op | source)
XLA Modules:
  0.0 69.6 jit_solution(1892187047409886134)
XLA Ops:
  0.6 1.2 %rims.1 = (bf16[320,128]{1,0:T(8,128)(2,1)S(1)}, bf16[320,128]{1,0:T(8,128)(2,1)S(1)}) custom-call(bf16[96,1024]{1,0:T(8,128)(2,1)} %feat_hbm.3, bf16[96,1024]{1,0:T(8,128)(2,1)} %cot_hbm.3, s32[1,1024]{1,0:T(1,128)} %bitcast.7, s32[2,27]{1,0:T(2,128)} %nb_hbm.3), custom_call_target="tpu_custom_call" | custom-call | bytes 1048576 | tf_op jit(solution)/shard_map/rims/pallas_call | solution.py:362
  1.9 2.6 %collective-permute-start = (bf16[320,128]{1,0:T(8,128)(2,1)S(1)}, bf16[320,128]{1,0:T(8,128)(2,1)S(1)}, u32[]{:S(2)}, u32[]{:S(2)}) collective-permute-start(bf16[320,128]{1,0:T(8,128)(2,1)S(1)} %get-tuple-element.22.first_ref), channel_id=1, source_target_pairs={{0,1},{2,3},{4,5},{6,7},{8,9},{10,11},{12,13},{14,15},{16,17},{18,... | collective-permute-start | bytes 245768 | tf_op jit(solution)/shard_map/ppermute | solution.py:406
  4.4 0.7 collective-permute-start.1
  5.1 3.7 %prep.1 = (bf16[2,864,1024]{2,1,0:T(8,128)(2,1)S(1)}, f32[2,96,1024]{2,1,0:T(8,128)S(1)}, bf16[288,864]{1,0:T(8,128)(2,1)S(1)}, bf16[288,864]{1,0:T(8,128)(2,1)S...) custom-call(bf16[96,1024]{1,0:T(8,128)(2,1)} %feat_hbm.3, bf16[96,1024]{1,0:T(8,128)(2,1)} %cot_hbm.3, ...), custom_call_target="tpu_custom_call" | custom-call | flops 4294967296 | bytes 1048576 | tf_op jit(solution)/shard_map/prep/pallas_call | solution.py:362
  8.8 0.0 collective-permute-done.first_ref.got_first_ref
  8.8 0.0 collective-permute-done.1.second_ref.got_second_ref
  8.8 0.7 %points.1 = (bf16[2,96,1024]{2,1,0:T(8,128)(2,1)S(1)}, bf16[2,864,256]{2,1,0:T(8,128)(2,1)S(1)}) custom-call(f32[2,96,1024]{2,1,0:T(8,128)S(1)} %get-tuple-element.17.part_ref, bf16[288,864]{1,0:T(8,128)(2,1)S(1)} %get-tuple-element.18.w1t_ref, bf16[288,864]{1,0:T(8,128)(2,1)S(1)} %get-tuple-element.19.wb_ref, ...), custom_call_target="tpu_custom_call" | custom-call | flops 1073741824 | bytes 1048576 | tf_op jit(solution)/shard_map/points/pallas_call | solution.py:362
  9.5 1.0 %terms_sent.1 = bf16[2048,128]{1,0:T(8,128)(2,1)S(1)} custom-call(bf16[2,864,1024]{2,1,0:T(8,128)(2,1)S(1)} %get-tuple-element.25.v_ref, bf16[2,864,256]{2,1,0:T(8,128)(2,1)S(1)} %get-tuple-element.26.rim_ref, bf16[2,96,1024]{2,1,0:T(8,128)(2,1)S(1)} %get-tuple-element.24.grad_ref), custom_call_target="tpu_custom_call" | custom-call | flops 2147483648 | bytes 1048576 | tf_op jit(solution)/shard_map/terms_sent/pallas_call | solution.py:362
  10.5 1.1 %collective-permute-start.2 = (bf16[2048,128]{1,0:T(8,128)(2,1)S(1)}, bf16[2048,128]{1,0:T(8,128)(2,1)S(1)}, u32[]{:S(2)}, u32[]{:S(2)}) collective-permute-start(bf16[2048,128]{1,0:T(8,128)(2,1)S(1)} %terms_sent.1), channel_id=1, source_target_pairs={{0,32},{1,33},{2,34},{3,35},{4,36},{5,37},{6,38},{7,39},{8,40},{9,... | collective-permute-start | bytes 1572872 | tf_op jit(solution)/shard_map/ppermute | solution.py:397
  11.5 1.0 %terms_kept.1.own_ref = f32[2048,128]{1,0:T(8,128)S(1)} custom-call(bf16[2,864,1024]{2,1,0:T(8,128)(2,1)S(1)} %get-tuple-element.25.v_ref, bf16[2,864,256]{2,1,0:T(8,128)(2,1)S(1)} %get-tuple-element.26.rim_ref, bf16[2,96,1024]{2,1,0:T(8,128)(2,1)S(1)} %get-tuple-element.24.grad_ref), custom_call_target="tpu_custom_call" | custom-call | flops 2147483648 | bytes 1048576 | tf_op jit(solution)/shard_map/terms_kept/pallas_call | solution.py:362
  12.5 0.6 collective-permute-done.2.got_ref
  13.1 0.9 %sum_core.1.after_ref = bf16[2048,128]{1,0:T(8,128)(2,1)} custom-call(f32[2048,128]{1,0:T(8,128)S(1)} %terms_kept.1.own_ref, bf16[2048,128]{1,0:T(8,128)(2,1)S(1)} %collective-permute-done.2.got_ref), custom_call_target="tpu_custom_call" | custom-call | bytes 1048576 | tf_op jit(solution)/shard_map/sum_core/pallas_call | solution.py:362
  14.0 13.2 %all-to-all-start = ((bf16[32,64,128]{2,1,0:T(8,128)(2,1)}), bf16[32,64,128]{2,1,0:T(8,128)(2,1)S(1)}, u32[]{:S(2)}, u32[]{:S(2)}) async-start(bf16[32,64,128]{2,1,0:T(8,128)(2,1)} %bitcast.3), calls=%async_computation | async-start | bytes 1048576 | tf_op jit(solution)/shard_map/all_to_all | solution.py:393
  27.2 4.8 %features.1.after_ref = bf16[96,1024]{1,0:T(8,128)(2,1)} custom-call(bf16[2,96,1024]{2,1,0:T(8,128)(2,1)S(1)} %get-tuple-element.24.grad_ref, bf16[320,128]{1,0:T(8,128)(2,1)S(1)} %collective-permute-done.first_ref.got_first_ref, bf16[320,128]{1,0:T(8,128)(2,1)S(1)} %collective-permute-done.1.second_ref.got_second_ref, ...), custom_call_target="tpu_custom_call" | custom-call | flops 3221225472 | bytes 1048576 | tf_op jit(solution)/shard_map/features/pallas_call | solution.py:362
  32.0 6.6 %all-to-all-done.got_ref = bf16[32,64,128]{2,1,0:T(8,128)(2,1)S(1)} async-done(((bf16[32,64,128]{2,1,0:T(8,128)(2,1)}), bf16[32,64,128]{2,1,0:T(8,128)(2,1)S(1)}, u32[]{:S(2)}, u32[]{:S(2)}) %all-to-all-start) | async-done | bytes 524320 | tf_op jit(solution)/shard_map/all_to_all | solution.py:393
  38.6 0.1 sum_around.1.refs_0_
  38.7 3.5 %collective-permute-start.5 = (bf16[64,128]{1,0:T(8,128)(2,1)S(1)}, bf16[64,128]{1,0:T(8,128)(2,1)S(1)}, u32[]{:S(2)}, u32[]{:S(2)}) collective-permute-start(bf16[64,128]{1,0:T(8,128)(2,1)S(1)} %sum_around.1.refs_0_), channel_id=1, source_target_pairs={{0,6},{1,7},{2,4},{3,5},{4,2},{5,3},{6,0},{7,1},{8,14},{9,15},{10,... | collective-permute-start | bytes 49160 | tf_op jit(solution)/shard_map/ppermute | solution.py:401
  42.2 1.5 %collective-permute-start.4 = (bf16[64,128]{1,0:T(8,128)(2,1)S(1)}, bf16[64,128]{1,0:T(8,128)(2,1)S(1)}, u32[]{:S(2)}, u32[]{:S(2)}) collective-permute-start(bf16[64,128]{1,0:T(8,128)(2,1)S(1)} %sum_around.1.refs_0_), channel_id=1, source_target_pairs={{0,4},{1,5},{2,6},{3,7},{4,0},{5,1},{6,2},{7,3},{8,12},{9,13},{10,... | collective-permute-start | bytes 49160 | tf_op jit(solution)/shard_map/ppermute | solution.py:401
  43.7 0.7 %collective-permute-start.3 = (bf16[64,128]{1,0:T(8,128)(2,1)S(1)}, bf16[64,128]{1,0:T(8,128)(2,1)S(1)}, u32[]{:S(2)}, u32[]{:S(2)}) collective-permute-start(bf16[64,128]{1,0:T(8,128)(2,1)S(1)} %sum_around.1.refs_0_), channel_id=1, source_target_pairs={{0,2},{1,3},{2,0},{3,1},{4,6},{5,7},{6,4},{7,5},{8,10},{9,11},{10,... | collective-permute-start | bytes 49160 | tf_op jit(solution)/shard_map/ppermute | solution.py:401
  44.4 0.0 collective-permute-done.5.refs_3_
  44.4 4.3 %collective-permute-done.4.refs_2_ = bf16[64,128]{1,0:T(8,128)(2,1)S(1)} collective-permute-done((bf16[64,128]{1,0:T(8,128)(2,1)S(1)}, bf16[64,128]{1,0:T(8,128)(2,1)S(1)}, u32[]{:S(2)}, u32[]{:S(2)}) %collective-permute-start.4) | collective-permute-done | bytes 16416 | tf_op jit(solution)/shard_map/ppermute | solution.py:401
  48.8 0.0 collective-permute-done.3.refs_1_
  48.8 0.1 sum_z.1
  48.8 13.2 %all_to_all.10 = bf16[32,64,128]{2,1,0:T(8,128)(2,1)S(1)} all-to-all(bf16[32,64,128]{2,1,0:T(8,128)(2,1)S(1)} %sum_z.1), channel_id=1, replica_groups={{0,1,8,9,16,17,24,25,64,65,72,73,80,81,88,89,128,129,136,137,144,145,15..., dimensions={0} | all-to-all | bytes 1048576 | tf_op jit(solution)/shard_map/all_to_all | solution.py:393
  62.0 4.3 %collective-permute-start.6 = (bf16[2048,128]{1,0:T(8,128)(2,1)S(1)}, bf16[2048,128]{1,0:T(8,128)(2,1)S(1)}, u32[]{:S(2)}, u32[]{:S(2)}) collective-permute-start(bf16[2048,128]{1,0:T(8,128)(2,1)S(1)} %bitcast.5), channel_id=1, source_target_pairs={{0,32},{1,33},{2,34},{3,35},{4,36},{5,37},{6,38},{7,39},{8,40},{9,... | collective-permute-start | bytes 1572872 | tf_op jit(solution)/shard_map/ppermute | solution.py:397
  66.3 1.3 %unpack_own.1 = (f32[27,96,96]{2,1,0:T(8,128)}, f32[27,96,96]{2,1,0:T(8,128)}) custom-call(bf16[2048,128]{1,0:T(8,128)(2,1)S(1)} %bitcast.6), custom_call_target="tpu_custom_call" | custom-call | bytes 1048576 | tf_op jit(solution)/shard_map/unpack_own/pallas_call | solution.py:362
  67.7 0.2 collective-permute-done.6.refs_0_
  67.9 1.7 %unpack_other.1 = (f32[27,96,96]{2,1,0:T(8,128)}, f32[27,96,96]{2,1,0:T(8,128)}) custom-call(bf16[2048,128]{1,0:T(8,128)(2,1)S(1)} %collective-permute-done.6.refs_0_, f32[27,96,96]{2,1,0:T(8,128)} %get-tuple-element.27.refs_1_, f32[27,96,96]{2,1,0:T(8,128)} %get-tuple-element.28.refs_2_), custom_call_target="tpu_custom_call", output_to_operand_aliasing={{0}: (1, {}), {1}: (2, {})} | custom-call | bytes 1048576 | tf_op jit(solution)/shard_map/unpack_other/pallas_call | solution.py:362
Async XLA Ops:
  1.9 6.9 %collective-permute-start = (bf16[320,128]{1,0:T(8,128)(2,1)S(1)}, bf16[320,128]{1,0:T(8,128)(2,1)S(1)}, u32[]{:S(2)}, u32[]{:S(2)}) collective-permute-start(bf16[320,128]{1,0:T(8,128)(2,1)S(1)} %get-tuple-element.22.first_ref), channel_id=1, source_target_pairs={{0,1},{2,3},{4,5},{6,7},{8,9},{10,11},{12,13},{14,15},{16,17},{18,... | collective-permute-start | bytes 245768 | tf_op jit(solution)/shard_map/ppermute | solution.py:406
  4.4 4.4 %collective-permute-start.1 = (bf16[320,128]{1,0:T(8,128)(2,1)S(1)}, bf16[320,128]{1,0:T(8,128)(2,1)S(1)}, u32[]{:S(2)}, u32[]{:S(2)}) collective-permute-start(bf16[320,128]{1,0:T(8,128)(2,1)S(1)} %get-tuple-element.23.second_ref), channel_id=1, source_target_pairs={{1,2},{3,4},{5,6},{7,8},{9,10},{11,12},{13,14},{15,16},{17,18},{19... | collective-permute-start | bytes 245768 | tf_op jit(solution)/shard_map/ppermute | solution.py:406
  10.5 2.6 %collective-permute-start.2 = (bf16[2048,128]{1,0:T(8,128)(2,1)S(1)}, bf16[2048,128]{1,0:T(8,128)(2,1)S(1)}, u32[]{:S(2)}, u32[]{:S(2)}) collective-permute-start(bf16[2048,128]{1,0:T(8,128)(2,1)S(1)} %terms_sent.1), channel_id=1, source_target_pairs={{0,32},{1,33},{2,34},{3,35},{4,36},{5,37},{6,38},{7,39},{8,40},{9,... | collective-permute-start | bytes 1572872 | tf_op jit(solution)/shard_map/ppermute | solution.py:397
  14.0 24.6 %all-to-all-start = ((bf16[32,64,128]{2,1,0:T(8,128)(2,1)}), bf16[32,64,128]{2,1,0:T(8,128)(2,1)S(1)}, u32[]{:S(2)}, u32[]{:S(2)}) async-start(bf16[32,64,128]{2,1,0:T(8,128)(2,1)} %bitcast.3), calls=%async_computation | async-start | bytes 1048576 | tf_op jit(solution)/shard_map/all_to_all | solution.py:393
  38.7 5.7 %collective-permute-start.5 = (bf16[64,128]{1,0:T(8,128)(2,1)S(1)}, bf16[64,128]{1,0:T(8,128)(2,1)S(1)}, u32[]{:S(2)}, u32[]{:S(2)}) collective-permute-start(bf16[64,128]{1,0:T(8,128)(2,1)S(1)} %sum_around.1.refs_0_), channel_id=1, source_target_pairs={{0,6},{1,7},{2,4},{3,5},{4,2},{5,3},{6,0},{7,1},{8,14},{9,15},{10,... | collective-permute-start | bytes 49160 | tf_op jit(solution)/shard_map/ppermute | solution.py:401
  42.2 6.6 %collective-permute-start.4 = (bf16[64,128]{1,0:T(8,128)(2,1)S(1)}, bf16[64,128]{1,0:T(8,128)(2,1)S(1)}, u32[]{:S(2)}, u32[]{:S(2)}) collective-permute-start(bf16[64,128]{1,0:T(8,128)(2,1)S(1)} %sum_around.1.refs_0_), channel_id=1, source_target_pairs={{0,4},{1,5},{2,6},{3,7},{4,0},{5,1},{6,2},{7,3},{8,12},{9,13},{10,... | collective-permute-start | bytes 49160 | tf_op jit(solution)/shard_map/ppermute | solution.py:401
  43.7 5.1 %collective-permute-start.3 = (bf16[64,128]{1,0:T(8,128)(2,1)S(1)}, bf16[64,128]{1,0:T(8,128)(2,1)S(1)}, u32[]{:S(2)}, u32[]{:S(2)}) collective-permute-start(bf16[64,128]{1,0:T(8,128)(2,1)S(1)} %sum_around.1.refs_0_), channel_id=1, source_target_pairs={{0,2},{1,3},{2,0},{3,1},{4,6},{5,7},{6,4},{7,5},{8,10},{9,11},{10,... | collective-permute-start | bytes 49160 | tf_op jit(solution)/shard_map/ppermute | solution.py:401
  62.0 5.9 %collective-permute-start.6 = (bf16[2048,128]{1,0:T(8,128)(2,1)S(1)}, bf16[2048,128]{1,0:T(8,128)(2,1)S(1)}, u32[]{:S(2)}, u32[]{:S(2)}) collective-permute-start(bf16[2048,128]{1,0:T(8,128)(2,1)S(1)} %bitcast.5), channel_id=1, source_target_pairs={{0,32},{1,33},{2,34},{3,35},{4,36},{5,37},{6,38},{7,39},{8,40},{9,... | collective-permute-start | bytes 1572872 | tf_op jit(solution)/shard_map/ppermute | solution.py:397

commit v6 on v5

--- a/solution.py
+++ b/solution.py
@@ -189,7 +189,10 @@
     ]
 
 
-def point_kernel(part_ref, w1t_ref, wb_ref, sel_ref, mask_ref, first_ref, second_ref, grad_ref, rim_ref, both_ref):
+def point_kernel(
+    part_ref, w1t_ref, wb_ref, sel_ref, mask_ref, v_ref, first_ref, second_ref,
+    sent_ref, grad_ref, rim_ref, both_ref,
+):
     low_ref, high_ref = lower_upper(first_ref, second_ref, both_ref)
     lows = spread_rim(low_ref[: 2 * CH, :], sel_ref[0])
     highs = spread_rim(high_ref[: 2 * CH, :], sel_ref[2])
@@ -207,13 +210,13 @@
     grad_ref[1] = (z * sigma).astype(BF16)
     ga = finish(1, wb_ref)
     grad_ref[0] = (ga * sigma * (1.0 + z * (1.0 - sigma))).astype(BF16)
-
-
-def term_kernel(kept, v_ref, rim_ref, grad_ref, out_ref):
-    which = core_index() if kept else 1 - core_index()
-    grad = grad_ref[which]
+    which = 1 - core_index()
+    write_terms(grad_ref[which], v_ref[which], rim_ref[which], sent_ref)
+
+
+def write_terms(grad, inner, rims, out_ref):
     gap = jnp.zeros((CH, 128), BF16)
-    inner = jnp.concatenate(
+    middle = jnp.concatenate(
         [
             jnp.concatenate([grad[:, 128:], gap], axis=1),
             grad,
@@ -229,11 +232,16 @@
         ],
         axis=0,
     )
-    value = (dot(inner, v_ref[which], NT) + dot(sides, rim_ref[which], NT)) * (262144.0 ** -0.5)
+    value = (dot(middle, inner, NT) + dot(sides, rims, NT)) * (262144.0 ** -0.5)
     value = jnp.concatenate([value, jnp.zeros((3 * CH, 32), F32)], axis=1).astype(out_ref.dtype)
     for k in range(7):
         out_ref[k * 3 * CH : (k + 1) * 3 * CH, :] = value[:, k * 128 : (k + 1) * 128]
     out_ref[21 * CH :, :] = jnp.zeros((HALF - 21 * CH, 128), out_ref.dtype)
+
+
+def kept_kernel(v_ref, rim_ref, grad_ref, out_ref):
+    which = core_index()
+    write_terms(grad_ref[which], v_ref[which], rim_ref[which], out_ref)
 
 
 def beside(payload_ref, own, below, w1t_ref):
@@ -284,8 +292,15 @@
     return lax.rem(lax.axis_index("group"), 2)
 
 
-def add_kernel(own_ref, got_ref, out_ref):
-    out_ref[...] = (own_ref[...] + got_ref[...].astype(F32)).astype(BF16)
+def add_kernel(own_ref, got_ref, out_hbm, sum_ref, sems):
+    copies = []
+    for k in range(4):
+        part = pl.ds(k * HALF // 4, HALF // 4)
+        sum_ref[part, :] = (own_ref[part, :] + got_ref[part, :].astype(F32)).astype(BF16)
+        copies.append(pltpu.make_async_copy(sum_ref.at[part], out_hbm.at[part], sems.at[k]))
+        copies[-1].start()
+    for copy in copies:
+        copy.wait()
 
 
 def rows_kernel(got_ref, after_ref, out_ref):
@@ -310,22 +325,19 @@
 
 def unpack_kernel(own, *refs):
     half_ref = refs[0]
-    one_hbm, two_hbm, packed_ref, out_ref, sems = refs[-5:]
-    packed_ref[...] = half_ref[...].astype(F32)
+    one_hbm, two_hbm, out_ref, sems = refs[-4:]
     lane = lax.broadcasted_iota(jnp.int32, (CH, 128), 1)
 
     def block_of(block):
         d, j = block // 9, block % 9
         at, off = j * CH // 128, j * CH % 128
         row = at * 3 * CH + d * CH
-        value = packed_ref[row : row + CH, :]
-        if off == 0:
-            return value
-        value = pltpu.roll(value, 128 - off, 1)
+        value = half_ref[row : row + CH, :]
         if off > 32:
-            more = pltpu.roll(packed_ref[row + 3 * CH : row + 4 * CH, :], 128 - off, 1)
-            value = jnp.where(lane < 128 - off, value, more)
-        return value
+            value = jnp.where(lane < off, half_ref[row + 3 * CH : row + 4 * CH, :], value)
+        if off > 0:
+            value = pltpu.roll(value, 128 - off, 1)
+        return value.astype(F32)
 
     def write(hbm, make):
         copies = []
@@ -445,28 +457,23 @@
         flops=4 << 30,
         name="prep",
     )
-    grad, rim = call(
+    sent, grad, rim = call(
         point_kernel,
-        [shape((2, CH, 1024)), shape((2, K9, 256))],
-        part, w1t, wb, sel, mask, got_first, got_second,
+        [shape((HALF, 128)), shape((2, CH, 1024)), shape((2, K9, 256))],
+        part, w1t, wb, sel, mask, v, got_first, got_second,
         scratch=[pltpu.VMEM((2, 3 * CH + 32, 128), BF16)],
         limit=16,
-        flops=1 << 30,
+        flops=2 << 30,
         name="points",
     )
-
-    def terms(kept):
-        return call(
-            functools.partial(term_kernel, kept),
-            shape((HALF, 128), F32 if kept else BF16),
-            v, rim, grad,
-            limit=16,
-            flops=2 << 30,
-            name="terms_kept" if kept else "terms_sent",
-        )
-
-    got = swap_core(terms(False))
-    value = call(add_kernel, shape((HALF, 128)), terms(True), got, name="sum_core")
+    got = swap_core(sent)
+    kept = call(kept_kernel, shape((HALF, 128), F32), v, rim, grad, limit=16, flops=2 << 30, name="terms_kept")
+    value = call(
+        add_kernel, shape((HALF, 128)), kept, got,
+        out_specs=HBM,
+        scratch=[pltpu.VMEM((HALF, 128), BF16), pltpu.SemaphoreType.DMA((4,))],
+        name="sum_core",
+    )
     moved = all_to_all(value.reshape(AROUND, HALF // AROUND, 128))
     features_out = call(
         out_kernel,
@@ -504,9 +511,7 @@
             specs={1: HBM, 2: HBM},
             out_specs=[HBM, HBM],
             aliases={} if own else {1: 0, 2: 1},
-            scratch=[
-                pltpu.VMEM((HALF, 128), F32), pltpu.VMEM((27, CH, CH), F32), pltpu.SemaphoreType.DMA((3,))
-            ],
+            scratch=[pltpu.VMEM((27, CH, CH), F32), pltpu.SemaphoreType.DMA((3,))],
             limit=16,
             name="unpack_own" if own else "unpack_other",
         )

time: 69.9 us -> 69.3 us (level)
  Pallas kernels: 16.4 us -> 15.7 us
    pallas_call x11 -> x10, Pallas kernels: 16.4 us -> 15.7 us  [call(): pl.pallas_call(kernel, out_shape=outs, in_specs=[specs.get(k, VMEM) for k...]
where the time goes in v6:
time: 69.3 us; the launch traced here: 69 us
  starting transfers between devices  27.6 us (40%)
  Pallas kernels  15.7 us (23%)
  blocking collectives  13.2 us (19%)
  waiting for transfers between devices  11.9 us (17%)
  between operations  0.73 us (1%)
    pallas_call x10, Pallas kernels, call(): pl.pallas_call(kernel, out_shape=outs, in_specs=[specs.get(k, VMEM) for k...  15.7 us
    all_to_all x1, starting transfers between devices, all_to_all(): lax.all_to_all(value, BOTH, 0, 0, axis_index_groups=around_groups(), tile...  13.2 us
    all_to_all x1, blocking collectives, all_to_all(): lax.all_to_all(value, BOTH, 0, 0, axis_index_groups=around_groups(), tile...  13.2 us
    all_to_all x1, waiting for transfers between devices, all_to_all(): lax.all_to_all(value, BOTH, 0, 0, axis_index_groups=around_groups(), tile...  6.62 us
    ppermute x3, starting transfers between devices, swap_z(): lax.ppermute(value, BOTH, device_pairs(lambda x, y, z, core: (x, y, z ^ 2...  5.74 us
    ppermute x2, starting transfers between devices, swap_core(): lax.ppermute(value, BOTH, device_pairs(lambda x, y, z, core: (x, y, z, 1...  5.37 us
    ppermute x3, waiting for transfers between devices, swap_z(): lax.ppermute(value, BOTH, device_pairs(lambda x, y, z, core: (x, y, z ^ 2...  4.32 us
    ppermute x2, starting transfers between devices, dev_swap(): return lax.ppermute(value, 'dev', pairs + [(j, i) for i, j in pairs])  3.21 us
  transfers between devices with their start and end apart: 8, of which 4 were waited for; matrix products, arithmetic and copies ran while one was open for 0% of the time, Pallas kernels for 15%

profile of v6, /device:TPU:1, one launch (start us, length us, event | category | flops | bytes accessed | tf_op | source)
XLA Modules:
  0.0 69.0 jit_solution(16904572003495288973)
XLA Ops:
  0.6 1.2 %rims.1 = (bf16[320,128]{1,0:T(8,128)(2,1)S(1)}, bf16[320,128]{1,0:T(8,128)(2,1)S(1)}) custom-call(bf16[96,1024]{1,0:T(8,128)(2,1)} %feat_hbm.3, bf16[96,1024]{1,0:T(8,128)(2,1)} %cot_hbm.3, s32[1,1024]{1,0:T(1,128)} %bitcast.7, s32[2,27]{1,0:T(2,128)} %nb_hbm.3), custom_call_target="tpu_custom_call" | custom-call | bytes 1048576 | tf_op jit(solution)/shard_map/rims/pallas_call | solution.py:374
  1.9 2.6 %collective-permute-start = (bf16[320,128]{1,0:T(8,128)(2,1)S(1)}, bf16[320,128]{1,0:T(8,128)(2,1)S(1)}, u32[]{:S(2)}, u32[]{:S(2)}) collective-permute-start(bf16[320,128]{1,0:T(8,128)(2,1)S(1)} %get-tuple-element.24.first_ref), channel_id=1, source_target_pairs={{0,1},{2,3},{4,5},{6,7},{8,9},{10,11},{12,13},{14,15},{16,17},{18,... | collective-permute-start | bytes 245768 | tf_op jit(solution)/shard_map/ppermute | solution.py:418
  4.4 0.7 collective-permute-start.1
  5.1 3.7 %prep.1 = (bf16[2,864,1024]{2,1,0:T(8,128)(2,1)S(1)}, f32[2,96,1024]{2,1,0:T(8,128)S(1)}, bf16[288,864]{1,0:T(8,128)(2,1)S(1)}, bf16[288,864]{1,0:T(8,128)(2,1)S...) custom-call(bf16[96,1024]{1,0:T(8,128)(2,1)} %feat_hbm.3, bf16[96,1024]{1,0:T(8,128)(2,1)} %cot_hbm.3, ...), custom_call_target="tpu_custom_call" | custom-call | flops 4294967296 | bytes 1048576 | tf_op jit(solution)/shard_map/prep/pallas_call | solution.py:374
  8.8 0.0 collective-permute-done.first_ref.got_first_ref
  8.8 0.0 collective-permute-done.1.second_ref.got_second_ref
  8.8 1.5 %points.1 = (bf16[2048,128]{1,0:T(8,128)(2,1)S(1)}, bf16[2,96,1024]{2,1,0:T(8,128)(2,1)S(1)}, bf16[2,864,256]{2,1,0:T(8,128)(2,1)S(1)}) custom-call(f32[2,96,1024]{2,1,0:T(8,128)S(1)} %get-tuple-element.18.part_ref, bf16[288,864]{1,0:T(8,128)(2,1)S(1)} %get-tuple-element.19.w1t_ref, bf16[288,864]{1,0:T(8,128)(2,1)S(1)} %get-tuple-element.20.wb_ref, ...), custom_call_target="tpu_custom_call" | custom-call | flops 2147483648 | bytes 1048576 | tf_op jit(solution)/shard_map/points/pallas_call | solution.py:374
  10.3 1.1 %collective-permute-start.2 = (bf16[2048,128]{1,0:T(8,128)(2,1)S(1)}, bf16[2048,128]{1,0:T(8,128)(2,1)S(1)}, u32[]{:S(2)}, u32[]{:S(2)}) collective-permute-start(bf16[2048,128]{1,0:T(8,128)(2,1)S(1)} %get-tuple-element.28), channel_id=1, source_target_pairs={{0,32},{1,33},{2,34},{3,35},{4,36},{5,37},{6,38},{7,39},{8,40},{9,... | collective-permute-start | bytes 1572872 | tf_op jit(solution)/shard_map/ppermute | solution.py:409
  11.4 1.0 %terms_kept.1.own_ref = f32[2048,128]{1,0:T(8,128)S(1)} custom-call(bf16[2,864,1024]{2,1,0:T(8,128)(2,1)S(1)} %get-tuple-element.23.v_ref, bf16[2,864,256]{2,1,0:T(8,128)(2,1)S(1)} %get-tuple-element.27.rim_ref, bf16[2,96,1024]{2,1,0:T(8,128)(2,1)S(1)} %get-tuple-element.26.grad_ref), custom_call_target="tpu_custom_call" | custom-call | flops 2147483648 | bytes 1048576 | tf_op jit(solution)/shard_map/terms_kept/pallas_call | solution.py:374
  12.3 0.6 collective-permute-done.2.got_ref
  12.9 0.8 %sum_core.1.after_ref = bf16[2048,128]{1,0:T(8,128)(2,1)} custom-call(f32[2048,128]{1,0:T(8,128)S(1)} %terms_kept.1.own_ref, bf16[2048,128]{1,0:T(8,128)(2,1)S(1)} %collective-permute-done.2.got_ref), custom_call_target="tpu_custom_call" | custom-call | bytes 1048576 | tf_op jit(solution)/shard_map/sum_core/pallas_call | solution.py:374
  13.8 13.2 %all-to-all-start = ((bf16[32,64,128]{2,1,0:T(8,128)(2,1)}), bf16[32,64,128]{2,1,0:T(8,128)(2,1)S(1)}, u32[]{:S(2)}, u32[]{:S(2)}) async-start(bf16[32,64,128]{2,1,0:T(8,128)(2,1)} %bitcast.3), calls=%async_computation | async-start | bytes 1048576 | tf_op jit(solution)/shard_map/all_to_all | solution.py:405
  27.0 4.8 %features.1.after_ref = bf16[96,1024]{1,0:T(8,128)(2,1)} custom-call(bf16[2,96,1024]{2,1,0:T(8,128)(2,1)S(1)} %get-tuple-element.26.grad_ref, bf16[320,128]{1,0:T(8,128)(2,1)S(1)} %collective-permute-done.first_ref.got_first_ref, bf16[320,128]{1,0:T(8,128)(2,1)S(1)} %collective-permute-done.1.second_ref.got_second_ref, ...), custom_call_target="tpu_custom_call" | custom-call | flops 3221225472 | bytes 1048576 | tf_op jit(solution)/shard_map/features/pallas_call | solution.py:374
  31.8 6.6 %all-to-all-done.got_ref = bf16[32,64,128]{2,1,0:T(8,128)(2,1)S(1)} async-done(((bf16[32,64,128]{2,1,0:T(8,128)(2,1)}), bf16[32,64,128]{2,1,0:T(8,128)(2,1)S(1)}, u32[]{:S(2)}, u32[]{:S(2)}) %all-to-all-start) | async-done | bytes 524320 | tf_op jit(solution)/shard_map/all_to_all | solution.py:405
  38.4 0.1 sum_around.1.refs_0_
  38.5 3.5 %collective-permute-start.5 = (bf16[64,128]{1,0:T(8,128)(2,1)S(1)}, bf16[64,128]{1,0:T(8,128)(2,1)S(1)}, u32[]{:S(2)}, u32[]{:S(2)}) collective-permute-start(bf16[64,128]{1,0:T(8,128)(2,1)S(1)} %sum_around.1.refs_0_), channel_id=1, source_target_pairs={{0,6},{1,7},{2,4},{3,5},{4,2},{5,3},{6,0},{7,1},{8,14},{9,15},{10,... | collective-permute-start | bytes 49160 | tf_op jit(solution)/shard_map/ppermute | solution.py:413
  42.0 1.5 %collective-permute-start.4 = (bf16[64,128]{1,0:T(8,128)(2,1)S(1)}, bf16[64,128]{1,0:T(8,128)(2,1)S(1)}, u32[]{:S(2)}, u32[]{:S(2)}) collective-permute-start(bf16[64,128]{1,0:T(8,128)(2,1)S(1)} %sum_around.1.refs_0_), channel_id=1, source_target_pairs={{0,4},{1,5},{2,6},{3,7},{4,0},{5,1},{6,2},{7,3},{8,12},{9,13},{10,... | collective-permute-start | bytes 49160 | tf_op jit(solution)/shard_map/ppermute | solution.py:413
  43.5 0.7 %collective-permute-start.3 = (bf16[64,128]{1,0:T(8,128)(2,1)S(1)}, bf16[64,128]{1,0:T(8,128)(2,1)S(1)}, u32[]{:S(2)}, u32[]{:S(2)}) collective-permute-start(bf16[64,128]{1,0:T(8,128)(2,1)S(1)} %sum_around.1.refs_0_), channel_id=1, source_target_pairs={{0,2},{1,3},{2,0},{3,1},{4,6},{5,7},{6,4},{7,5},{8,10},{9,11},{10,... | collective-permute-start | bytes 49160 | tf_op jit(solution)/shard_map/ppermute | solution.py:413
  44.2 0.0 collective-permute-done.5.refs_3_
  44.2 4.3 %collective-permute-done.4.refs_2_ = bf16[64,128]{1,0:T(8,128)(2,1)S(1)} collective-permute-done((bf16[64,128]{1,0:T(8,128)(2,1)S(1)}, bf16[64,128]{1,0:T(8,128)(2,1)S(1)}, u32[]{:S(2)}, u32[]{:S(2)}) %collective-permute-start.4) | collective-permute-done | bytes 16416 | tf_op jit(solution)/shard_map/ppermute | solution.py:413
  48.6 0.0 collective-permute-done.3.refs_1_
  48.6 0.1 sum_z.1
  48.6 13.2 %all_to_all.10 = bf16[32,64,128]{2,1,0:T(8,128)(2,1)S(1)} all-to-all(bf16[32,64,128]{2,1,0:T(8,128)(2,1)S(1)} %sum_z.1), channel_id=1, replica_groups={{0,1,8,9,16,17,24,25,64,65,72,73,80,81,88,89,128,129,136,137,144,145,15..., dimensions={0} | all-to-all | bytes 1048576 | tf_op jit(solution)/shard_map/all_to_all | solution.py:405
  61.8 4.3 %collective-permute-start.6 = (bf16[2048,128]{1,0:T(8,128)(2,1)S(1)}, bf16[2048,128]{1,0:T(8,128)(2,1)S(1)}, u32[]{:S(2)}, u32[]{:S(2)}) collective-permute-start(bf16[2048,128]{1,0:T(8,128)(2,1)S(1)} %bitcast.5), channel_id=1, source_target_pairs={{0,32},{1,33},{2,34},{3,35},{4,36},{5,37},{6,38},{7,39},{8,40},{9,... | collective-permute-start | bytes 1572872 | tf_op jit(solution)/shard_map/ppermute | solution.py:409
  66.1 1.2 %unpack_own.1 = (f32[27,96,96]{2,1,0:T(8,128)}, f32[27,96,96]{2,1,0:T(8,128)}) custom-call(bf16[2048,128]{1,0:T(8,128)(2,1)S(1)} %bitcast.6), custom_call_target="tpu_custom_call" | custom-call | bytes 1048576 | tf_op jit(solution)/shard_map/unpack_own/pallas_call | solution.py:374
  67.3 0.3 collective-permute-done.6.refs_0_
  67.7 1.4 %unpack_other.1 = (f32[27,96,96]{2,1,0:T(8,128)}, f32[27,96,96]{2,1,0:T(8,128)}) custom-call(bf16[2048,128]{1,0:T(8,128)(2,1)S(1)} %collective-permute-done.6.refs_0_, f32[27,96,96]{2,1,0:T(8,128)} %get-tuple-element.29.refs_1_, f32[27,96,96]{2,1,0:T(8,128)} %get-tuple-element.30.refs_2_), custom_call_target="tpu_custom_call", output_to_operand_aliasing={{0}: (1, {}), {1}: (2, {})} | custom-call | bytes 1048576 | tf_op jit(solution)/shard_map/unpack_other/pallas_call | solution.py:374
Async XLA Ops:
  1.9 6.9 %collective-permute-start = (bf16[320,128]{1,0:T(8,128)(2,1)S(1)}, bf16[320,128]{1,0:T(8,128)(2,1)S(1)}, u32[]{:S(2)}, u32[]{:S(2)}) collective-permute-start(bf16[320,128]{1,0:T(8,128)(2,1)S(1)} %get-tuple-element.24.first_ref), channel_id=1, source_target_pairs={{0,1},{2,3},{4,5},{6,7},{8,9},{10,11},{12,13},{14,15},{16,17},{18,... | collective-permute-start | bytes 245768 | tf_op jit(solution)/shard_map/ppermute | solution.py:418
  4.4 4.4 %collective-permute-start.1 = (bf16[320,128]{1,0:T(8,128)(2,1)S(1)}, bf16[320,128]{1,0:T(8,128)(2,1)S(1)}, u32[]{:S(2)}, u32[]{:S(2)}) collective-permute-start(bf16[320,128]{1,0:T(8,128)(2,1)S(1)} %get-tuple-element.25.second_ref), channel_id=1, source_target_pairs={{1,2},{3,4},{5,6},{7,8},{9,10},{11,12},{13,14},{15,16},{17,18},{19... | collective-permute-start | bytes 245768 | tf_op jit(solution)/shard_map/ppermute | solution.py:418
  10.3 2.6 %collective-permute-start.2 = (bf16[2048,128]{1,0:T(8,128)(2,1)S(1)}, bf16[2048,128]{1,0:T(8,128)(2,1)S(1)}, u32[]{:S(2)}, u32[]{:S(2)}) collective-permute-start(bf16[2048,128]{1,0:T(8,128)(2,1)S(1)} %get-tuple-element.28), channel_id=1, source_target_pairs={{0,32},{1,33},{2,34},{3,35},{4,36},{5,37},{6,38},{7,39},{8,40},{9,... | collective-permute-start | bytes 1572872 | tf_op jit(solution)/shard_map/ppermute | solution.py:409
  13.8 24.6 %all-to-all-start = ((bf16[32,64,128]{2,1,0:T(8,128)(2,1)}), bf16[32,64,128]{2,1,0:T(8,128)(2,1)S(1)}, u32[]{:S(2)}, u32[]{:S(2)}) async-start(bf16[32,64,128]{2,1,0:T(8,128)(2,1)} %bitcast.3), calls=%async_computation | async-start | bytes 1048576 | tf_op jit(solution)/shard_map/all_to_all | solution.py:405
  38.5 5.7 %collective-permute-start.5 = (bf16[64,128]{1,0:T(8,128)(2,1)S(1)}, bf16[64,128]{1,0:T(8,128)(2,1)S(1)}, u32[]{:S(2)}, u32[]{:S(2)}) collective-permute-start(bf16[64,128]{1,0:T(8,128)(2,1)S(1)} %sum_around.1.refs_0_), channel_id=1, source_target_pairs={{0,6},{1,7},{2,4},{3,5},{4,2},{5,3},{6,0},{7,1},{8,14},{9,15},{10,... | collective-permute-start | bytes 49160 | tf_op jit(solution)/shard_map/ppermute | solution.py:413
  42.0 6.6 %collective-permute-start.4 = (bf16[64,128]{1,0:T(8,128)(2,1)S(1)}, bf16[64,128]{1,0:T(8,128)(2,1)S(1)}, u32[]{:S(2)}, u32[]{:S(2)}) collective-permute-start(bf16[64,128]{1,0:T(8,128)(2,1)S(1)} %sum_around.1.refs_0_), channel_id=1, source_target_pairs={{0,4},{1,5},{2,6},{3,7},{4,0},{5,1},{6,2},{7,3},{8,12},{9,13},{10,... | collective-permute-start | bytes 49160 | tf_op jit(solution)/shard_map/ppermute | solution.py:413
  43.5 5.1 %collective-permute-start.3 = (bf16[64,128]{1,0:T(8,128)(2,1)S(1)}, bf16[64,128]{1,0:T(8,128)(2,1)S(1)}, u32[]{:S(2)}, u32[]{:S(2)}) collective-permute-start(bf16[64,128]{1,0:T(8,128)(2,1)S(1)} %sum_around.1.refs_0_), channel_id=1, source_target_pairs={{0,2},{1,3},{2,0},{3,1},{4,6},{5,7},{6,4},{7,5},{8,10},{9,11},{10,... | collective-permute-start | bytes 49160 | tf_op jit(solution)/shard_map/ppermute | solution.py:413
  61.8 5.9 %collective-permute-start.6 = (bf16[2048,128]{1,0:T(8,128)(2,1)S(1)}, bf16[2048,128]{1,0:T(8,128)(2,1)S(1)}, u32[]{:S(2)}, u32[]{:S(2)}) collective-permute-start(bf16[2048,128]{1,0:T(8,128)(2,1)S(1)} %bitcast.5), channel_id=1, source_target_pairs={{0,32},{1,33},{2,34},{3,35},{4,36},{5,37},{6,38},{7,39},{8,40},{9,... | collective-permute-start | bytes 1572872 | tf_op jit(solution)/shard_map/ppermute | solution.py:409

commit v7 on v6

--- a/solution.py
+++ b/solution.py
@@ -108,8 +108,8 @@
         table = jnp.concatenate([masks[edge]] + rows + [jnp.zeros((13, 128), F32)], axis=0)
         out_ref[3 * CH :, :] = table.astype(BF16)
     odd = dev_parity()
-    first_ref[...] = both_ref[1 - odd]
-    second_ref[...] = both_ref[odd]
+    first_ref[...] = both_ref[odd]
+    second_ref[...] = both_ref[1 - odd]
 
 
 def dev_parity():
@@ -120,7 +120,7 @@
     both_ref[0] = first_ref[...]
     both_ref[1] = second_ref[...]
     odd = dev_parity()
-    return both_ref.at[1 - odd], both_ref.at[odd]
+    return both_ref.at[odd], both_ref.at[1 - odd]
 
 
 def turned(w_ref, d):
@@ -439,8 +439,8 @@
         ],
         name="rims",
     )
-    got_first = dev_swap(first, 0)
-    got_second = dev_swap(second, 1)
+    got_first = dev_swap(first, 1)
+    got_second = dev_swap(second, 0)
     v, part, w1t, wb, sel, mask = call(
         prep_kernel,
         [
@@ -494,7 +494,8 @@
         rows_kernel, shape((HALF // AROUND, 128)), moved, in_hbm(features_out),
         specs={1: HBM}, name="sum_around",
     )
-    arrived = [value] + [swap_z(value, k) for k in range(1, 4)]
+    arrived = {k: swap_z(value, k) for k in (1, 3, 2)}
+    arrived = [value] + [arrived[k] for k in (1, 2, 3)]
     value = call(
         total_kernel, shape((AROUND, HALF // AROUND, 128)), *arrived,
         scratch=[pltpu.VMEM((4, HALF // AROUND, 128), BF16)],

time: 69.3 us -> 68.3 us (0.986)
  waiting for transfers between devices: 11.9 us -> 10.3 us
    ppermute x2, starting transfers between devices: 3.21 us -> 6.1 us  [dev_swap(): return lax.ppermute(value, 'dev', pairs + [(j, i) for i, j in pairs])]
    all_to_all x1, starting transfers between devices: 13.2 us -> 10.5 us  [all_to_all(): lax.all_to_all(value, BOTH, 0, 0, axis_index_groups=around_groups(), tile...]
    ppermute x3, waiting for transfers between devices: 4.32 us -> 2.7 us  [swap_z(): lax.ppermute(value, BOTH, device_pairs(lambda x, y, z, core: (x, y, z ^ 2...]
  transfers between devices with their start and end apart: 8 -> 8, of which waited for: 4 -> 4; matrix products, arithmetic and copies ran while one was open for 0% -> 0% of each run, Pallas kernels for 15% -> 16%
where the time goes in v7:
time: 68.3 us; the launch traced here: 68 us
  starting transfers between devices  28 us (41%)
  Pallas kernels  15.7 us (23%)
  blocking collectives  13.4 us (20%)
  waiting for transfers between devices  10.3 us (15%)
  between operations  0.73 us (1%)
    pallas_call x10, Pallas kernels, call(): pl.pallas_call(kernel, out_shape=outs, in_specs=[specs.get(k, VMEM) for k...  15.7 us
    all_to_all x1, blocking collectives, all_to_all(): lax.all_to_all(value, BOTH, 0, 0, axis_index_groups=around_groups(), tile...  13.4 us
    all_to_all x1, starting transfers between devices, all_to_all(): lax.all_to_all(value, BOTH, 0, 0, axis_index_groups=around_groups(), tile...  10.5 us
    all_to_all x1, waiting for transfers between devices, all_to_all(): lax.all_to_all(value, BOTH, 0, 0, axis_index_groups=around_groups(), tile...  6.63 us
    ppermute x2, starting transfers between devices, dev_swap(): return lax.ppermute(value, 'dev', pairs + [(j, i) for i, j in pairs])  6.1 us
    ppermute x3, starting transfers between devices, swap_z(): lax.ppermute(value, BOTH, device_pairs(lambda x, y, z, core: (x, y, z ^ 2...  5.74 us
    ppermute x2, starting transfers between devices, swap_core(): lax.ppermute(value, BOTH, device_pairs(lambda x, y, z, core: (x, y, z, 1...  5.62 us
    ppermute x3, waiting for transfers between devices, swap_z(): lax.ppermute(value, BOTH, device_pairs(lambda x, y, z, core: (x, y, z ^ 2...  2.7 us
  transfers between devices with their start and end apart: 8, of which 4 were waited for; matrix products, arithmetic and copies ran while one was open for 0% of the time, Pallas kernels for 16%

profile of v7, /device:TPU:1, one launch (start us, length us, event | category | flops | bytes accessed | tf_op | source)
XLA Modules:
  0.0 68.0 jit_solution(7157801211837038833)
XLA Ops:
  0.6 1.2 %rims.1 = (bf16[320,128]{1,0:T(8,128)(2,1)S(1)}, bf16[320,128]{1,0:T(8,128)(2,1)S(1)}) custom-call(bf16[96,1024]{1,0:T(8,128)(2,1)} %feat_hbm.3, bf16[96,1024]{1,0:T(8,128)(2,1)} %cot_hbm.3, s32[1,1024]{1,0:T(1,128)} %bitcast.7, s32[2,27]{1,0:T(2,128)} %nb_hbm.3), custom_call_target="tpu_custom_call" | custom-call | bytes 1048576 | tf_op jit(solution)/shard_map/rims/pallas_call | solution.py:374
  1.9 0.7 collective-permute-start
  2.5 5.4 %collective-permute-start.1 = (bf16[320,128]{1,0:T(8,128)(2,1)S(1)}, bf16[320,128]{1,0:T(8,128)(2,1)S(1)}, u32[]{:S(2)}, u32[]{:S(2)}) collective-permute-start(bf16[320,128]{1,0:T(8,128)(2,1)S(1)} %get-tuple-element.25.second_ref), channel_id=1, source_target_pairs={{0,1},{2,3},{4,5},{6,7},{8,9},{10,11},{12,13},{14,15},{16,17},{18,... | collective-permute-start | bytes 245768 | tf_op jit(solution)/shard_map/ppermute | solution.py:418
  8.0 3.7 %prep.1 = (bf16[2,864,1024]{2,1,0:T(8,128)(2,1)S(1)}, f32[2,96,1024]{2,1,0:T(8,128)S(1)}, bf16[288,864]{1,0:T(8,128)(2,1)S(1)}, bf16[288,864]{1,0:T(8,128)(2,1)S...) custom-call(bf16[96,1024]{1,0:T(8,128)(2,1)} %feat_hbm.3, bf16[96,1024]{1,0:T(8,128)(2,1)} %cot_hbm.3, ...), custom_call_target="tpu_custom_call" | custom-call | flops 4294967296 | bytes 1048576 | tf_op jit(solution)/shard_map/prep/pallas_call | solution.py:374
  11.7 0.0 collective-permute-done.first_ref.got_first_ref
  11.7 0.0 collective-permute-done.1.second_ref.got_second_ref
  11.7 1.5 %points.1 = (bf16[2048,128]{1,0:T(8,128)(2,1)S(1)}, bf16[2,96,1024]{2,1,0:T(8,128)(2,1)S(1)}, bf16[2,864,256]{2,1,0:T(8,128)(2,1)S(1)}) custom-call(f32[2,96,1024]{2,1,0:T(8,128)S(1)} %get-tuple-element.18.part_ref, bf16[288,864]{1,0:T(8,128)(2,1)S(1)} %get-tuple-element.19.w1t_ref, bf16[288,864]{1,0:T(8,128)(2,1)S(1)} %get-tuple-element.20.wb_ref, ...), custom_call_target="tpu_custom_call" | custom-call | flops 2147483648 | bytes 1048576 | tf_op jit(solution)/shard_map/points/pallas_call | solution.py:374
  13.2 1.3 %collective-permute-start.2 = (bf16[2048,128]{1,0:T(8,128)(2,1)S(1)}, bf16[2048,128]{1,0:T(8,128)(2,1)S(1)}, u32[]{:S(2)}, u32[]{:S(2)}) collective-permute-start(bf16[2048,128]{1,0:T(8,128)(2,1)S(1)} %get-tuple-element.28), channel_id=1, source_target_pairs={{0,32},{1,33},{2,34},{3,35},{4,36},{5,37},{6,38},{7,39},{8,40},{9,... | collective-permute-start | bytes 1572872 | tf_op jit(solution)/shard_map/ppermute | solution.py:409
  14.5 1.0 %terms_kept.1.own_ref = f32[2048,128]{1,0:T(8,128)S(1)} custom-call(bf16[2,864,1024]{2,1,0:T(8,128)(2,1)S(1)} %get-tuple-element.23.v_ref, bf16[2,864,256]{2,1,0:T(8,128)(2,1)S(1)} %get-tuple-element.27.rim_ref, bf16[2,96,1024]{2,1,0:T(8,128)(2,1)S(1)} %get-tuple-element.26.grad_ref), custom_call_target="tpu_custom_call" | custom-call | flops 2147483648 | bytes 1048576 | tf_op jit(solution)/shard_map/terms_kept/pallas_call | solution.py:374
  15.5 0.6 collective-permute-done.2.got_ref
  16.1 0.8 %sum_core.1.after_ref = bf16[2048,128]{1,0:T(8,128)(2,1)} custom-call(f32[2048,128]{1,0:T(8,128)S(1)} %terms_kept.1.own_ref, bf16[2048,128]{1,0:T(8,128)(2,1)S(1)} %collective-permute-done.2.got_ref), custom_call_target="tpu_custom_call" | custom-call | bytes 1048576 | tf_op jit(solution)/shard_map/sum_core/pallas_call | solution.py:374
  16.9 10.5 %all-to-all-start = ((bf16[32,64,128]{2,1,0:T(8,128)(2,1)}), bf16[32,64,128]{2,1,0:T(8,128)(2,1)S(1)}, u32[]{:S(2)}, u32[]{:S(2)}) async-start(bf16[32,64,128]{2,1,0:T(8,128)(2,1)} %bitcast.3), calls=%async_computation | async-start | bytes 1048576 | tf_op jit(solution)/shard_map/all_to_all | solution.py:405
  27.5 4.7 %features.1.after_ref = bf16[96,1024]{1,0:T(8,128)(2,1)} custom-call(bf16[2,96,1024]{2,1,0:T(8,128)(2,1)S(1)} %get-tuple-element.26.grad_ref, bf16[320,128]{1,0:T(8,128)(2,1)S(1)} %collective-permute-done.first_ref.got_first_ref, bf16[320,128]{1,0:T(8,128)(2,1)S(1)} %collective-permute-done.1.second_ref.got_second_ref, ...), custom_call_target="tpu_custom_call" | custom-call | flops 3221225472 | bytes 1048576 | tf_op jit(solution)/shard_map/features/pallas_call | solution.py:374
  32.2 6.6 %all-to-all-done.got_ref = bf16[32,64,128]{2,1,0:T(8,128)(2,1)S(1)} async-done(((bf16[32,64,128]{2,1,0:T(8,128)(2,1)}), bf16[32,64,128]{2,1,0:T(8,128)(2,1)S(1)}, u32[]{:S(2)}, u32[]{:S(2)}) %all-to-all-start) | async-done | bytes 524320 | tf_op jit(solution)/shard_map/all_to_all | solution.py:405
  38.8 0.1 sum_around.1.refs_0_
  38.9 1.9 %collective-permute-start.5 = (bf16[64,128]{1,0:T(8,128)(2,1)S(1)}, bf16[64,128]{1,0:T(8,128)(2,1)S(1)}, u32[]{:S(2)}, u32[]{:S(2)}) collective-permute-start(bf16[64,128]{1,0:T(8,128)(2,1)S(1)} %sum_around.1.refs_0_), channel_id=1, source_target_pairs={{0,6},{1,7},{2,4},{3,5},{4,2},{5,3},{6,0},{7,1},{8,14},{9,15},{10,... | collective-permute-start | bytes 49160 | tf_op jit(solution)/shard_map/ppermute | solution.py:413
  40.9 2.3 %collective-permute-start.4 = (bf16[64,128]{1,0:T(8,128)(2,1)S(1)}, bf16[64,128]{1,0:T(8,128)(2,1)S(1)}, u32[]{:S(2)}, u32[]{:S(2)}) collective-permute-start(bf16[64,128]{1,0:T(8,128)(2,1)S(1)} %sum_around.1.refs_0_), channel_id=1, source_target_pairs={{0,4},{1,5},{2,6},{3,7},{4,0},{5,1},{6,2},{7,3},{8,12},{9,13},{10,... | collective-permute-start | bytes 49160 | tf_op jit(solution)/shard_map/ppermute | solution.py:413
  43.2 1.5 %collective-permute-start.3 = (bf16[64,128]{1,0:T(8,128)(2,1)S(1)}, bf16[64,128]{1,0:T(8,128)(2,1)S(1)}, u32[]{:S(2)}, u32[]{:S(2)}) collective-permute-start(bf16[64,128]{1,0:T(8,128)(2,1)S(1)} %sum_around.1.refs_0_), channel_id=1, source_target_pairs={{0,2},{1,3},{2,0},{3,1},{4,6},{5,7},{6,4},{7,5},{8,10},{9,11},{10,... | collective-permute-start | bytes 49160 | tf_op jit(solution)/shard_map/ppermute | solution.py:413
  44.7 0.0 collective-permute-done.5.refs_3_
  44.7 2.7 %collective-permute-done.4.refs_2_ = bf16[64,128]{1,0:T(8,128)(2,1)S(1)} collective-permute-done((bf16[64,128]{1,0:T(8,128)(2,1)S(1)}, bf16[64,128]{1,0:T(8,128)(2,1)S(1)}, u32[]{:S(2)}, u32[]{:S(2)}) %collective-permute-start.4) | collective-permute-done | bytes 16416 | tf_op jit(solution)/shard_map/ppermute | solution.py:413
  47.4 0.0 collective-permute-done.3.refs_1_
  47.4 0.1 sum_z.1
  47.4 13.4 %all_to_all.10 = bf16[32,64,128]{2,1,0:T(8,128)(2,1)S(1)} all-to-all(bf16[32,64,128]{2,1,0:T(8,128)(2,1)S(1)} %sum_z.1), channel_id=1, replica_groups={{0,1,8,9,16,17,24,25,64,65,72,73,80,81,88,89,128,129,136,137,144,145,15..., dimensions={0} | all-to-all | bytes 1048576 | tf_op jit(solution)/shard_map/all_to_all | solution.py:405
  60.8 4.3 %collective-permute-start.6 = (bf16[2048,128]{1,0:T(8,128)(2,1)S(1)}, bf16[2048,128]{1,0:T(8,128)(2,1)S(1)}, u32[]{:S(2)}, u32[]{:S(2)}) collective-permute-start(bf16[2048,128]{1,0:T(8,128)(2,1)S(1)} %bitcast.5), channel_id=1, source_target_pairs={{0,32},{1,33},{2,34},{3,35},{4,36},{5,37},{6,38},{7,39},{8,40},{9,... | collective-permute-start | bytes 1572872 | tf_op jit(solution)/shard_map/ppermute | solution.py:409
  65.1 1.2 %unpack_own.1 = (f32[27,96,96]{2,1,0:T(8,128)}, f32[27,96,96]{2,1,0:T(8,128)}) custom-call(bf16[2048,128]{1,0:T(8,128)(2,1)S(1)} %bitcast.6), custom_call_target="tpu_custom_call" | custom-call | bytes 1048576 | tf_op jit(solution)/shard_map/unpack_own/pallas_call | solution.py:374
  66.3 0.3 collective-permute-done.6.refs_0_
  66.7 1.4 %unpack_other.1 = (f32[27,96,96]{2,1,0:T(8,128)}, f32[27,96,96]{2,1,0:T(8,128)}) custom-call(bf16[2048,128]{1,0:T(8,128)(2,1)S(1)} %collective-permute-done.6.refs_0_, f32[27,96,96]{2,1,0:T(8,128)} %get-tuple-element.29.refs_1_, f32[27,96,96]{2,1,0:T(8,128)} %get-tuple-element.30.refs_2_), custom_call_target="tpu_custom_call", output_to_operand_aliasing={{0}: (1, {}), {1}: (2, {})} | custom-call | bytes 1048576 | tf_op jit(solution)/shard_map/unpack_other/pallas_call | solution.py:374
Async XLA Ops:
  1.9 9.8 %collective-permute-start = (bf16[320,128]{1,0:T(8,128)(2,1)S(1)}, bf16[320,128]{1,0:T(8,128)(2,1)S(1)}, u32[]{:S(2)}, u32[]{:S(2)}) collective-permute-start(bf16[320,128]{1,0:T(8,128)(2,1)S(1)} %get-tuple-element.24.first_ref), channel_id=1, source_target_pairs={{1,2},{3,4},{5,6},{7,8},{9,10},{11,12},{13,14},{15,16},{17,18},{19... | collective-permute-start | bytes 245768 | tf_op jit(solution)/shard_map/ppermute | solution.py:418
  2.5 9.2 %collective-permute-start.1 = (bf16[320,128]{1,0:T(8,128)(2,1)S(1)}, bf16[320,128]{1,0:T(8,128)(2,1)S(1)}, u32[]{:S(2)}, u32[]{:S(2)}) collective-permute-start(bf16[320,128]{1,0:T(8,128)(2,1)S(1)} %get-tuple-element.25.second_ref), channel_id=1, source_target_pairs={{0,1},{2,3},{4,5},{6,7},{8,9},{10,11},{12,13},{14,15},{16,17},{18,... | collective-permute-start | bytes 245768 | tf_op jit(solution)/shard_map/ppermute | solution.py:418
  13.2 2.8 %collective-permute-start.2 = (bf16[2048,128]{1,0:T(8,128)(2,1)S(1)}, bf16[2048,128]{1,0:T(8,128)(2,1)S(1)}, u32[]{:S(2)}, u32[]{:S(2)}) collective-permute-start(bf16[2048,128]{1,0:T(8,128)(2,1)S(1)} %get-tuple-element.28), channel_id=1, source_target_pairs={{0,32},{1,33},{2,34},{3,35},{4,36},{5,37},{6,38},{7,39},{8,40},{9,... | collective-permute-start | bytes 1572872 | tf_op jit(solution)/shard_map/ppermute | solution.py:409
  16.9 21.9 %all-to-all-start = ((bf16[32,64,128]{2,1,0:T(8,128)(2,1)}), bf16[32,64,128]{2,1,0:T(8,128)(2,1)S(1)}, u32[]{:S(2)}, u32[]{:S(2)}) async-start(bf16[32,64,128]{2,1,0:T(8,128)(2,1)} %bitcast.3), calls=%async_computation | async-start | bytes 1048576 | tf_op jit(solution)/shard_map/all_to_all | solution.py:405
  38.9 5.7 %collective-permute-start.5 = (bf16[64,128]{1,0:T(8,128)(2,1)S(1)}, bf16[64,128]{1,0:T(8,128)(2,1)S(1)}, u32[]{:S(2)}, u32[]{:S(2)}) collective-permute-start(bf16[64,128]{1,0:T(8,128)(2,1)S(1)} %sum_around.1.refs_0_), channel_id=1, source_target_pairs={{0,6},{1,7},{2,4},{3,5},{4,2},{5,3},{6,0},{7,1},{8,14},{9,15},{10,... | collective-permute-start | bytes 49160 | tf_op jit(solution)/shard_map/ppermute | solution.py:413
  40.9 6.5 %collective-permute-start.4 = (bf16[64,128]{1,0:T(8,128)(2,1)S(1)}, bf16[64,128]{1,0:T(8,128)(2,1)S(1)}, u32[]{:S(2)}, u32[]{:S(2)}) collective-permute-start(bf16[64,128]{1,0:T(8,128)(2,1)S(1)} %sum_around.1.refs_0_), channel_id=1, source_target_pairs={{0,4},{1,5},{2,6},{3,7},{4,0},{5,1},{6,2},{7,3},{8,12},{9,13},{10,... | collective-permute-start | bytes 49160 | tf_op jit(solution)/shard_map/ppermute | solution.py:413
  43.2 4.2 %collective-permute-start.3 = (bf16[64,128]{1,0:T(8,128)(2,1)S(1)}, bf16[64,128]{1,0:T(8,128)(2,1)S(1)}, u32[]{:S(2)}, u32[]{:S(2)}) collective-permute-start(bf16[64,128]{1,0:T(8,128)(2,1)S(1)} %sum_around.1.refs_0_), channel_id=1, source_target_pairs={{0,2},{1,3},{2,0},{3,1},{4,6},{5,7},{6,4},{7,5},{8,10},{9,11},{10,... | collective-permute-start | bytes 49160 | tf_op jit(solution)/shard_map/ppermute | solution.py:413
  60.8 5.8 %collective-permute-start.6 = (bf16[2048,128]{1,0:T(8,128)(2,1)S(1)}, bf16[2048,128]{1,0:T(8,128)(2,1)S(1)}, u32[]{:S(2)}, u32[]{:S(2)}) collective-permute-start(bf16[2048,128]{1,0:T(8,128)(2,1)S(1)} %bitcast.5), channel_id=1, source_target_pairs={{0,32},{1,33},{2,34},{3,35},{4,36},{5,37},{6,38},{7,39},{8,40},{9,... | collective-permute-start | bytes 1572872 | tf_op jit(solution)/shard_map/ppermute | solution.py:409

commit v8 on v7

--- a/solution.py
+++ b/solution.py
@@ -292,18 +292,11 @@
     return lax.rem(lax.axis_index("group"), 2)
 
 
-def add_kernel(own_ref, got_ref, out_hbm, sum_ref, sems):
-    copies = []
-    for k in range(4):
-        part = pl.ds(k * HALF // 4, HALF // 4)
-        sum_ref[part, :] = (own_ref[part, :] + got_ref[part, :].astype(F32)).astype(BF16)
-        copies.append(pltpu.make_async_copy(sum_ref.at[part], out_hbm.at[part], sems.at[k]))
-        copies[-1].start()
-    for copy in copies:
-        copy.wait()
-
-
-def rows_kernel(got_ref, after_ref, out_ref):
+def add_kernel(own_ref, got_ref, out_ref):
+    out_ref[...] = (own_ref[...] + got_ref[...].astype(F32)).astype(BF16)
+
+
+def rows_kernel(got_ref, out_ref):
     total = got_ref[0].astype(F32)
     for k in range(1, AROUND):
         total += got_ref[k].astype(F32)
@@ -468,13 +461,11 @@
     )
     got = swap_core(sent)
     kept = call(kept_kernel, shape((HALF, 128), F32), v, rim, grad, limit=16, flops=2 << 30, name="terms_kept")
-    value = call(
-        add_kernel, shape((HALF, 128)), kept, got,
-        out_specs=HBM,
-        scratch=[pltpu.VMEM((HALF, 128), BF16), pltpu.SemaphoreType.DMA((4,))],
-        name="sum_core",
-    )
+    value = call(add_kernel, shape((HALF, 128)), kept, got, name="sum_core")
     moved = all_to_all(value.reshape(AROUND, HALF // AROUND, 128))
+    value = call(rows_kernel, shape((HALF // AROUND, 128)), moved, name="sum_around")
+    arrived = {k: swap_z(value, k) for k in (1, 3, 2)}
+    arrived = [value] + [arrived[k] for k in (1, 2, 3)]
     features_out = call(
         out_kernel,
         shape((CH, 1024)),
@@ -491,13 +482,8 @@
         name="features",
     )
     value = call(
-        rows_kernel, shape((HALF // AROUND, 128)), moved, in_hbm(features_out),
-        specs={1: HBM}, name="sum_around",
-    )
-    arrived = {k: swap_z(value, k) for k in (1, 3, 2)}
-    arrived = [value] + [arrived[k] for k in (1, 2, 3)]
-    value = call(
-        total_kernel, shape((AROUND, HALF // AROUND, 128)), *arrived,
+        total_kernel, shape((AROUND, HALF // AROUND, 128)), *arrived, in_hbm(features_out),
+        specs={4: HBM},
         scratch=[pltpu.VMEM((4, HALF // AROUND, 128), BF16)],
         name="sum_z",
     )

time: 68.3 us -> 68.8 us (level)
  blocking collectives: 13.4 us -> 35.1 us
  starting transfers between devices: 28 us -> 16.8 us
  waiting for transfers between devices: 10.3 us -> 0.93 us
  Pallas kernels: 15.7 us -> 15 us
    all_to_all x1 -> x2, blocking collectives: 13.4 us -> 35.1 us  [all_to_all(): lax.all_to_all(value, BOTH, 0, 0, axis_index_groups=around_groups(), tile...]
    all_to_all x1 -> x0, starting transfers between devices: 10.5 us -> none  [all_to_all(): lax.all_to_all(value, BOTH, 0, 0, axis_index_groups=around_groups(), tile...]
    all_to_all x1 -> x0, waiting for transfers between devices: 6.63 us -> none  [all_to_all(): lax.all_to_all(value, BOTH, 0, 0, axis_index_groups=around_groups(), tile...]
    ppermute x3, waiting for transfers between devices: 2.7 us -> 0.01 us  [swap_z(): lax.ppermute(value, BOTH, device_pairs(lambda x, y, z, core: (x, y, z ^ 2...]
    pallas_call x10, Pallas kernels: 15.7 us -> 15 us  [call(): pl.pallas_call(kernel, out_shape=outs, in_specs=[specs.get(k, VMEM) for k...]
  transfers between devices with their start and end apart: 8 -> 7, of which waited for: 4 -> 2; matrix products, arithmetic and copies ran while one was open for 0% -> 0% of each run, Pallas kernels for 16% -> 16%
where the time goes in v8:
time: 68.8 us; the launch traced here: 68.5 us
  blocking collectives  35.1 us (51%)
  starting transfers between devices  16.8 us (24%)
  Pallas kernels  15 us (22%)
  waiting for transfers between devices  0.93 us (1%)
  between operations  0.74 us (1%)
    all_to_all x2, blocking collectives, all_to_all(): lax.all_to_all(value, BOTH, 0, 0, axis_index_groups=around_groups(), tile...  35.1 us
    pallas_call x10, Pallas kernels, call(): pl.pallas_call(kernel, out_shape=outs, in_specs=[specs.get(k, VMEM) for k...  15 us
    ppermute x2, starting transfers between devices, dev_swap(): return lax.ppermute(value, 'dev', pairs + [(j, i) for i, j in pairs])  6.1 us
    ppermute x3, starting transfers between devices, swap_z(): lax.ppermute(value, BOTH, device_pairs(lambda x, y, z, core: (x, y, z ^ 2...  5.74 us
    ppermute x2, starting transfers between devices, swap_core(): lax.ppermute(value, BOTH, device_pairs(lambda x, y, z, core: (x, y, z, 1...  4.93 us
  transfers between devices with their start and end apart: 7, of which 2 were waited for; matrix products, arithmetic and copies ran while one was open for 0% of the time, Pallas kernels for 16%

profile of v8, /device:TPU:1, one launch (start us, length us, event | category | flops | bytes accessed | tf_op | source)
XLA Modules:
  0.0 68.5 jit_solution(10400994906031057289)
XLA Ops:
  0.6 1.2 %rims.1 = (bf16[320,128]{1,0:T(8,128)(2,1)S(1)}, bf16[320,128]{1,0:T(8,128)(2,1)S(1)}) custom-call(bf16[96,1024]{1,0:T(8,128)(2,1)} %feat_hbm.3, bf16[96,1024]{1,0:T(8,128)(2,1)} %cot_hbm.3, s32[1,1024]{1,0:T(1,128)} %bitcast.8, s32[2,27]{1,0:T(2,128)} %nb_hbm.3), custom_call_target="tpu_custom_call" | custom-call | bytes 1048576 | tf_op jit(solution)/shard_map/rims/pallas_call | solution.py:367
  1.9 0.7 collective-permute-start
  2.5 5.4 %collective-permute-start.1 = (bf16[320,128]{1,0:T(8,128)(2,1)S(1)}, bf16[320,128]{1,0:T(8,128)(2,1)S(1)}, u32[]{:S(2)}, u32[]{:S(2)}) collective-permute-start(bf16[320,128]{1,0:T(8,128)(2,1)S(1)} %get-tuple-element.25.second_ref), channel_id=1, source_target_pairs={{0,1},{2,3},{4,5},{6,7},{8,9},{10,11},{12,13},{14,15},{16,17},{18,... | collective-permute-start | bytes 245768 | tf_op jit(solution)/shard_map/ppermute | solution.py:411
  8.0 3.7 %prep.1 = (bf16[2,864,1024]{2,1,0:T(8,128)(2,1)S(1)}, f32[2,96,1024]{2,1,0:T(8,128)S(1)}, bf16[288,864]{1,0:T(8,128)(2,1)S(1)}, bf16[288,864]{1,0:T(8,128)(2,1)S...) custom-call(bf16[96,1024]{1,0:T(8,128)(2,1)} %feat_hbm.3, bf16[96,1024]{1,0:T(8,128)(2,1)} %cot_hbm.3, ...), custom_call_target="tpu_custom_call" | custom-call | flops 4294967296 | bytes 1048576 | tf_op jit(solution)/shard_map/prep/pallas_call | solution.py:367
  11.7 0.0 collective-permute-done.first_ref.got_first_ref
  11.7 0.0 collective-permute-done.1.second_ref.got_second_ref
  11.7 1.5 %points.1 = (bf16[2048,128]{1,0:T(8,128)(2,1)S(1)}, bf16[2,96,1024]{2,1,0:T(8,128)(2,1)S(1)}, bf16[2,864,256]{2,1,0:T(8,128)(2,1)S(1)}) custom-call(f32[2,96,1024]{2,1,0:T(8,128)S(1)} %get-tuple-element.18.part_ref, bf16[288,864]{1,0:T(8,128)(2,1)S(1)} %get-tuple-element.19.w1t_ref, bf16[288,864]{1,0:T(8,128)(2,1)S(1)} %get-tuple-element.20.wb_ref, ...), custom_call_target="tpu_custom_call" | custom-call | flops 2147483648 | bytes 1048576 | tf_op jit(solution)/shard_map/points/pallas_call | solution.py:367
  13.2 1.3 %collective-permute-start.2 = (bf16[2048,128]{1,0:T(8,128)(2,1)S(1)}, bf16[2048,128]{1,0:T(8,128)(2,1)S(1)}, u32[]{:S(2)}, u32[]{:S(2)}) collective-permute-start(bf16[2048,128]{1,0:T(8,128)(2,1)S(1)} %get-tuple-element.28), channel_id=1, source_target_pairs={{0,32},{1,33},{2,34},{3,35},{4,36},{5,37},{6,38},{7,39},{8,40},{9,... | collective-permute-start | bytes 1572872 | tf_op jit(solution)/shard_map/ppermute | solution.py:402
  14.5 1.0 %terms_kept.1.own_ref = f32[2048,128]{1,0:T(8,128)S(1)} custom-call(bf16[2,864,1024]{2,1,0:T(8,128)(2,1)S(1)} %get-tuple-element.23.v_ref, bf16[2,864,256]{2,1,0:T(8,128)(2,1)S(1)} %get-tuple-element.27.rim_ref, bf16[2,96,1024]{2,1,0:T(8,128)(2,1)S(1)} %get-tuple-element.26.grad_ref), custom_call_target="tpu_custom_call" | custom-call | flops 2147483648 | bytes 1048576 | tf_op jit(solution)/shard_map/terms_kept/pallas_call | solution.py:367
  15.5 0.6 collective-permute-done.2.got_ref
  16.1 0.1 sum_core.1
  16.2 21.7 %all_to_all.10.got_ref = bf16[32,64,128]{2,1,0:T(8,128)(2,1)S(1)} all-to-all(bf16[32,64,128]{2,1,0:T(8,128)(2,1)S(1)} %bitcast.7), channel_id=1, replica_groups={{0,1,8,9,16,17,24,25,64,65,72,73,80,81,88,89,128,129,136,137,144,145,15..., dimensions={0} | all-to-all | bytes 1048576 | tf_op jit(solution)/shard_map/all_to_all | solution.py:398
  37.9 0.1 sum_around.1.after_ref.refs_0_
  38.0 1.9 %collective-permute-start.5 = (bf16[64,128]{1,0:T(8,128)(2,1)S(1)}, bf16[64,128]{1,0:T(8,128)(2,1)S(1)}, u32[]{:S(2)}, u32[]{:S(2)}) collective-permute-start(bf16[64,128]{1,0:T(8,128)(2,1)S(1)} %sum_around.1.after_ref.refs_0_), channel_id=1, source_target_pairs={{0,6},{1,7},{2,4},{3,5},{4,2},{5,3},{6,0},{7,1},{8,14},{9,15},{10,... | collective-permute-start | bytes 49160 | tf_op jit(solution)/shard_map/ppermute | solution.py:406
  39.9 2.3 %collective-permute-start.4 = (bf16[64,128]{1,0:T(8,128)(2,1)S(1)}, bf16[64,128]{1,0:T(8,128)(2,1)S(1)}, u32[]{:S(2)}, u32[]{:S(2)}) collective-permute-start(bf16[64,128]{1,0:T(8,128)(2,1)S(1)} %sum_around.1.after_ref.refs_0_), channel_id=1, source_target_pairs={{0,4},{1,5},{2,6},{3,7},{4,0},{5,1},{6,2},{7,3},{8,12},{9,13},{10,... | collective-permute-start | bytes 49160 | tf_op jit(solution)/shard_map/ppermute | solution.py:406
  42.2 1.5 %collective-permute-start.3 = (bf16[64,128]{1,0:T(8,128)(2,1)S(1)}, bf16[64,128]{1,0:T(8,128)(2,1)S(1)}, u32[]{:S(2)}, u32[]{:S(2)}) collective-permute-start(bf16[64,128]{1,0:T(8,128)(2,1)S(1)} %sum_around.1.after_ref.refs_0_), channel_id=1, source_target_pairs={{0,2},{1,3},{2,0},{3,1},{4,6},{5,7},{6,4},{7,5},{8,10},{9,11},{10,... | collective-permute-start | bytes 49160 | tf_op jit(solution)/shard_map/ppermute | solution.py:406
  43.7 4.8 %features.1.refs_4_ = bf16[96,1024]{1,0:T(8,128)(2,1)} custom-call(bf16[2,96,1024]{2,1,0:T(8,128)(2,1)S(1)} %get-tuple-element.26.grad_ref, bf16[320,128]{1,0:T(8,128)(2,1)S(1)} %collective-permute-done.first_ref.got_first_ref, bf16[320,128]{1,0:T(8,128)(2,1)S(1)} %collective-permute-done.1.second_ref.got_second_ref, ...), custom_call_target="tpu_custom_call" | custom-call | flops 3221225472 | bytes 1048576 | tf_op jit(solution)/shard_map/features/pallas_call | solution.py:367
  48.5 0.0 collective-permute-done.5.refs_3_
  48.5 0.0 collective-permute-done.4.refs_2_
  48.5 0.0 collective-permute-done.3.refs_1_
  48.5 0.1 sum_z.1
  48.6 13.4 %all_to_all.11 = bf16[32,64,128]{2,1,0:T(8,128)(2,1)S(1)} all-to-all(bf16[32,64,128]{2,1,0:T(8,128)(2,1)S(1)} %sum_z.1), channel_id=1, replica_groups={{0,1,8,9,16,17,24,25,64,65,72,73,80,81,88,89,128,129,136,137,144,145,15..., dimensions={0} | all-to-all | bytes 1048576 | tf_op jit(solution)/shard_map/all_to_all | solution.py:398
  62.0 3.6 %collective-permute-start.6 = (bf16[2048,128]{1,0:T(8,128)(2,1)S(1)}, bf16[2048,128]{1,0:T(8,128)(2,1)S(1)}, u32[]{:S(2)}, u32[]{:S(2)}) collective-permute-start(bf16[2048,128]{1,0:T(8,128)(2,1)S(1)} %bitcast.5), channel_id=1, source_target_pairs={{0,32},{1,33},{2,34},{3,35},{4,36},{5,37},{6,38},{7,39},{8,40},{9,... | collective-permute-start | bytes 1572872 | tf_op jit(solution)/shard_map/ppermute | solution.py:402
  65.6 1.2 %unpack_own.1 = (f32[27,96,96]{2,1,0:T(8,128)}, f32[27,96,96]{2,1,0:T(8,128)}) custom-call(bf16[2048,128]{1,0:T(8,128)(2,1)S(1)} %bitcast.6), custom_call_target="tpu_custom_call" | custom-call | bytes 1048576 | tf_op jit(solution)/shard_map/unpack_own/pallas_call | solution.py:367
  66.8 0.3 collective-permute-done.6.refs_0_
  67.2 1.4 %unpack_other.1 = (f32[27,96,96]{2,1,0:T(8,128)}, f32[27,96,96]{2,1,0:T(8,128)}) custom-call(bf16[2048,128]{1,0:T(8,128)(2,1)S(1)} %collective-permute-done.6.refs_0_, f32[27,96,96]{2,1,0:T(8,128)} %get-tuple-element.29.refs_1_, f32[27,96,96]{2,1,0:T(8,128)} %get-tuple-element.30.refs_2_), custom_call_target="tpu_custom_call", output_to_operand_aliasing={{0}: (1, {}), {1}: (2, {})} | custom-call | bytes 1048576 | tf_op jit(solution)/shard_map/unpack_other/pallas_call | solution.py:367
Async XLA Ops:
  1.9 9.8 %collective-permute-start = (bf16[320,128]{1,0:T(8,128)(2,1)S(1)}, bf16[320,128]{1,0:T(8,128)(2,1)S(1)}, u32[]{:S(2)}, u32[]{:S(2)}) collective-permute-start(bf16[320,128]{1,0:T(8,128)(2,1)S(1)} %get-tuple-element.24.first_ref), channel_id=1, source_target_pairs={{1,2},{3,4},{5,6},{7,8},{9,10},{11,12},{13,14},{15,16},{17,18},{19... | collective-permute-start | bytes 245768 | tf_op jit(solution)/shard_map/ppermute | solution.py:411
  2.5 9.2 %collective-permute-start.1 = (bf16[320,128]{1,0:T(8,128)(2,1)S(1)}, bf16[320,128]{1,0:T(8,128)(2,1)S(1)}, u32[]{:S(2)}, u32[]{:S(2)}) collective-permute-start(bf16[320,128]{1,0:T(8,128)(2,1)S(1)} %get-tuple-element.25.second_ref), channel_id=1, source_target_pairs={{0,1},{2,3},{4,5},{6,7},{8,9},{10,11},{12,13},{14,15},{16,17},{18,... | collective-permute-start | bytes 245768 | tf_op jit(solution)/shard_map/ppermute | solution.py:411
  13.2 2.8 %collective-permute-start.2 = (bf16[2048,128]{1,0:T(8,128)(2,1)S(1)}, bf16[2048,128]{1,0:T(8,128)(2,1)S(1)}, u32[]{:S(2)}, u32[]{:S(2)}) collective-permute-start(bf16[2048,128]{1,0:T(8,128)(2,1)S(1)} %get-tuple-element.28), channel_id=1, source_target_pairs={{0,32},{1,33},{2,34},{3,35},{4,36},{5,37},{6,38},{7,39},{8,40},{9,... | collective-permute-start | bytes 1572872 | tf_op jit(solution)/shard_map/ppermute | solution.py:402
  38.0 10.5 %collective-permute-start.5 = (bf16[64,128]{1,0:T(8,128)(2,1)S(1)}, bf16[64,128]{1,0:T(8,128)(2,1)S(1)}, u32[]{:S(2)}, u32[]{:S(2)}) collective-permute-start(bf16[64,128]{1,0:T(8,128)(2,1)S(1)} %sum_around.1.after_ref.refs_0_), channel_id=1, source_target_pairs={{0,6},{1,7},{2,4},{3,5},{4,2},{5,3},{6,0},{7,1},{8,14},{9,15},{10,... | collective-permute-start | bytes 49160 | tf_op jit(solution)/shard_map/ppermute | solution.py:406
  39.9 8.6 %collective-permute-start.4 = (bf16[64,128]{1,0:T(8,128)(2,1)S(1)}, bf16[64,128]{1,0:T(8,128)(2,1)S(1)}, u32[]{:S(2)}, u32[]{:S(2)}) collective-permute-start(bf16[64,128]{1,0:T(8,128)(2,1)S(1)} %sum_around.1.after_ref.refs_0_), channel_id=1, source_target_pairs={{0,4},{1,5},{2,6},{3,7},{4,0},{5,1},{6,2},{7,3},{8,12},{9,13},{10,... | collective-permute-start | bytes 49160 | tf_op jit(solution)/shard_map/ppermute | solution.py:406
  42.2 6.3 %collective-permute-start.3 = (bf16[64,128]{1,0:T(8,128)(2,1)S(1)}, bf16[64,128]{1,0:T(8,128)(2,1)S(1)}, u32[]{:S(2)}, u32[]{:S(2)}) collective-permute-start(bf16[64,128]{1,0:T(8,128)(2,1)S(1)} %sum_around.1.after_ref.refs_0_), channel_id=1, source_target_pairs={{0,2},{1,3},{2,0},{3,1},{4,6},{5,7},{6,4},{7,5},{8,10},{9,11},{10,... | collective-permute-start | bytes 49160 | tf_op jit(solution)/shard_map/ppermute | solution.py:406
  62.0 5.2 %collective-permute-start.6 = (bf16[2048,128]{1,0:T(8,128)(2,1)S(1)}, bf16[2048,128]{1,0:T(8,128)(2,1)S(1)}, u32[]{:S(2)}, u32[]{:S(2)}) collective-permute-start(bf16[2048,128]{1,0:T(8,128)(2,1)S(1)} %bitcast.5), channel_id=1, source_target_pairs={{0,32},{1,33},{2,34},{3,35},{4,36},{5,37},{6,38},{7,39},{8,40},{9,... | collective-permute-start | bytes 1572872 | tf_op jit(solution)/shard_map/ppermute | solution.py:402

commit v9 on v7

--- a/solution.py
+++ b/solution.py
@@ -307,18 +307,15 @@
     total = got_ref[0].astype(F32)
     for k in range(1, AROUND):
         total += got_ref[k].astype(F32)
-    out_ref[...] = total.astype(BF16)
-
-
-def total_kernel(*refs):
-    out_ref, slots_ref = refs[-2:]
-    me = lax.rem(lax.axis_index("dev"), 8) // 2
-    for k in range(4):
-        slots_ref[me ^ k] = refs[k][...]
-    total = slots_ref[0].astype(F32)
-    for k in range(1, 4):
-        total += slots_ref[k].astype(F32)
-    total = total.astype(BF16)
+    out_ref[...] = total
+
+
+def pair_kernel(own_ref, got_ref, out_ref):
+    out_ref[...] = own_ref[...] + got_ref[...]
+
+
+def total_kernel(own_ref, got_ref, out_ref):
+    total = (own_ref[...] + got_ref[...]).astype(BF16)
     for k in range(AROUND):
         out_ref[k] = total
 
@@ -491,15 +488,12 @@
         name="features",
     )
     value = call(
-        rows_kernel, shape((HALF // AROUND, 128)), moved, in_hbm(features_out),
+        rows_kernel, shape((HALF // AROUND, 128), F32), moved, in_hbm(features_out),
         specs={1: HBM}, name="sum_around",
     )
-    arrived = {k: swap_z(value, k) for k in (1, 3, 2)}
-    arrived = [value] + [arrived[k] for k in (1, 2, 3)]
+    value = call(pair_kernel, shape((HALF // AROUND, 128), F32), value, swap_z(value, 1), name="sum_pair")
     value = call(
-        total_kernel, shape((AROUND, HALF // AROUND, 128)), *arrived,
-        scratch=[pltpu.VMEM((4, HALF // AROUND, 128), BF16)],
-        name="sum_z",
+        total_kernel, shape((AROUND, HALF // AROUND, 128)), value, swap_z(value, 3), name="sum_z"
     )
     mine = all_to_all(value).reshape(HALF, 128)
     other = swap_core(mine)

time: 68.3 us -> 69.7 us (1.020)
  waiting for transfers between devices: 10.3 us -> 13.7 us
  starting transfers between devices: 28 us -> 25.8 us
    ppermute x3 -> x2, waiting for transfers between devices: 2.7 us -> 6.16 us  [swap_z(): lax.ppermute(value, BOTH, device_pairs(lambda x, y, z, core: (x, y, z ^ 2...]
    ppermute x3 -> x2, starting transfers between devices: 5.74 us -> 2.63 us  [swap_z(): lax.ppermute(value, BOTH, device_pairs(lambda x, y, z, core: (x, y, z ^ 2...]
    ppermute x2, starting transfers between devices: 5.62 us -> 6.54 us  [swap_core(): lax.ppermute(value, BOTH, device_pairs(lambda x, y, z, core: (x, y, z, 1...]
    pallas_call x10 -> x11, Pallas kernels: 15.7 us -> 15.7 us  [call(): pl.pallas_call(kernel, out_shape=outs, in_specs=[specs.get(k, VMEM) for k...]
  transfers between devices with their start and end apart: 8 -> 7, of which waited for: 4 -> 5; matrix products, arithmetic and copies ran while one was open for 0% -> 0% of each run, Pallas kernels for 16% -> 15%
where the time goes in v9:
time: 69.7 us; the launch traced here: 69.4 us
  starting transfers between devices  25.8 us (37%)
  Pallas kernels  15.7 us (23%)
  waiting for transfers between devices  13.7 us (20%)
  blocking collectives  13.4 us (19%)
  between operations  0.73 us (1%)
    pallas_call x11, Pallas kernels, call(): pl.pallas_call(kernel, out_shape=outs, in_specs=[specs.get(k, VMEM) for k...  15.7 us
    all_to_all x1, blocking collectives, all_to_all(): lax.all_to_all(value, BOTH, 0, 0, axis_index_groups=around_groups(), tile...  13.4 us
    all_to_all x1, starting transfers between devices, all_to_all(): lax.all_to_all(value, BOTH, 0, 0, axis_index_groups=around_groups(), tile...  10.5 us
    all_to_all x1, waiting for transfers between devices, all_to_all(): lax.all_to_all(value, BOTH, 0, 0, axis_index_groups=around_groups(), tile...  6.63 us
    ppermute x2, starting transfers between devices, swap_core(): lax.ppermute(value, BOTH, device_pairs(lambda x, y, z, core: (x, y, z, 1...  6.54 us
    ppermute x2, waiting for transfers between devices, swap_z(): lax.ppermute(value, BOTH, device_pairs(lambda x, y, z, core: (x, y, z ^ 2...  6.16 us
    ppermute x2, starting transfers between devices, dev_swap(): return lax.ppermute(value, 'dev', pairs + [(j, i) for i, j in pairs])  6.1 us
    ppermute x2, starting transfers between devices, swap_z(): lax.ppermute(value, BOTH, device_pairs(lambda x, y, z, core: (x, y, z ^ 2...  2.63 us
  transfers between devices with their start and end apart: 7, of which 5 were waited for; matrix products, arithmetic and copies ran while one was open for 0% of the time, Pallas kernels for 15%

profile of v9, /device:TPU:1, one launch (start us, length us, event | category | flops | bytes accessed | tf_op | source)
XLA Modules:
  0.0 69.4 jit_solution(15249560632096842848)
XLA Ops:
  0.6 1.2 %rims.1 = (bf16[320,128]{1,0:T(8,128)(2,1)S(1)}, bf16[320,128]{1,0:T(8,128)(2,1)S(1)}) custom-call(bf16[96,1024]{1,0:T(8,128)(2,1)} %feat_hbm.3, bf16[96,1024]{1,0:T(8,128)(2,1)} %cot_hbm.3, s32[1,1024]{1,0:T(1,128)} %bitcast.7, s32[2,27]{1,0:T(2,128)} %nb_hbm.3), custom_call_target="tpu_custom_call" | custom-call | bytes 1048576 | tf_op jit(solution)/shard_map/rims/pallas_call | solution.py:371
  1.9 0.7 collective-permute-start
  2.5 5.4 %collective-permute-start.1 = (bf16[320,128]{1,0:T(8,128)(2,1)S(1)}, bf16[320,128]{1,0:T(8,128)(2,1)S(1)}, u32[]{:S(2)}, u32[]{:S(2)}) collective-permute-start(bf16[320,128]{1,0:T(8,128)(2,1)S(1)} %get-tuple-element.25.second_ref), channel_id=1, source_target_pairs={{0,1},{2,3},{4,5},{6,7},{8,9},{10,11},{12,13},{14,15},{16,17},{18,... | collective-permute-start | bytes 245768 | tf_op jit(solution)/shard_map/ppermute | solution.py:415
  8.0 3.7 %prep.1 = (bf16[2,864,1024]{2,1,0:T(8,128)(2,1)S(1)}, f32[2,96,1024]{2,1,0:T(8,128)S(1)}, bf16[288,864]{1,0:T(8,128)(2,1)S(1)}, bf16[288,864]{1,0:T(8,128)(2,1)S...) custom-call(bf16[96,1024]{1,0:T(8,128)(2,1)} %feat_hbm.3, bf16[96,1024]{1,0:T(8,128)(2,1)} %cot_hbm.3, ...), custom_call_target="tpu_custom_call" | custom-call | flops 4294967296 | bytes 1048576 | tf_op jit(solution)/shard_map/prep/pallas_call | solution.py:371
  11.7 0.0 collective-permute-done.first_ref.got_first_ref
  11.7 0.0 collective-permute-done.1.second_ref.got_second_ref
  11.7 1.5 %points.1 = (bf16[2048,128]{1,0:T(8,128)(2,1)S(1)}, bf16[2,96,1024]{2,1,0:T(8,128)(2,1)S(1)}, bf16[2,864,256]{2,1,0:T(8,128)(2,1)S(1)}) custom-call(f32[2,96,1024]{2,1,0:T(8,128)S(1)} %get-tuple-element.18.part_ref, bf16[288,864]{1,0:T(8,128)(2,1)S(1)} %get-tuple-element.19.w1t_ref, bf16[288,864]{1,0:T(8,128)(2,1)S(1)} %get-tuple-element.20.wb_ref, ...), custom_call_target="tpu_custom_call" | custom-call | flops 2147483648 | bytes 1048576 | tf_op jit(solution)/shard_map/points/pallas_call | solution.py:371
  13.2 1.3 %collective-permute-start.2 = (bf16[2048,128]{1,0:T(8,128)(2,1)S(1)}, bf16[2048,128]{1,0:T(8,128)(2,1)S(1)}, u32[]{:S(2)}, u32[]{:S(2)}) collective-permute-start(bf16[2048,128]{1,0:T(8,128)(2,1)S(1)} %get-tuple-element.28), channel_id=1, source_target_pairs={{0,32},{1,33},{2,34},{3,35},{4,36},{5,37},{6,38},{7,39},{8,40},{9,... | collective-permute-start | bytes 1572872 | tf_op jit(solution)/shard_map/ppermute | solution.py:406
  14.5 1.0 %terms_kept.1.own_ref = f32[2048,128]{1,0:T(8,128)S(1)} custom-call(bf16[2,864,1024]{2,1,0:T(8,128)(2,1)S(1)} %get-tuple-element.23.v_ref, bf16[2,864,256]{2,1,0:T(8,128)(2,1)S(1)} %get-tuple-element.27.rim_ref, bf16[2,96,1024]{2,1,0:T(8,128)(2,1)S(1)} %get-tuple-element.26.grad_ref), custom_call_target="tpu_custom_call" | custom-call | flops 2147483648 | bytes 1048576 | tf_op jit(solution)/shard_map/terms_kept/pallas_call | solution.py:371
  15.5 0.6 collective-permute-done.2.got_ref
  16.1 0.8 %sum_core.1.after_ref = bf16[2048,128]{1,0:T(8,128)(2,1)} custom-call(f32[2048,128]{1,0:T(8,128)S(1)} %terms_kept.1.own_ref, bf16[2048,128]{1,0:T(8,128)(2,1)S(1)} %collective-permute-done.2.got_ref), custom_call_target="tpu_custom_call" | custom-call | bytes 1048576 | tf_op jit(solution)/shard_map/sum_core/pallas_call | solution.py:371
  16.9 10.5 %all-to-all-start = ((bf16[32,64,128]{2,1,0:T(8,128)(2,1)}), bf16[32,64,128]{2,1,0:T(8,128)(2,1)S(1)}, u32[]{:S(2)}, u32[]{:S(2)}) async-start(bf16[32,64,128]{2,1,0:T(8,128)(2,1)} %bitcast.3), calls=%async_computation | async-start | bytes 1048576 | tf_op jit(solution)/shard_map/all_to_all | solution.py:402
  27.5 4.7 %features.1.after_ref = bf16[96,1024]{1,0:T(8,128)(2,1)} custom-call(bf16[2,96,1024]{2,1,0:T(8,128)(2,1)S(1)} %get-tuple-element.26.grad_ref, bf16[320,128]{1,0:T(8,128)(2,1)S(1)} %collective-permute-done.first_ref.got_first_ref, bf16[320,128]{1,0:T(8,128)(2,1)S(1)} %collective-permute-done.1.second_ref.got_second_ref, ...), custom_call_target="tpu_custom_call" | custom-call | flops 3221225472 | bytes 1048576 | tf_op jit(solution)/shard_map/features/pallas_call | solution.py:371
  32.2 6.6 %all-to-all-done.got_ref = bf16[32,64,128]{2,1,0:T(8,128)(2,1)S(1)} async-done(((bf16[32,64,128]{2,1,0:T(8,128)(2,1)}), bf16[32,64,128]{2,1,0:T(8,128)(2,1)S(1)}, u32[]{:S(2)}, u32[]{:S(2)}) %all-to-all-start) | async-done | bytes 524320 | tf_op jit(solution)/shard_map/all_to_all | solution.py:402
  38.8 0.1 sum_around.1.own_ref
  38.9 0.9 %collective-permute-start.3 = (f32[64,128]{1,0:T(8,128)S(1)}, f32[64,128]{1,0:T(8,128)S(1)}, u32[]{:S(2)}, u32[]{:S(2)}) collective-permute-start(f32[64,128]{1,0:T(8,128)S(1)} %sum_around.1.own_ref), channel_id=1, source_target_pairs={{0,2},{1,3},{2,0},{3,1},{4,6},{5,7},{6,4},{7,5},{8,10},{9,11},{10,... | collective-permute-start | bytes 98312 | tf_op jit(solution)/shard_map/ppermute | solution.py:410
  39.9 3.0 %collective-permute-done.3.got_ref = f32[64,128]{1,0:T(8,128)S(1)} collective-permute-done((f32[64,128]{1,0:T(8,128)S(1)}, f32[64,128]{1,0:T(8,128)S(1)}, u32[]{:S(2)}, u32[]{:S(2)}) %collective-permute-start.3) | collective-permute-done | bytes 32800 | tf_op jit(solution)/shard_map/ppermute | solution.py:410
  42.9 1.7 %collective-permute-start.4 = (f32[64,128]{1,0:T(8,128)S(1)}, f32[64,128]{1,0:T(8,128)S(1)}, u32[]{:S(2)}, u32[]{:S(2)}) collective-permute-start(f32[64,128]{1,0:T(8,128)S(1)} %sum_pair.1.own_ref), channel_id=1, source_target_pairs={{0,6},{1,7},{2,4},{3,5},{4,2},{5,3},{6,0},{7,1},{8,14},{9,15},{10,... | collective-permute-start | bytes 98312 | tf_op jit(solution)/shard_map/ppermute | solution.py:410
  44.5 3.2 %collective-permute-done.4.got_ref = f32[64,128]{1,0:T(8,128)S(1)} collective-permute-done((f32[64,128]{1,0:T(8,128)S(1)}, f32[64,128]{1,0:T(8,128)S(1)}, u32[]{:S(2)}, u32[]{:S(2)}) %collective-permute-start.4) | collective-permute-done | bytes 32800 | tf_op jit(solution)/shard_map/ppermute | solution.py:410
  47.7 0.1 sum_z.1
  47.8 13.4 %all_to_all.10 = bf16[32,64,128]{2,1,0:T(8,128)(2,1)S(1)} all-to-all(bf16[32,64,128]{2,1,0:T(8,128)(2,1)S(1)} %sum_z.1), channel_id=1, replica_groups={{0,1,8,9,16,17,24,25,64,65,72,73,80,81,88,89,128,129,136,137,144,145,15..., dimensions={0} | all-to-all | bytes 1048576 | tf_op jit(solution)/shard_map/all_to_all | solution.py:402
  61.2 5.2 %collective-permute-start.5 = (bf16[2048,128]{1,0:T(8,128)(2,1)S(1)}, bf16[2048,128]{1,0:T(8,128)(2,1)S(1)}, u32[]{:S(2)}, u32[]{:S(2)}) collective-permute-start(bf16[2048,128]{1,0:T(8,128)(2,1)S(1)} %bitcast.5), channel_id=1, source_target_pairs={{0,32},{1,33},{2,34},{3,35},{4,36},{5,37},{6,38},{7,39},{8,40},{9,... | collective-permute-start | bytes 1572872 | tf_op jit(solution)/shard_map/ppermute | solution.py:406
  66.4 1.2 %unpack_own.1 = (f32[27,96,96]{2,1,0:T(8,128)}, f32[27,96,96]{2,1,0:T(8,128)}) custom-call(bf16[2048,128]{1,0:T(8,128)(2,1)S(1)} %bitcast.6), custom_call_target="tpu_custom_call" | custom-call | bytes 1048576 | tf_op jit(solution)/shard_map/unpack_own/pallas_call | solution.py:371
  67.6 0.3 collective-permute-done.5.refs_0_
  68.0 1.4 %unpack_other.1 = (f32[27,96,96]{2,1,0:T(8,128)}, f32[27,96,96]{2,1,0:T(8,128)}) custom-call(bf16[2048,128]{1,0:T(8,128)(2,1)S(1)} %collective-permute-done.5.refs_0_, f32[27,96,96]{2,1,0:T(8,128)} %get-tuple-element.29.refs_1_, f32[27,96,96]{2,1,0:T(8,128)} %get-tuple-element.30.refs_2_), custom_call_target="tpu_custom_call", output_to_operand_aliasing={{0}: (1, {}), {1}: (2, {})} | custom-call | bytes 1048576 | tf_op jit(solution)/shard_map/unpack_other/pallas_call | solution.py:371
  (1 shorter events, 0.0 us)
Async XLA Ops:
  1.9 9.8 %collective-permute-start = (bf16[320,128]{1,0:T(8,128)(2,1)S(1)}, bf16[320,128]{1,0:T(8,128)(2,1)S(1)}, u32[]{:S(2)}, u32[]{:S(2)}) collective-permute-start(bf16[320,128]{1,0:T(8,128)(2,1)S(1)} %get-tuple-element.24.first_ref), channel_id=1, source_target_pairs={{1,2},{3,4},{5,6},{7,8},{9,10},{11,12},{13,14},{15,16},{17,18},{19... | collective-permute-start | bytes 245768 | tf_op jit(solution)/shard_map/ppermute | solution.py:415
  2.5 9.2 %collective-permute-start.1 = (bf16[320,128]{1,0:T(8,128)(2,1)S(1)}, bf16[320,128]{1,0:T(8,128)(2,1)S(1)}, u32[]{:S(2)}, u32[]{:S(2)}) collective-permute-start(bf16[320,128]{1,0:T(8,128)(2,1)S(1)} %get-tuple-element.25.second_ref), channel_id=1, source_target_pairs={{0,1},{2,3},{4,5},{6,7},{8,9},{10,11},{12,13},{14,15},{16,17},{18,... | collective-permute-start | bytes 245768 | tf_op jit(solution)/shard_map/ppermute | solution.py:415
  13.2 2.8 %collective-permute-start.2 = (bf16[2048,128]{1,0:T(8,128)(2,1)S(1)}, bf16[2048,128]{1,0:T(8,128)(2,1)S(1)}, u32[]{:S(2)}, u32[]{:S(2)}) collective-permute-start(bf16[2048,128]{1,0:T(8,128)(2,1)S(1)} %get-tuple-element.28), channel_id=1, source_target_pairs={{0,32},{1,33},{2,34},{3,35},{4,36},{5,37},{6,38},{7,39},{8,40},{9,... | collective-permute-start | bytes 1572872 | tf_op jit(solution)/shard_map/ppermute | solution.py:406
  16.9 21.9 %all-to-all-start = ((bf16[32,64,128]{2,1,0:T(8,128)(2,1)}), bf16[32,64,128]{2,1,0:T(8,128)(2,1)S(1)}, u32[]{:S(2)}, u32[]{:S(2)}) async-start(bf16[32,64,128]{2,1,0:T(8,128)(2,1)} %bitcast.3), calls=%async_computation | async-start | bytes 1048576 | tf_op jit(solution)/shard_map/all_to_all | solution.py:402
  38.9 3.9 %collective-permute-start.3 = (f32[64,128]{1,0:T(8,128)S(1)}, f32[64,128]{1,0:T(8,128)S(1)}, u32[]{:S(2)}, u32[]{:S(2)}) collective-permute-start(f32[64,128]{1,0:T(8,128)S(1)} %sum_around.1.own_ref), channel_id=1, source_target_pairs={{0,2},{1,3},{2,0},{3,1},{4,6},{5,7},{6,4},{7,5},{8,10},{9,11},{10,... | collective-permute-start | bytes 98312 | tf_op jit(solution)/shard_map/ppermute | solution.py:410
  42.9 4.9 %collective-permute-start.4 = (f32[64,128]{1,0:T(8,128)S(1)}, f32[64,128]{1,0:T(8,128)S(1)}, u32[]{:S(2)}, u32[]{:S(2)}) collective-permute-start(f32[64,128]{1,0:T(8,128)S(1)} %sum_pair.1.own_ref), channel_id=1, source_target_pairs={{0,6},{1,7},{2,4},{3,5},{4,2},{5,3},{6,0},{7,1},{8,14},{9,15},{10,... | collective-permute-start | bytes 98312 | tf_op jit(solution)/shard_map/ppermute | solution.py:410
  61.2 6.8 %collective-permute-start.5 = (bf16[2048,128]{1,0:T(8,128)(2,1)S(1)}, bf16[2048,128]{1,0:T(8,128)(2,1)S(1)}, u32[]{:S(2)}, u32[]{:S(2)}) collective-permute-start(bf16[2048,128]{1,0:T(8,128)(2,1)S(1)} %bitcast.5), channel_id=1, source_target_pairs={{0,32},{1,33},{2,34},{3,35},{4,36},{5,37},{6,38},{7,39},{8,40},{9,... | collective-permute-start | bytes 1572872 | tf_op jit(solution)/shard_map/ppermute | solution.py:406
